TPU v7x, 32 devices: a whole 2x2x4 slice. The times are simulated.
32 devices in a mesh: dp: 8 (over y, x, core), seq: 4 (over z).
Axes of the slice: x: 2, y: 2, z: 4, core: 2. Of those that a mesh axis runs over, the one named last changes fastest.
Arguments:
- hidden: bfloat16 [8, 512, 4096], P('dp', 'seq'), may hold values from -6 to 6
- head_weight: bfloat16 [16384, 4096], P('seq', 'dp'), may hold values from -0.09375 to 0.09375
- head_bias: bfloat16 [16384], P('seq'), may hold values from -4 to 4
- argmax: int32 [8, 16384], replicated, may hold values from 0 to 512, as said below
- lengths: int32 [8], replicated, may hold values from 128 to 512
- query_terms: bfloat16 [32, 16384], P('dp'), may hold values from 0 to 1
- score_grad: bfloat16 [32, 8], P('dp'), may hold values from -18 to 18
Outputs:
- hidden_grad: bfloat16 [8, 512, 4096], P('dp', 'seq')
Inputs may be any that keep to these rules, and one draw needn't show every extreme that they name: `argmax`: every document has exactly 4096 vocabulary entries whose saved position is below 512; all other entries hold 512. For every document, at most 2048 vocabulary entries have their saved position in one aligned block of 128 positions, and in every draw some document reaches 2048 in every block of its first half.
All inputs are finite; a program needn't handle non-finite values.
Results may differ from a plain program's by a relative error of at most 0.005.
Values may be sent and summed in bfloat16 or wider, within the bound.
No kernel may reach another device: no remote copies, remote signals or barrier semaphores. Data moves between devices by JAX's collectives and lax.ppermute only.
A program may use at most 128 MiB of HBM per device.

v0:
```python
import jax
import jax.numpy as jnp
from jax import lax
from jax.sharding import PartitionSpec as P

ACT = 4096


def on_device(hidden, head_weight, head_bias, argmax, lengths, query_terms, score_grad):
    slices = lax.all_to_all(hidden, "dp", split_axis=2, concat_axis=0, tiled=True)
    weights, biases = (
        lax.all_gather(head_weight, "seq", axis=0, tiled=True),
        lax.all_gather(head_bias, "seq", axis=0, tiled=True),
    )
    doc_count, tok_rows, slice_width = slices.shape
    vocab_size = argmax.shape[1]
    capacity = 2 * ACT // lax.axis_size("seq")
    offset = lax.axis_index("seq") * tok_rows
    local_pos = argmax - offset
    inside = (local_pos >= 0) & (local_pos < tok_rows)
    group_width = 128
    group_count = vocab_size // group_width
    lower = lax.broadcasted_iota(jnp.int32, (group_width, group_width), 0)
    upper = lax.broadcasted_iota(jnp.int32, (group_width, group_width), 1)
    running = (lower <= upper).astype(jnp.bfloat16)
    grouped = inside.astype(jnp.bfloat16).reshape(doc_count, group_count, group_width)
    within = jnp.einsum("dgk,kj->dgj", grouped, running, preferred_element_type=jnp.float32)
    group_rows = lax.broadcasted_iota(jnp.int32, (group_count, group_count), 0)
    group_cols = lax.broadcasted_iota(jnp.int32, (group_count, group_count), 1)
    earlier = (group_rows < group_cols).astype(jnp.float32)
    before = jnp.einsum("dg,gh->dh", within[:, :, -1], earlier, precision=lax.Precision.HIGHEST)
    counted = (within + before[:, :, None]).reshape(doc_count, vocab_size).astype(jnp.int32)
    targets = lax.broadcasted_iota(jnp.int32, (capacity,), 0) + 1
    found = jax.vmap(lambda row: jnp.searchsorted(row, targets, side="left"))(counted)
    slot_vocab = jnp.minimum(found, vocab_size - 1)
    slot_used = targets[None, :] - 1 < counted[:, -1:]
    slot_global = jnp.take_along_axis(argmax, slot_vocab, axis=1)
    slot_pos = jnp.clip(slot_global - offset, 0, tok_rows - 1)
    usable = slot_used & (slot_global < lengths[:, None])
    doc_block = 8
    block_count = doc_count // doc_block
    slot_weights = weights[slot_vocab]

    def blocked(stacked):
        return stacked.reshape((block_count, doc_block) + stacked.shape[1:])

    def forward_block(packed):
        part_slices, part_pos, weight_rows = packed
        hidden_rows = jax.vmap(lambda source, where_at: source[where_at])(part_slices, part_pos)
        return jnp.einsum(
            "dcw,dcw->dc", hidden_rows, weight_rows, preferred_element_type=jnp.float32
        )

    partial_value = lax.map(
        forward_block, (blocked(slices), blocked(slot_pos), blocked(slot_weights))
    )
    partial_value = partial_value.reshape(doc_count, capacity)
    queries, score_all = (
        lax.all_gather(query_terms, "dp", axis=0, tiled=True),
        lax.all_gather(score_grad, "dp", axis=0, tiled=True),
    )
    logits = lax.psum(partial_value, "dp")
    pooled_grad = jnp.einsum("jd,jv->dv", score_all, queries, preferred_element_type=jnp.float32)
    hit_grad = jnp.take_along_axis(pooled_grad, slot_vocab, axis=1)
    shifted = logits + biases.astype(jnp.float32)[slot_vocab]
    factor = hit_grad * jax.nn.sigmoid(shifted) / (1.0 + jax.nn.softplus(shifted))
    pooled_delta = jnp.where(usable, factor, jnp.zeros_like(factor)).astype(jnp.bfloat16)

    def backward_block(packed):
        part_pos, weight_rows, part_delta = packed
        tok_ids = lax.broadcasted_iota(jnp.int32, (part_pos.shape[0], tok_rows, capacity), 1)
        spread = jnp.where(
            tok_ids == part_pos[:, None, :], part_delta[:, None, :], jnp.zeros((), jnp.bfloat16)
        )
        return jnp.einsum(
            "dtc,dcw->dtw", spread, weight_rows, preferred_element_type=jnp.float32
        ).astype(jnp.bfloat16)

    grad_slices = lax.map(
        backward_block, (blocked(slot_pos), blocked(slot_weights), blocked(pooled_delta))
    )
    grad_slices = grad_slices.reshape(doc_count, tok_rows, slice_width)
    return lax.all_to_all(grad_slices, "dp", split_axis=0, concat_axis=2, tiled=True)


def solution(mesh):
    return jax.shard_map(
        on_device,
        mesh=mesh,
        in_specs=(
            P("dp", "seq", None),
            P("seq", "dp"),
            P("seq"),
            P(),
            P(),
            P("dp", None),
            P("dp", None),
        ),
        out_specs=P("dp", "seq", None),
        check_vma=False,
    )
```

profile of v0, /device:TPU:0, one launch (start us, length us, event | category | flops | bytes accessed | tf_op | source)
XLA Modules:
  0.0 2191.0 jit_solution(1094213863027543341)
XLA Ops:
  6.5 0.7 all-gather.7.cloned.1.call-update
  7.3 0.7 all-gather.5.cloned.1.call-update
  8.0 5.0 copy.17
  13.0 0.5 broadcast.179
  13.6 23.3 %reduce.4 = bf16[4096,128]{1,0:T(8,128)(2,1)} reduce(bf16[4096,1,128]{2,1,0:T(2,128)(2,1)S(1)} %bitcast.74, bf16[]{:T(256)} %broadcast.179), dimensions={1}, to_apply=%bitcast.51.reduce_sub_computation | reduce | bytes 2097154
  36.9 2.1 reshape.136
  39.1 5.2 all-to-all-start
  44.3 14.0 all_gather.15
  58.3 0.1 and_bitcast_fusion
  58.5 0.2 fusion.13
  58.7 0.1 fusion.27
  58.8 0.1 add_convert_fusion
  58.9 0.2 copy.16
  59.1 0.3 copy.35
  59.5 1507.8 %while.32 = (s32[]{:T(128)}, u32[8,2048]{1,0:T(8,128)S(1)}, u32[8,2048]{1,0:T(8,128)S(1)}, s32[8,16384]{1,0:T(8,128)S(1)}, s32[]{:T(128)}, /*index=5*/s32[]{:T(128)}) while((s32[]{:T(128)}, u32[8,2048]{1,0:T(8,128)S(1)}, u32[8,2048]{1,0:T(8,128)S(1)}, s32[8,16384]{1,0:T(8,128)S(1)}, s32[]{:T(128)}, /*index=5*/s32[]{:T(128)}) %tuple.48), condition=%wide.region_1.2_spmd.clone, body=%wide.region_0.1_spmd.clone.sunk | while | flops 378883 | bytes 1359953 | solution.py:34
  59.5 100.3 %gather_fusion = s32[16384]{0:T(1024)S(1)} fusion(s32[8,16384]{1,0:T(8,128)S(1)} %get-tuple-element.175, u32[16384]{0:T(1024)S(1)} %bitcast.65), kind=kCustom, calls=%fused_computation.clone.clone.1 | custom fusion | bytes 262144 | tf_op jit(solution)/shard_map/vmap(jit(searchsorted))/vmap(jit(_searchsorted_scan_impl))/while/body/eval_jaxpr/gather | solution.py:34
  159.9 0.1 select_select_fusion.5
  160.1 100.3 %gather_fusion = s32[16384]{0:T(1024)S(1)} fusion(s32[8,16384]{1,0:T(8,128)S(1)} %get-tuple-element.175, u32[16384]{0:T(1024)S(1)} %bitcast.65), kind=kCustom, calls=%fused_computation.clone.clone.1 | custom fusion | bytes 262144 | tf_op jit(solution)/shard_map/vmap(jit(searchsorted))/vmap(jit(_searchsorted_scan_impl))/while/body/eval_jaxpr/gather | solution.py:34
  260.4 0.1 select_select_fusion.5
  260.6 100.3 %gather_fusion = s32[16384]{0:T(1024)S(1)} fusion(s32[8,16384]{1,0:T(8,128)S(1)} %get-tuple-element.175, u32[16384]{0:T(1024)S(1)} %bitcast.65), kind=kCustom, calls=%fused_computation.clone.clone.1 | custom fusion | bytes 262144 | tf_op jit(solution)/shard_map/vmap(jit(searchsorted))/vmap(jit(_searchsorted_scan_impl))/while/body/eval_jaxpr/gather | solution.py:34
  361.0 0.1 select_select_fusion.5
  361.1 100.3 %gather_fusion = s32[16384]{0:T(1024)S(1)} fusion(s32[8,16384]{1,0:T(8,128)S(1)} %get-tuple-element.175, u32[16384]{0:T(1024)S(1)} %bitcast.65), kind=kCustom, calls=%fused_computation.clone.clone.1 | custom fusion | bytes 262144 | tf_op jit(solution)/shard_map/vmap(jit(searchsorted))/vmap(jit(_searchsorted_scan_impl))/while/body/eval_jaxpr/gather | solution.py:34
  461.5 0.1 select_select_fusion.5
  461.6 100.3 %gather_fusion = s32[16384]{0:T(1024)S(1)} fusion(s32[8,16384]{1,0:T(8,128)S(1)} %get-tuple-element.175, u32[16384]{0:T(1024)S(1)} %bitcast.65), kind=kCustom, calls=%fused_computation.clone.clone.1 | custom fusion | bytes 262144 | tf_op jit(solution)/shard_map/vmap(jit(searchsorted))/vmap(jit(_searchsorted_scan_impl))/while/body/eval_jaxpr/gather | solution.py:34
  562.0 0.1 select_select_fusion.5
  562.1 100.3 %gather_fusion = s32[16384]{0:T(1024)S(1)} fusion(s32[8,16384]{1,0:T(8,128)S(1)} %get-tuple-element.175, u32[16384]{0:T(1024)S(1)} %bitcast.65), kind=kCustom, calls=%fused_computation.clone.clone.1 | custom fusion | bytes 262144 | tf_op jit(solution)/shard_map/vmap(jit(searchsorted))/vmap(jit(_searchsorted_scan_impl))/while/body/eval_jaxpr/gather | solution.py:34
  662.5 0.1 select_select_fusion.5
  662.7 100.3 %gather_fusion = s32[16384]{0:T(1024)S(1)} fusion(s32[8,16384]{1,0:T(8,128)S(1)} %get-tuple-element.175, u32[16384]{0:T(1024)S(1)} %bitcast.65), kind=kCustom, calls=%fused_computation.clone.clone.1 | custom fusion | bytes 262144 | tf_op jit(solution)/shard_map/vmap(jit(searchsorted))/vmap(jit(_searchsorted_scan_impl))/while/body/eval_jaxpr/gather | solution.py:34
  763.0 0.1 select_select_fusion.5
  763.2 100.3 %gather_fusion = s32[16384]{0:T(1024)S(1)} fusion(s32[8,16384]{1,0:T(8,128)S(1)} %get-tuple-element.175, u32[16384]{0:T(1024)S(1)} %bitcast.65), kind=kCustom, calls=%fused_computation.clone.clone.1 | custom fusion | bytes 262144 | tf_op jit(solution)/shard_map/vmap(jit(searchsorted))/vmap(jit(_searchsorted_scan_impl))/while/body/eval_jaxpr/gather | solution.py:34
  863.6 0.1 select_select_fusion.5
  863.7 100.3 %gather_fusion = s32[16384]{0:T(1024)S(1)} fusion(s32[8,16384]{1,0:T(8,128)S(1)} %get-tuple-element.175, u32[16384]{0:T(1024)S(1)} %bitcast.65), kind=kCustom, calls=%fused_computation.clone.clone.1 | custom fusion | bytes 262144 | tf_op jit(solution)/shard_map/vmap(jit(searchsorted))/vmap(jit(_searchsorted_scan_impl))/while/body/eval_jaxpr/gather | solution.py:34
  964.1 0.1 select_select_fusion.5
  964.2 100.3 %gather_fusion = s32[16384]{0:T(1024)S(1)} fusion(s32[8,16384]{1,0:T(8,128)S(1)} %get-tuple-element.175, u32[16384]{0:T(1024)S(1)} %bitcast.65), kind=kCustom, calls=%fused_computation.clone.clone.1 | custom fusion | bytes 262144 | tf_op jit(solution)/shard_map/vmap(jit(searchsorted))/vmap(jit(_searchsorted_scan_impl))/while/body/eval_jaxpr/gather | solution.py:34
  1064.6 0.1 select_select_fusion.5
  1064.8 100.3 %gather_fusion = s32[16384]{0:T(1024)S(1)} fusion(s32[8,16384]{1,0:T(8,128)S(1)} %get-tuple-element.175, u32[16384]{0:T(1024)S(1)} %bitcast.65), kind=kCustom, calls=%fused_computation.clone.clone.1 | custom fusion | bytes 262144 | tf_op jit(solution)/shard_map/vmap(jit(searchsorted))/vmap(jit(_searchsorted_scan_impl))/while/body/eval_jaxpr/gather | solution.py:34
  1165.1 0.1 select_select_fusion.5
  1165.3 100.3 %gather_fusion = s32[16384]{0:T(1024)S(1)} fusion(s32[8,16384]{1,0:T(8,128)S(1)} %get-tuple-element.175, u32[16384]{0:T(1024)S(1)} %bitcast.65), kind=kCustom, calls=%fused_computation.clone.clone.1 | custom fusion | bytes 262144 | tf_op jit(solution)/shard_map/vmap(jit(searchsorted))/vmap(jit(_searchsorted_scan_impl))/while/body/eval_jaxpr/gather | solution.py:34
  1265.6 0.1 select_select_fusion.5
  1265.8 100.3 %gather_fusion = s32[16384]{0:T(1024)S(1)} fusion(s32[8,16384]{1,0:T(8,128)S(1)} %get-tuple-element.175, u32[16384]{0:T(1024)S(1)} %bitcast.65), kind=kCustom, calls=%fused_computation.clone.clone.1 | custom fusion | bytes 262144 | tf_op jit(solution)/shard_map/vmap(jit(searchsorted))/vmap(jit(_searchsorted_scan_impl))/while/body/eval_jaxpr/gather | solution.py:34
  1366.2 0.1 select_select_fusion.5
  1366.3 100.3 %gather_fusion = s32[16384]{0:T(1024)S(1)} fusion(s32[8,16384]{1,0:T(8,128)S(1)} %get-tuple-element.175, u32[16384]{0:T(1024)S(1)} %bitcast.65), kind=kCustom, calls=%fused_computation.clone.clone.1 | custom fusion | bytes 262144 | tf_op jit(solution)/shard_map/vmap(jit(searchsorted))/vmap(jit(_searchsorted_scan_impl))/while/body/eval_jaxpr/gather | solution.py:34
  1466.7 0.1 select_select_fusion.5
  1466.8 100.3 %gather_fusion = s32[16384]{0:T(1024)S(1)} fusion(s32[8,16384]{1,0:T(8,128)S(1)} %get-tuple-element.175, u32[16384]{0:T(1024)S(1)} %bitcast.65), kind=kCustom, calls=%fused_computation.clone.clone.1 | custom fusion | bytes 262144 | tf_op jit(solution)/shard_map/vmap(jit(searchsorted))/vmap(jit(_searchsorted_scan_impl))/while/body/eval_jaxpr/gather | solution.py:34
  1567.2 0.1 select_select_fusion.5
  1567.3 100.3 %gather_fusion.3 = s32[16384]{0:T(1024)S(1)} fusion(s32[8,16384]{1,0:T(8,128)S(1)} %copy-done, s32[16384]{0:T(1024)S(1)} %bitcast.67), kind=kCustom, calls=%fused_computation.3 | custom fusion | bytes 262144 | tf_op jit(solution)/shard_map/jit(take_along_axis)/gather | solution.py:37
  1667.8 90.5 %gather_fusion.2 = f32[16384]{0:T(1024)S(1)} fusion(f32[16384]{0:T(1024)S(1)} %convert_element_type.32, s32[16384]{0:T(1024)S(1)} %broadcast_clamp_fusion), kind=kCustom, calls=%fused_computation.2 | custom fusion | bytes 196608 | tf_op jit(solution)/shard_map/gather | solution.py:65
  1758.3 0.7 fusion.19
  1759.0 10.3 all-gather
  1769.3 0.7 slice_reduce_fusion
  1770.0 4.3 reshape.137
  1774.3 1.1 copy.26
  1775.4 1.5 copy.18
  1776.9 187.8 %gather_fusion.5 = bf16[16384,512]{1,0:T(8,128)(2,1)} fusion(bf16[8,128,512]{2,1,0:T(8,128)(2,1)S(1)} %bitcast.66, s32[16384]{0:T(1024)S(1)} %bitcast.69), kind=kCustom, calls=%fused_computation.5 | custom fusion | bytes 33685504 | tf_op jit(solution)/shard_map/while/body/eval_jaxpr/vmap()/gather | solution.py:49
  1964.7 1.3 reshape.126
  1966.1 74.6 %gather_fusion.1 = bf16[16384,512]{1,0:T(8,128)(2,1)} fusion(bf16[16384,512]{1,0:T(8,128)(2,1)} %all-gather.5.cloned.1.call-done, s32[16384]{0:T(1024)S(1)} %broadcast_clamp_fusion), kind=kCustom, calls=%fused_computation.1 | custom fusion | bytes 33619968 | tf_op jit(solution)/shard_map/gather | solution.py:42
  2040.7 13.9 fusion.3
  2054.6 0.3 fusion.31
  2055.0 100.3 %gather_fusion.4 = f32[16384]{0:T(1024)S(1)} fusion(f32[8,16384]{1,0:T(8,128)S(1)} %fusion.31, s32[16384]{0:T(1024)S(1)} %bitcast.68), kind=kCustom, calls=%fused_computation.4 | custom fusion | bytes 262144 | tf_op jit(solution)/shard_map/jit(take_along_axis)/gather | solution.py:64
  2155.3 0.9 fusion.28
  2156.3 8.1 fusion.10
  2164.4 18.0 all_to_all.33
  2182.4 0.7 copy.19
  2183.1 1.3 copy.20
  (125 shorter events, 1.8 us)
Async XLA Ops:
  6.5 37.8 %copy-start.3 = (bf16[4096]{0:T(1024)(128)(2,1)S(1)}, bf16[4096]{0:T(1024)(128)(2,1)}, u32[]{:S(2)}) copy-start(bf16[4096]{0:T(1024)(128)(2,1)} %param.11) | copy-start | bytes 24580
  6.5 51.8 %copy-start = (s32[8,16384]{1,0:T(8,128)S(1)}, s32[8,16384]{1,0:T(8,128)}, u32[]{:S(2)}) copy-start(s32[8,16384]{1,0:T(8,128)} %param.12) | copy-start | bytes 1572868
  6.5 1958.2 %all-gather.7.cloned.1.call-start = ((), (), s32[]{:S(2)}) async-start(), calls=%async_computation.4 | async-start | bytes 1179648 | tf_op jit(solution)/shard_map/all_gather | solution.py:59
  7.3 1958.8 %all-gather.5.cloned.1.call-start = ((), (), s32[]{:S(2)}) async-start(), calls=%async_computation.2 | async-start | bytes 20971520 | tf_op jit(solution)/shard_map/all_gather | solution.py:12
  39.1 1731.0 %all-to-all-start = ((bf16[8,2,32768]{2,1,0:T(2,128)(2,1)}), bf16[8,2,32768]{2,1,0:T(2,128)(2,1)}, u32[]{:S(2)}, u32[]{:S(2)}) async-start(bf16[8,2,32768]{2,1,0:T(2,128)(2,1)} %reshape.136), calls=%async_computation | async-start | bytes 2097152 | tf_op jit(solution)/shard_map/all_to_all | solution.py:10
  44.2 2111.1 %all-reduce.2.cloned.1.call-start = ((), (), s32[]{:S(2)}) async-start(), calls=%async_computation.3 | async-start | bytes 131072 | tf_op jit(solution)/shard_map/psum | solution.py:62
  1667.7 91.3 %copy-start.5 = (bf16[4,8]{1,0:T(4,128)(2,1)S(1)}, bf16[4,8]{1,0:T(4,128)(2,1)}, u32[]{:S(2)}) copy-start(bf16[4,8]{1,0:T(4,128)(2,1)} %param.15) | copy-start | bytes 196
  2040.7 13.9 copy-start.2
  2054.9 100.4 %copy-start.4 = (s32[8]{0:T(128)S(1)}, s32[8]{0:T(128)}, u32[]{:S(2)}) copy-start(s32[8]{0:T(128)} %slice_reduce_fusion) | copy-start | bytes 100
  2054.9 100.4 %copy-start.6 = (s32[8]{0:T(128)S(1)}, s32[8]{0:T(128)}, u32[]{:S(2)}) copy-start(s32[8]{0:T(128)} %param.13) | copy-start | bytes 100
  2054.9 101.3 %copy-start.1 = (s32[8,2048]{1,0:T(8,128)S(1)}, s32[8,2048]{1,0:T(8,128)}, u32[]{:S(2)}) copy-start(s32[8,2048]{1,0:T(8,128)} %get-tuple-element.129) | copy-start | bytes 196612
Sparse Core Ops, SparseCore 0:
  9.2 26.1 all-gather.6
  37.0 287.0 all-gather.4
  2054.7 67.5 all-reduce.1
where the time goes:
time: 2200 us; the launch traced here: 2190 us
  local copies, waits for them, and re-layouts  2080 us (95%)
  blocking collectives  42.3 us (2%)
  other arithmetic  40.8 us (2%)
    gather x15, local copies, waits for them, and re-layouts, on_device(): jnp.searchsorted(row, targets, side='left')  1500 us
    gather x1, local copies, waits for them, and re-layouts, forward_block(): source[where_at]  188 us
    gather x2, local copies, waits for them, and re-layouts, on_device(): hit_grad = jnp.take_along_axis(pooled_grad, slot_vocab, axis=1)  100 us
    gather x2, local copies, waits for them, and re-layouts, on_device(): slot_global = jnp.take_along_axis(argmax, slot_vocab, axis=1)  100 us
    gather x2, local copies, waits for them, and re-layouts, on_device(): shifted = logits + biases.astype(jnp.float32)[slot_vocab]  90.6 us
    gather x1, local copies, waits for them, and re-layouts, on_device(): slot_weights = weights[slot_vocab]  74.6 us
  transfers between devices with their start and end apart: 4, of which 0 were waited for; matrix products, arithmetic and copies ran while one was open for 93% of the time, Pallas kernels for 0%

commit v1 on v0

v1 whole, which is shorter than its diff:
```python
import functools

import jax
import jax.numpy as jnp
from jax import lax
from jax.experimental import pallas as pl
from jax.experimental.pallas import tpu as pltpu
from jax.sharding import PartitionSpec as P

F32, BF16, I32 = jnp.float32, jnp.bfloat16, jnp.int32
CHUNKS = 2
VMEM_LIMIT = 44 * 1024 * 1024


def tile_of(total, want):
    return want if total % want == 0 else total


def forward_kernel(blocks, tile, place, code, weights, own, *rest):
    from_right, from_left = rest[: blocks - 1], rest[blocks - 1 : 2 * (blocks - 1)]
    out, rows = rest[2 * (blocks - 1) :]
    part = own.shape[1]
    doc = pl.program_id(0)
    rows[pl.ds(0, part), :] = own[0]
    for slot in range(1, blocks):
        where_at = pl.ds(slot * part, part)

        @pl.when(place[0] + slot < blocks)
        def _(slot=slot, where_at=where_at):
            rows[where_at, :] = from_right[slot - 1][0]

        @pl.when(place[0] + slot >= blocks)
        def _(slot=slot, where_at=where_at):
            rows[where_at, :] = from_left[blocks - slot - 1][0]

    held = rows[...]
    for start in range(0, weights.shape[1], tile):
        cols = pl.ds(start, tile)
        scores = jnp.dot(held, weights[:, cols], preferred_element_type=F32)
        ids = lax.broadcasted_iota(I32, scores.shape, 0)
        hit = ids == code[pl.ds(doc, 1), cols]
        out[pl.ds(doc, 1), cols] = jnp.sum(jnp.where(hit, scores, 0.0), axis=0, keepdims=True)


def backward_kernel(blocks, tile, code, weights, logits, pooled, bias, *rest):
    outs, delta = rest[:blocks], rest[blocks]
    part = outs[0].shape[1]
    doc = pl.program_id(0)

    @pl.when(doc == 0)
    def _():
        x = logits[...] + bias[...]
        soft = jnp.maximum(x, 0.0) + jnp.log1p(jnp.exp(-jnp.abs(x)))
        factor = pooled[...] * jax.nn.sigmoid(x) / (1.0 + soft)
        delta[...] = factor.astype(BF16).astype(F32)

    total = jnp.zeros((blocks * part, weights.shape[1]), F32)
    for start in range(0, weights.shape[0], tile):
        cols = pl.ds(start, tile)
        ids = lax.broadcasted_iota(I32, (blocks * part, tile), 0)
        hit = ids == code[pl.ds(doc, 1), cols]
        spread = jnp.where(hit, delta[pl.ds(doc, 1), cols], 0.0).astype(BF16)
        total += jnp.dot(spread, weights[cols, :], preferred_element_type=F32)
    for slot in range(blocks):
        outs[slot][0] = total[slot * part : (slot + 1) * part]


def forward(place, code, weights_t, own, from_right, from_left):
    docs, part, width = own.shape
    blocks = len(from_right) + 1
    entries = weights_t.shape[1]
    rows = pl.BlockSpec((1, part, width), lambda d, s: (d, 0, 0))
    flops = 2 * docs * blocks * part * width * entries
    return pl.pallas_call(
        functools.partial(forward_kernel, blocks, tile_of(entries, 512)),
        out_shape=jax.ShapeDtypeStruct((docs, entries), F32),
        grid_spec=pltpu.PrefetchScalarGridSpec(
            num_scalar_prefetch=1,
            grid=(docs,),
            in_specs=[
                pl.BlockSpec((docs, entries), lambda d, s: (0, 0)),
                pl.BlockSpec((width, entries), lambda d, s: (0, 0)),
            ]
            + [rows] * (2 * blocks - 1),
            out_specs=pl.BlockSpec((docs, entries), lambda d, s: (0, 0)),
            scratch_shapes=[pltpu.VMEM((blocks * part, width), BF16)],
        ),
        compiler_params=pltpu.CompilerParams(vmem_limit_bytes=VMEM_LIMIT),
        cost_estimate=pl.CostEstimate(flops=flops, bytes_accessed=8 << 20, transcendentals=0),
        name="forward",
    )(place, code, weights_t, own, *from_right, *from_left)


def backward(code, weights, logits, pooled, bias, blocks, part):
    docs, entries = code.shape
    width = weights.shape[1]
    whole = pl.BlockSpec((docs, entries), lambda d: (0, 0))
    flops = 2 * docs * blocks * part * width * entries
    return pl.pallas_call(
        functools.partial(backward_kernel, blocks, tile_of(entries, 512)),
        out_shape=[jax.ShapeDtypeStruct((docs, part, width), F32)] * blocks,
        grid=(docs,),
        in_specs=[
            whole,
            pl.BlockSpec((entries, width), lambda d: (0, 0)),
            whole,
            whole,
            pl.BlockSpec((1, entries), lambda d: (0, 0)),
        ],
        out_specs=[pl.BlockSpec((1, part, width), lambda d: (d, 0, 0))] * blocks,
        scratch_shapes=[pltpu.VMEM((docs, entries), F32)],
        compiler_params=pltpu.CompilerParams(vmem_limit_bytes=VMEM_LIMIT),
        cost_estimate=pl.CostEstimate(flops=flops, bytes_accessed=8 << 20, transcendentals=0),
        name="backward",
    )(code, weights, logits, pooled, bias)


def gather_chain(own, blocks):
    from_right, from_left = [], []
    a = b = own
    for hop in range(1, blocks):
        a = lax.ppermute(a, "seq", [(i, i - 1) for i in range(1, blocks - hop + 1)])
        b = lax.ppermute(b, "seq", [(i, i + 1) for i in range(hop - 1, blocks - 1)])
        from_right.append(a)
        from_left.append(b)
    return from_right, from_left


def reduce_chain(grads, blocks):
    up = down = None
    for hop in range(1, blocks):
        a, b = grads[blocks - hop], grads[hop]
        if hop > 1:
            a, b = a + up.astype(F32), b + down.astype(F32)
        up = lax.ppermute(a.astype(BF16), "seq", [(i, i + 1) for i in range(hop)])
        down = lax.ppermute(b.astype(BF16), "seq", [(i, i - 1) for i in range(blocks - hop, blocks)])
    total = grads[0]
    if up is not None:
        total = total + up.astype(F32) + down.astype(F32)
    return total.astype(BF16)


def sum_over_dp(value, size):
    step = 1
    while step < size:
        value = value + lax.ppermute(value, "dp", [(i, i ^ step) for i in range(size)])
        step *= 2
    return value


def on_device(hidden, head_weight, head_bias, argmax, lengths, query_terms, score_grad):
    blocks, size = lax.axis_size("seq"), lax.axis_size("dp")
    z = lax.axis_index("seq")
    tok_rows = hidden.shape[1]
    entries, width = head_weight.shape
    part = tok_rows // CHUNKS

    queries = lax.all_gather(
        lax.dynamic_slice_in_dim(query_terms, z * entries, entries, 1), "dp", axis=0, tiled=True
    )
    score_all = lax.all_gather(score_grad, "dp", axis=0, tiled=True)
    pooled = jnp.einsum("jd,jv->dv", score_all, queries, preferred_element_type=F32)
    bias = head_bias.astype(F32)[None, :]
    weights_t = head_weight.T

    saved = lax.dynamic_slice_in_dim(argmax, z * entries, entries, 1)
    block = saved // tok_rows
    inner = saved - block * tok_rows
    slot = jnp.where(block >= z, block - z, block - z + blocks)
    kept = (block < blocks) & (saved < lengths[:, None])
    place = jnp.reshape(z, (1,)).astype(I32)

    results = []
    for chunk in range(CHUNKS):
        first = chunk * part
        here = kept & (inner >= first) & (inner < first + part)
        code = jnp.where(here, slot * part + inner - first, -1)
        sent = hidden[:, first : first + part]
        sent = sent.reshape(-1, part, size, width).transpose(2, 0, 1, 3).reshape(-1, part, width)
        own = lax.all_to_all(sent, "dp", split_axis=0, concat_axis=0, tiled=True)
        from_right, from_left = gather_chain(own, blocks)
        partial = forward(place, code, weights_t, own, from_right, from_left)
        logits = sum_over_dp(partial, size)
        grads = backward(code, head_weight, logits, pooled, bias, blocks, part)
        mine = reduce_chain(grads, blocks)
        back = lax.all_to_all(mine, "dp", split_axis=0, concat_axis=0, tiled=True)
        back = back.reshape(size, -1, part, width).transpose(1, 2, 0, 3)
        results.append(back.reshape(-1, part, size * width))
    return jnp.concatenate(results, axis=1)


def solution(mesh):
    return jax.shard_map(
        on_device,
        mesh=mesh,
        in_specs=(
            P("dp", "seq", None),
            P("seq", "dp"),
            P("seq"),
            P(),
            P(),
            P("dp", None),
            P("dp", None),
        ),
        out_specs=P("dp", "seq", None),
        check_vma=False,
    )
```

time: 2200 us -> 266 us (0.12)
  the two profiles are of different devices: /device:TPU:0 before, /device:TPU:16 now
where the time goes in v1:
time: 266 us; the launch traced here: 265 us
  waiting for transfers between devices  87.6 us (33%)
  starting transfers between devices  72.2 us (27%)
  blocking collectives  42.8 us (16%)
  Pallas kernels  42.8 us (16%)
  local copies, waits for them, and re-layouts  12.3 us (5%)
  other arithmetic  6.61 us (2%)
    ppermute x6, waiting for transfers between devices, reduce_chain(): lax.ppermute(b.astype(BF16), 'seq', [(i, i - 1) for i in range(blocks - h...  30.5 us
    all_to_all x2, blocking collectives, on_device(): own = lax.all_to_all(sent, 'dp', split_axis=0, concat_axis=0, tiled=True)  25.4 us
    pallas_call x2, Pallas kernels, forward(): pl.pallas_call(functools.partial(forward_kernel, blocks, tile_of(entries,...  22.6 us
    ppermute x6, waiting for transfers between devices, reduce_chain(): up = lax.ppermute(a.astype(BF16), 'seq', [(i, i + 1) for i in range(hop)])  21.9 us
    pallas_call x2, Pallas kernels, backward(): pl.pallas_call(functools.partial(backward_kernel, blocks, tile_of(entries...  20.3 us
    ppermute x6, starting transfers between devices, gather_chain(): b = lax.ppermute(b, 'seq', [(i, i + 1) for i in range(hop - 1, blocks - 1)])  18.9 us
    ppermute x6, starting transfers between devices, reduce_chain(): lax.ppermute(b.astype(BF16), 'seq', [(i, i - 1) for i in range(blocks - h...  15.8 us
    ppermute x6, waiting for transfers between devices, gather_chain(): b = lax.ppermute(b, 'seq', [(i, i + 1) for i in range(hop - 1, blocks - 1)])  15.4 us
  transfers between devices with their start and end apart: 32, of which 16 were waited for; matrix products, arithmetic and copies ran while one was open for 5% of the time, Pallas kernels for 16%

profile of v1, /device:TPU:16, one launch (start us, length us, event | category | flops | bytes accessed | tf_op | source)
XLA Modules:
  0.0 265.1 jit_solution(11642508121802557022)
XLA Ops:
  0.0 1.3 fusion.4
  1.4 13.3 %all_to_all.20.own = bf16[8,64,512]{2,1,0:T(8,128)(2,1)S(1)} all-to-all(bf16[8,64,512]{2,1,0:T(8,128)(2,1)S(1)} %bitcast.45), channel_id=1, replica_groups=mesh['dp'=8,'seq'=4] {'dp'}, dimensions={0} | all-to-all | bytes 1048576 | tf_op jit(solution)/shard_map/all_to_all | solution.py:180
  14.6 2.3 collective-permute-start
  17.0 3.5 %collective-permute-start.3 = (bf16[8,64,512]{2,1,0:T(8,128)(2,1)S(1)}, bf16[8,64,512]{2,1,0:T(8,128)(2,1)S(1)}, u32[]{:S(2)}, u32[]{:S(2)}) collective-permute-start(bf16[8,64,512]{2,1,0:T(8,128)(2,1)S(1)} %all_to_all.20.own), channel_id=1, source_target_pairs={{0,1},{1,2},{2,3},{4,5},{5,6},{6,7},{8,9},{9,10},{10,11},{12,13},{... | collective-permute-start | bytes 1572872 | tf_op jit(solution)/shard_map/ppermute | solution.py:123
  20.5 12.2 %all_to_all.21.own = bf16[8,64,512]{2,1,0:T(8,128)(2,1)S(1)} all-to-all(bf16[8,64,512]{2,1,0:T(8,128)(2,1)S(1)} %bitcast.46), channel_id=1, replica_groups=mesh['dp'=8,'seq'=4] {'dp'}, dimensions={0} | all-to-all | bytes 1048576 | tf_op jit(solution)/shard_map/all_to_all | solution.py:180
  32.7 2.3 collective-permute-start.15
  35.0 3.5 %collective-permute-start.18 = (bf16[8,64,512]{2,1,0:T(8,128)(2,1)S(1)}, bf16[8,64,512]{2,1,0:T(8,128)(2,1)S(1)}, u32[]{:S(2)}, u32[]{:S(2)}) collective-permute-start(bf16[8,64,512]{2,1,0:T(8,128)(2,1)S(1)} %all_to_all.21.own), channel_id=1, source_target_pairs={{0,1},{1,2},{2,3},{4,5},{5,6},{6,7},{8,9},{9,10},{10,11},{12,13},{... | collective-permute-start | bytes 1572872 | tf_op jit(solution)/shard_map/ppermute | solution.py:123
  38.6 3.1 %collective-permute-start.1 = (bf16[8,64,512]{2,1,0:T(8,128)(2,1)S(1)}, bf16[8,64,512]{2,1,0:T(8,128)(2,1)}, u32[]{:S(2)}, u32[]{:S(2)}) collective-permute-start(bf16[8,64,512]{2,1,0:T(8,128)(2,1)S(1)} %collective-permute-done.rest_0_), channel_id=1, source_target_pairs={{1,0},{2,1},{5,4},{6,5},{9,8},{10,9},{13,12},{14,13},{17,16},{18,1... | collective-permute-start | bytes 1572872 | tf_op jit(solution)/shard_map/ppermute | solution.py:122
  41.7 1.9 collective-permute-start.4
  43.6 6.4 %copy.14 = bf16[4096,512]{0,1:T(8,128)(2,1)} copy(bf16[4096,512]{1,0:T(8,128)(2,1)} %weights.3) | data formatting | bytes 8388608 | tf_op args[1]
  50.0 4.8 %collective-permute-start.16 = (bf16[8,64,512]{2,1,0:T(8,128)(2,1)S(1)}, bf16[8,64,512]{2,1,0:T(8,128)(2,1)S(1)}, u32[]{:S(2)}, u32[]{:S(2)}) collective-permute-start(bf16[8,64,512]{2,1,0:T(8,128)(2,1)S(1)} %collective-permute-done.15.rest_0_), channel_id=1, source_target_pairs={{1,0},{2,1},{5,4},{6,5},{9,8},{10,9},{13,12},{14,13},{17,16},{18,1... | collective-permute-start | bytes 1572872 | tf_op jit(solution)/shard_map/ppermute | solution.py:122
  54.8 1.9 collective-permute-start.19
  56.8 1.9 collective-permute-done.1.rest_1_
  58.6 0.7 collective-permute-start.2
  59.3 3.8 %collective-permute-done.4.rest_4_ = bf16[8,64,512]{2,1,0:T(8,128)(2,1)} collective-permute-done((bf16[8,64,512]{2,1,0:T(8,128)(2,1)S(1)}, bf16[8,64,512]{2,1,0:T(8,128)(2,1)}, u32[]{:S(2)}, u32[]{:S(2)}) %collective-permute-start.4) | collective-permute-done | bytes 524320 | tf_op jit(solution)/shard_map/ppermute | solution.py:123
  63.1 3.6 %collective-permute-start.5 = (bf16[8,64,512]{2,1,0:T(8,128)(2,1)}, bf16[8,64,512]{2,1,0:T(8,128)(2,1)S(1)}, u32[]{:S(2)}, u32[]{:S(2)}) collective-permute-start(bf16[8,64,512]{2,1,0:T(8,128)(2,1)} %collective-permute-done.4.rest_4_), channel_id=1, source_target_pairs={{2,3},{6,7},{10,11},{14,15},{18,19},{22,23},{26,27},{30,31}} | collective-permute-start | bytes 1572872 | tf_op jit(solution)/shard_map/ppermute | solution.py:123
  66.7 1.1 and_select_fusion
  68.0 0.7 collective-permute-start.17
  68.7 4.7 %collective-permute-done.19.rest_4_ = bf16[8,64,512]{2,1,0:T(8,128)(2,1)S(1)} collective-permute-done((bf16[8,64,512]{2,1,0:T(8,128)(2,1)S(1)}, bf16[8,64,512]{2,1,0:T(8,128)(2,1)S(1)}, u32[]{:S(2)}, u32[]{:S(2)}) %collective-permute-start.19) | collective-permute-done | bytes 524320 | tf_op jit(solution)/shard_map/ppermute | solution.py:123
  73.4 4.4 %collective-permute-start.20 = (bf16[8,64,512]{2,1,0:T(8,128)(2,1)S(1)}, bf16[8,64,512]{2,1,0:T(8,128)(2,1)S(1)}, u32[]{:S(2)}, u32[]{:S(2)}) collective-permute-start(bf16[8,64,512]{2,1,0:T(8,128)(2,1)S(1)} %collective-permute-done.19.rest_4_), channel_id=1, source_target_pairs={{2,3},{6,7},{10,11},{14,15},{18,19},{22,23},{26,27},{30,31}} | collective-permute-start | bytes 1572872 | tf_op jit(solution)/shard_map/ppermute | solution.py:123
  77.8 6.9 %collective-permute-done.5.rest_5_ = bf16[8,64,512]{2,1,0:T(8,128)(2,1)S(1)} collective-permute-done((bf16[8,64,512]{2,1,0:T(8,128)(2,1)}, bf16[8,64,512]{2,1,0:T(8,128)(2,1)S(1)}, u32[]{:S(2)}, u32[]{:S(2)}) %collective-permute-start.5) | collective-permute-done | bytes 524320 | tf_op jit(solution)/shard_map/ppermute | solution.py:123
  84.7 2.2 copy-done.2
  86.9 11.8 %forward.2 = f32[8,4096]{1,0:T(8,128)S(1)} custom-call(s32[1]{0:T(128)} %bitcast.place, s32[8,4096]{1,0:T(8,128)S(1)} %get-tuple-element.27.code, bf16[512,4096]{1,0:T(8,128)(2,1)S(1)} %bitcast.39, bf16[8,64,512]{2,1,0:T(8,128)(2,1)S(1)} %all_to_all.20.own, bf16[8,64,512]{2,1,0:T(8,128)(2,1)S(1)} %collective-permute-done.rest_0_, ...), custom_call_target="tpu_custom_call" | custom-call | flops 8589934592 | bytes 8388608 | tf_op jit(solution)/shard_map/forward/pallas_call | solution.py:74
  98.8 10.8 %forward.3 = f32[8,4096]{1,0:T(8,128)S(1)} custom-call(s32[1]{0:T(128)} %bitcast.place, s32[8,4096]{1,0:T(8,128)S(1)} %get-tuple-element.28.code, bf16[512,4096]{1,0:T(8,128)(2,1)S(1)} %bitcast.40, bf16[8,64,512]{2,1,0:T(8,128)(2,1)S(1)} %all_to_all.21.own, bf16[8,64,512]{2,1,0:T(8,128)(2,1)S(1)} %collective-permute-done.15.rest_0_, ...), custom_call_target="tpu_custom_call" | custom-call | flops 8589934592 | bytes 8388608 | tf_op jit(solution)/shard_map/forward/pallas_call | solution.py:74
  109.7 0.5 collective-permute-start.21
  110.2 0.6 collective-permute-start.7
  110.8 9.3 %all-gather = bf16[8,4,4096]{2,1,0:T(4,128)(2,1)S(1)} all-gather(bf16[1,4,4096]{2,1,0:T(4,128)(2,1)S(1)} %dynamic-slice_bitcast_fusion), channel_id=1, replica_groups=mesh['dp'=8,'seq'=4] {'dp'}, dimensions={0}, use_global_device_ids=true | all-gather | bytes 294912 | tf_op jit(solution)/shard_map/all_gather | solution.py:158
  120.2 8.1 %all-gather.1 = bf16[8,4,8]{2,1,0:T(4,128)(2,1)S(1)} all-gather(bf16[1,4,8]{2,1,0:T(4,128)(2,1)S(1)} %bitcast.52), channel_id=1, replica_groups=mesh['dp'=8,'seq'=4] {'dp'}, dimensions={0}, use_global_device_ids=true | all-gather | bytes 576 | tf_op jit(solution)/shard_map/all_gather | solution.py:161
  128.3 1.4 collective-permute-start.22
  129.8 0.8 collective-permute-start.8
  130.5 0.2 convolution_bitcast_fusion.pooled
  130.7 3.4 %collective-permute-done.22 = f32[8,4096]{1,0:T(8,128)S(1)} collective-permute-done((f32[8,4096]{1,0:T(8,128)S(1)}, f32[8,4096]{1,0:T(8,128)S(1)}, u32[]{:S(2)}, u32[]{:S(2)}) %collective-permute-start.22) | collective-permute-done | bytes 131104 | tf_op jit(solution)/shard_map/ppermute | solution.py:146
  134.2 1.4 collective-permute-start.23
  135.6 2.2 copy-done.1
  137.8 10.1 %backward.2 = (f32[8,64,512]{2,1,0:T(8,128)S(1)}, f32[8,64,512]{2,1,0:T(8,128)S(1)}, f32[8,64,512]{2,1,0:T(8,128)S(1)}, f32[8,64,512]{2,1,0:T(8,128)S(1)}) custom-call(s32[8,4096]{1,0:T(8,128)S(1)} %get-tuple-element.27.code, bf16[4096,512]{1,0:T(8,128)(2,1)S(1)} %copy-done.1, f32[8,4096]{1,0:T(8,128)S(1)} %add.72.logits, ...), custom_call_target="tpu_custom_call" | custom-call | flops 8589934592 | bytes 8388608 | tf_op jit(solution)/shard_map/backward/pallas_call | solution.py:99
  148.0 0.7 collective-permute-start.9
  148.7 10.1 %backward.3 = (f32[8,64,512]{2,1,0:T(8,128)S(1)}, f32[8,64,512]{2,1,0:T(8,128)S(1)}, f32[8,64,512]{2,1,0:T(8,128)S(1)}, f32[8,64,512]{2,1,0:T(8,128)S(1)}) custom-call(s32[8,4096]{1,0:T(8,128)S(1)} %get-tuple-element.28.code, bf16[4096,512]{1,0:T(8,128)(2,1)S(1)} %copy-done.1, f32[8,4096]{1,0:T(8,128)S(1)} %add.81.logits, ...), custom_call_target="tpu_custom_call" | custom-call | flops 8589934592 | bytes 8388608 | tf_op jit(solution)/shard_map/backward/pallas_call | solution.py:99
  158.9 0.7 collective-permute-start.24
  159.8 1.3 collective-permute-start.10
  161.3 1.3 collective-permute-start.25
  162.6 14.0 %collective-permute-done.10 = bf16[8,64,512]{2,1,0:T(8,128)(2,1)S(1)} collective-permute-done((bf16[8,64,512]{2,1,0:T(8,128)(2,1)S(1)}, bf16[8,64,512]{2,1,0:T(8,128)(2,1)S(1)}, u32[]{:S(2)}, u32[]{:S(2)}) %collective-permute-start.10) | collective-permute-done | bytes 524320 | tf_op jit(solution)/shard_map/ppermute | solution.py:135
  176.8 1.3 collective-permute-start.12
  178.1 7.9 %collective-permute-done.25 = bf16[8,64,512]{2,1,0:T(8,128)(2,1)S(1)} collective-permute-done((bf16[8,64,512]{2,1,0:T(8,128)(2,1)S(1)}, bf16[8,64,512]{2,1,0:T(8,128)(2,1)S(1)}, u32[]{:S(2)}, u32[]{:S(2)}) %collective-permute-start.25) | collective-permute-done | bytes 524320 | tf_op jit(solution)/shard_map/ppermute | solution.py:135
  186.2 1.3 collective-permute-start.27
  187.5 1.8 collective-permute-done.12
  189.4 7.5 %collective-permute-start.13 = (bf16[8,64,512]{2,1,0:T(8,128)(2,1)S(1)}, bf16[8,64,512]{2,1,0:T(8,128)(2,1)S(1)}, u32[]{:S(2)}, u32[]{:S(2)}) collective-permute-start(bf16[8,64,512]{2,1,0:T(8,128)(2,1)S(1)} %add_convert_fusion.7), channel_id=1, source_target_pairs={{2,1},{3,2},{6,5},{7,6},{10,9},{11,10},{14,13},{15,14},{18,17},{19... | collective-permute-start | bytes 1572872 | tf_op jit(solution)/shard_map/ppermute | solution.py:136
  196.9 6.0 %collective-permute-done.27 = bf16[8,64,512]{2,1,0:T(8,128)(2,1)S(1)} collective-permute-done((bf16[8,64,512]{2,1,0:T(8,128)(2,1)S(1)}, bf16[8,64,512]{2,1,0:T(8,128)(2,1)S(1)}, u32[]{:S(2)}, u32[]{:S(2)}) %collective-permute-start.27) | collective-permute-done | bytes 524320 | tf_op jit(solution)/shard_map/ppermute | solution.py:136
  203.1 1.9 collective-permute-start.28
  205.1 4.0 %collective-permute-start.11 = (bf16[8,64,512]{2,1,0:T(8,128)(2,1)S(1)}, bf16[8,64,512]{2,1,0:T(8,128)(2,1)S(1)}, u32[]{:S(2)}, u32[]{:S(2)}) collective-permute-start(bf16[8,64,512]{2,1,0:T(8,128)(2,1)S(1)} %get-tuple-element.21), channel_id=1, source_target_pairs={{0,1},{1,2},{2,3},{4,5},{5,6},{6,7},{8,9},{9,10},{10,11},{12,13},{... | collective-permute-start | bytes 1572872 | tf_op jit(solution)/shard_map/ppermute | solution.py:135
  209.0 5.2 %collective-permute-done.13 = bf16[8,64,512]{2,1,0:T(8,128)(2,1)S(1)} collective-permute-done((bf16[8,64,512]{2,1,0:T(8,128)(2,1)S(1)}, bf16[8,64,512]{2,1,0:T(8,128)(2,1)S(1)}, u32[]{:S(2)}, u32[]{:S(2)}) %collective-permute-start.13) | collective-permute-done | bytes 524320 | tf_op jit(solution)/shard_map/ppermute | solution.py:136
  214.4 1.9 collective-permute-start.14
  216.3 4.0 %collective-permute-start.26 = (bf16[8,64,512]{2,1,0:T(8,128)(2,1)S(1)}, bf16[8,64,512]{2,1,0:T(8,128)(2,1)S(1)}, u32[]{:S(2)}, u32[]{:S(2)}) collective-permute-start(bf16[8,64,512]{2,1,0:T(8,128)(2,1)S(1)} %get-tuple-element.25), channel_id=1, source_target_pairs={{0,1},{1,2},{2,3},{4,5},{5,6},{6,7},{8,9},{9,10},{10,11},{12,13},{... | collective-permute-start | bytes 1572872 | tf_op jit(solution)/shard_map/ppermute | solution.py:135
  220.3 5.2 %collective-permute-done.28 = bf16[8,64,512]{2,1,0:T(8,128)(2,1)S(1)} collective-permute-done((bf16[8,64,512]{2,1,0:T(8,128)(2,1)S(1)}, bf16[8,64,512]{2,1,0:T(8,128)(2,1)S(1)}, u32[]{:S(2)}, u32[]{:S(2)}) %collective-permute-start.28) | collective-permute-done | bytes 524320 | tf_op jit(solution)/shard_map/ppermute | solution.py:136
  225.4 1.0 add_convert_fusion.1
  226.4 1.9 collective-permute-start.29
  228.3 8.4 %collective-permute-done.14 = bf16[8,64,512]{2,1,0:T(8,128)(2,1)S(1)} collective-permute-done((bf16[8,64,512]{2,1,0:T(8,128)(2,1)S(1)}, bf16[8,64,512]{2,1,0:T(8,128)(2,1)S(1)}, u32[]{:S(2)}, u32[]{:S(2)}) %collective-permute-start.14) | collective-permute-done | bytes 524320 | tf_op jit(solution)/shard_map/ppermute | solution.py:136
  236.7 1.0 add_convert_fusion.5
  237.7 3.5 %all-to-all-start.1 = ((bf16[8,64,512]{2,1,0:T(8,128)(2,1)}), bf16[8,64,512]{2,1,0:T(8,128)(2,1)S(1)}, u32[]{:S(2)}, u32[]{:S(2)}) async-start(bf16[8,64,512]{2,1,0:T(8,128)(2,1)} %add_convert_fusion.5), calls=%async_computation.1 | async-start | bytes 1048576 | tf_op jit(solution)/shard_map/all_to_all | solution.py:186
  241.2 4.0 %collective-permute-done.29 = bf16[8,64,512]{2,1,0:T(8,128)(2,1)S(1)} collective-permute-done((bf16[8,64,512]{2,1,0:T(8,128)(2,1)}, bf16[8,64,512]{2,1,0:T(8,128)(2,1)S(1)}, u32[]{:S(2)}, u32[]{:S(2)}) %collective-permute-start.29) | collective-permute-done | bytes 524320 | tf_op jit(solution)/shard_map/ppermute | solution.py:136
  245.2 1.0 add_convert_fusion
  246.2 4.7 %all-to-all-done.1 = bf16[8,64,512]{2,1,0:T(8,128)(2,1)S(1)} async-done(((bf16[8,64,512]{2,1,0:T(8,128)(2,1)}), bf16[8,64,512]{2,1,0:T(8,128)(2,1)S(1)}, u32[]{:S(2)}, u32[]{:S(2)}) %all-to-all-start.1) | async-done | bytes 524320 | tf_op jit(solution)/shard_map/all_to_all | solution.py:186
  250.9 3.5 %all-to-all-start.3 = ((bf16[8,64,512]{2,1,0:T(8,128)(2,1)}), bf16[8,64,512]{2,1,0:T(8,128)(2,1)S(1)}, u32[]{:S(2)}, u32[]{:S(2)}) async-start(bf16[8,64,512]{2,1,0:T(8,128)(2,1)} %add_convert_fusion), calls=%async_computation.3 | async-start | bytes 1048576 | tf_op jit(solution)/shard_map/all_to_all | solution.py:186
  254.4 9.6 %all-to-all-done.3 = bf16[8,64,512]{2,1,0:T(8,128)(2,1)S(1)} async-done(((bf16[8,64,512]{2,1,0:T(8,128)(2,1)}), bf16[8,64,512]{2,1,0:T(8,128)(2,1)S(1)}, u32[]{:S(2)}, u32[]{:S(2)}) %all-to-all-start.3) | async-done | bytes 524320 | tf_op jit(solution)/shard_map/all_to_all | solution.py:186
  264.1 1.1 pad_maximum_fusion
  (50 shorter events, 2.0 us)
Async XLA Ops:
  0.0 110.8 %copy-start = (bf16[4,16384]{1,0:T(4,128)(2,1)S(1)}, bf16[4,16384]{1,0:T(4,128)(2,1)}, u32[]{:S(2)}) copy-start(bf16[4,16384]{1,0:T(4,128)(2,1)} %param.12) | copy-start | bytes 393220
  14.6 24.0 %collective-permute-start = (bf16[8,64,512]{2,1,0:T(8,128)(2,1)S(1)}, bf16[8,64,512]{2,1,0:T(8,128)(2,1)S(1)}, u32[]{:S(2)}, u32[]{:S(2)}) collective-permute-start(bf16[8,64,512]{2,1,0:T(8,128)(2,1)S(1)} %all_to_all.20.own), channel_id=1, source_target_pairs={{1,0},{2,1},{3,2},{5,4},{6,5},{7,6},{9,8},{10,9},{11,10},{13,12},{... | collective-permute-start | bytes 1572872 | tf_op jit(solution)/shard_map/ppermute | solution.py:122
  17.0 24.7 %collective-permute-start.3 = (bf16[8,64,512]{2,1,0:T(8,128)(2,1)S(1)}, bf16[8,64,512]{2,1,0:T(8,128)(2,1)S(1)}, u32[]{:S(2)}, u32[]{:S(2)}) collective-permute-start(bf16[8,64,512]{2,1,0:T(8,128)(2,1)S(1)} %all_to_all.20.own), channel_id=1, source_target_pairs={{0,1},{1,2},{2,3},{4,5},{5,6},{6,7},{8,9},{9,10},{10,11},{12,13},{... | collective-permute-start | bytes 1572872 | tf_op jit(solution)/shard_map/ppermute | solution.py:123
  32.7 17.3 %collective-permute-start.15 = (bf16[8,64,512]{2,1,0:T(8,128)(2,1)S(1)}, bf16[8,64,512]{2,1,0:T(8,128)(2,1)S(1)}, u32[]{:S(2)}, u32[]{:S(2)}) collective-permute-start(bf16[8,64,512]{2,1,0:T(8,128)(2,1)S(1)} %all_to_all.21.own), channel_id=1, source_target_pairs={{1,0},{2,1},{3,2},{5,4},{6,5},{7,6},{9,8},{10,9},{11,10},{13,12},{... | collective-permute-start | bytes 1572872 | tf_op jit(solution)/shard_map/ppermute | solution.py:122
  35.0 19.8 %collective-permute-start.18 = (bf16[8,64,512]{2,1,0:T(8,128)(2,1)S(1)}, bf16[8,64,512]{2,1,0:T(8,128)(2,1)S(1)}, u32[]{:S(2)}, u32[]{:S(2)}) collective-permute-start(bf16[8,64,512]{2,1,0:T(8,128)(2,1)S(1)} %all_to_all.21.own), channel_id=1, source_target_pairs={{0,1},{1,2},{2,3},{4,5},{5,6},{6,7},{8,9},{9,10},{10,11},{12,13},{... | collective-permute-start | bytes 1572872 | tf_op jit(solution)/shard_map/ppermute | solution.py:123
  38.6 20.0 %collective-permute-start.1 = (bf16[8,64,512]{2,1,0:T(8,128)(2,1)S(1)}, bf16[8,64,512]{2,1,0:T(8,128)(2,1)}, u32[]{:S(2)}, u32[]{:S(2)}) collective-permute-start(bf16[8,64,512]{2,1,0:T(8,128)(2,1)S(1)} %collective-permute-done.rest_0_), channel_id=1, source_target_pairs={{1,0},{2,1},{5,4},{6,5},{9,8},{10,9},{13,12},{14,13},{17,16},{18,1... | collective-permute-start | bytes 1572872 | tf_op jit(solution)/shard_map/ppermute | solution.py:122
  41.7 21.4 %collective-permute-start.4 = (bf16[8,64,512]{2,1,0:T(8,128)(2,1)S(1)}, bf16[8,64,512]{2,1,0:T(8,128)(2,1)}, u32[]{:S(2)}, u32[]{:S(2)}) collective-permute-start(bf16[8,64,512]{2,1,0:T(8,128)(2,1)S(1)} %collective-permute-done.3.rest_3_), channel_id=1, source_target_pairs={{1,2},{2,3},{5,6},{6,7},{9,10},{10,11},{13,14},{14,15},{17,18},{18... | collective-permute-start | bytes 1572872 | tf_op jit(solution)/shard_map/ppermute | solution.py:123
  43.6 23.1 %copy-start.5 = (s32[8]{0:T(128)S(1)}, s32[8]{0:T(128)}, u32[]{:S(2)}) copy-start(s32[8]{0:T(128)} %param.11) | copy-start | bytes 100
  50.0 18.0 %collective-permute-start.16 = (bf16[8,64,512]{2,1,0:T(8,128)(2,1)S(1)}, bf16[8,64,512]{2,1,0:T(8,128)(2,1)S(1)}, u32[]{:S(2)}, u32[]{:S(2)}) collective-permute-start(bf16[8,64,512]{2,1,0:T(8,128)(2,1)S(1)} %collective-permute-done.15.rest_0_), channel_id=1, source_target_pairs={{1,0},{2,1},{5,4},{6,5},{9,8},{10,9},{13,12},{14,13},{17,16},{18,1... | collective-permute-start | bytes 1572872 | tf_op jit(solution)/shard_map/ppermute | solution.py:122
  54.8 18.6 %collective-permute-start.19 = (bf16[8,64,512]{2,1,0:T(8,128)(2,1)S(1)}, bf16[8,64,512]{2,1,0:T(8,128)(2,1)S(1)}, u32[]{:S(2)}, u32[]{:S(2)}) collective-permute-start(bf16[8,64,512]{2,1,0:T(8,128)(2,1)S(1)} %collective-permute-done.18.rest_3_), channel_id=1, source_target_pairs={{1,2},{2,3},{5,6},{6,7},{9,10},{10,11},{13,14},{14,15},{17,18},{18... | collective-permute-start | bytes 1572872 | tf_op jit(solution)/shard_map/ppermute | solution.py:123
  58.6 19.2 %collective-permute-start.2 = (bf16[8,64,512]{2,1,0:T(8,128)(2,1)}, bf16[8,64,512]{2,1,0:T(8,128)(2,1)S(1)}, u32[]{:S(2)}, u32[]{:S(2)}) collective-permute-start(bf16[8,64,512]{2,1,0:T(8,128)(2,1)} %collective-permute-done.1.rest_1_), channel_id=1, source_target_pairs={{1,0},{5,4},{9,8},{13,12},{17,16},{21,20},{25,24},{29,28}} | collective-permute-start | bytes 1572872 | tf_op jit(solution)/shard_map/ppermute | solution.py:122
  63.1 21.6 %collective-permute-start.5 = (bf16[8,64,512]{2,1,0:T(8,128)(2,1)}, bf16[8,64,512]{2,1,0:T(8,128)(2,1)S(1)}, u32[]{:S(2)}, u32[]{:S(2)}) collective-permute-start(bf16[8,64,512]{2,1,0:T(8,128)(2,1)} %collective-permute-done.4.rest_4_), channel_id=1, source_target_pairs={{2,3},{6,7},{10,11},{14,15},{18,19},{22,23},{26,27},{30,31}} | collective-permute-start | bytes 1572872 | tf_op jit(solution)/shard_map/ppermute | solution.py:123
  68.0 30.8 %collective-permute-start.17 = (bf16[8,64,512]{2,1,0:T(8,128)(2,1)S(1)}, bf16[8,64,512]{2,1,0:T(8,128)(2,1)S(1)}, u32[]{:S(2)}, u32[]{:S(2)}) collective-permute-start(bf16[8,64,512]{2,1,0:T(8,128)(2,1)S(1)} %collective-permute-done.16.rest_1_), channel_id=1, source_target_pairs={{1,0},{5,4},{9,8},{13,12},{17,16},{21,20},{25,24},{29,28}} | collective-permute-start | bytes 1572872 | tf_op jit(solution)/shard_map/ppermute | solution.py:122
  73.4 25.4 %collective-permute-start.20 = (bf16[8,64,512]{2,1,0:T(8,128)(2,1)S(1)}, bf16[8,64,512]{2,1,0:T(8,128)(2,1)S(1)}, u32[]{:S(2)}, u32[]{:S(2)}) collective-permute-start(bf16[8,64,512]{2,1,0:T(8,128)(2,1)S(1)} %collective-permute-done.19.rest_4_), channel_id=1, source_target_pairs={{2,3},{6,7},{10,11},{14,15},{18,19},{22,23},{26,27},{30,31}} | collective-permute-start | bytes 1572872 | tf_op jit(solution)/shard_map/ppermute | solution.py:123
  84.7 2.2 copy-start.2
  98.7 11.5 %collective-permute-start.6 = (f32[8,4096]{1,0:T(8,128)S(1)}, f32[8,4096]{1,0:T(8,128)S(1)}, u32[]{:S(2)}, u32[]{:S(2)}) collective-permute-start(f32[8,4096]{1,0:T(8,128)S(1)} %forward.2), channel_id=1, source_target_pairs={{0,4},{4,0},{8,12},{12,8},{16,20},{20,16},{24,28},{28,24},{1,5},{5... | collective-permute-start | bytes 393224 | tf_op jit(solution)/shard_map/ppermute | solution.py:146
  98.8 21.4 %copy-start.3 = (bf16[4096]{0:T(1024)(128)(2,1)S(1)}, bf16[4096]{0:T(1024)(128)(2,1)}, u32[]{:S(2)}) copy-start(bf16[4096]{0:T(1024)(128)(2,1)} %param.9) | copy-start | bytes 24580
  98.8 21.4 %copy-start.4 = (bf16[4,8]{1,0:T(4,128)(2,1)S(1)}, bf16[4,8]{1,0:T(4,128)(2,1)}, u32[]{:S(2)}) copy-start(bf16[4,8]{1,0:T(4,128)(2,1)} %param.13) | copy-start | bytes 196
  109.7 18.7 %collective-permute-start.21 = (f32[8,4096]{1,0:T(8,128)S(1)}, f32[8,4096]{1,0:T(8,128)S(1)}, u32[]{:S(2)}, u32[]{:S(2)}) collective-permute-start(f32[8,4096]{1,0:T(8,128)S(1)} %forward.3), channel_id=1, source_target_pairs={{0,4},{4,0},{8,12},{12,8},{16,20},{20,16},{24,28},{28,24},{1,5},{5... | collective-permute-start | bytes 393224 | tf_op jit(solution)/shard_map/ppermute | solution.py:146
  110.2 19.5 %collective-permute-start.7 = (f32[8,4096]{1,0:T(8,128)S(1)}, f32[8,4096]{1,0:T(8,128)S(1)}, u32[]{:S(2)}, u32[]{:S(2)}) collective-permute-start(f32[8,4096]{1,0:T(8,128)S(1)} %add.70), channel_id=1, source_target_pairs={{0,8},{4,12},{8,0},{12,4},{16,24},{20,28},{24,16},{28,20},{1,9},{5... | collective-permute-start | bytes 393224 | tf_op jit(solution)/shard_map/ppermute | solution.py:146
  128.3 5.8 %collective-permute-start.22 = (f32[8,4096]{1,0:T(8,128)S(1)}, f32[8,4096]{1,0:T(8,128)S(1)}, u32[]{:S(2)}, u32[]{:S(2)}) collective-permute-start(f32[8,4096]{1,0:T(8,128)S(1)} %add.79), channel_id=1, source_target_pairs={{0,8},{4,12},{8,0},{12,4},{16,24},{20,28},{24,16},{28,20},{1,9},{5... | collective-permute-start | bytes 393224 | tf_op jit(solution)/shard_map/ppermute | solution.py:146
  129.8 5.8 %collective-permute-start.8 = (f32[8,4096]{1,0:T(8,128)S(1)}, f32[8,4096]{1,0:T(8,128)S(1)}, u32[]{:S(2)}, u32[]{:S(2)}) collective-permute-start(f32[8,4096]{1,0:T(8,128)S(1)} %add.71), channel_id=1, source_target_pairs={{0,16},{4,20},{8,24},{12,28},{16,0},{20,4},{24,8},{28,12},{1,17},{... | collective-permute-start | bytes 393224 | tf_op jit(solution)/shard_map/ppermute | solution.py:146
  134.2 14.5 %collective-permute-start.23 = (f32[8,4096]{1,0:T(8,128)S(1)}, f32[8,4096]{1,0:T(8,128)S(1)}, u32[]{:S(2)}, u32[]{:S(2)}) collective-permute-start(f32[8,4096]{1,0:T(8,128)S(1)} %add.80), channel_id=1, source_target_pairs={{0,16},{4,20},{8,24},{12,28},{16,0},{20,4},{24,8},{28,12},{1,17},{... | collective-permute-start | bytes 393224 | tf_op jit(solution)/shard_map/ppermute | solution.py:146
  135.6 2.2 copy-start.1
  148.0 11.7 %collective-permute-start.9 = (bf16[8,64,512]{2,1,0:T(8,128)(2,1)S(1)}, bf16[8,64,512]{2,1,0:T(8,128)(2,1)S(1)}, u32[]{:S(2)}, u32[]{:S(2)}) collective-permute-start(bf16[8,64,512]{2,1,0:T(8,128)(2,1)S(1)} %convert_element_type.79), channel_id=1, source_target_pairs={{0,1},{4,5},{8,9},{12,13},{16,17},{20,21},{24,25},{28,29}} | collective-permute-start | bytes 1572872 | tf_op jit(solution)/shard_map/ppermute | solution.py:135
  158.9 2.2 collective-permute-start.24
  159.8 16.8 %collective-permute-start.10 = (bf16[8,64,512]{2,1,0:T(8,128)(2,1)S(1)}, bf16[8,64,512]{2,1,0:T(8,128)(2,1)S(1)}, u32[]{:S(2)}, u32[]{:S(2)}) collective-permute-start(bf16[8,64,512]{2,1,0:T(8,128)(2,1)S(1)} %add_convert_fusion.9), channel_id=1, source_target_pairs={{0,1},{1,2},{4,5},{5,6},{8,9},{9,10},{12,13},{13,14},{16,17},{17,1... | collective-permute-start | bytes 1572872 | tf_op jit(solution)/shard_map/ppermute | solution.py:135
  161.3 24.7 %collective-permute-start.25 = (bf16[8,64,512]{2,1,0:T(8,128)(2,1)S(1)}, bf16[8,64,512]{2,1,0:T(8,128)(2,1)S(1)}, u32[]{:S(2)}, u32[]{:S(2)}) collective-permute-start(bf16[8,64,512]{2,1,0:T(8,128)(2,1)S(1)} %add_convert_fusion.4), channel_id=1, source_target_pairs={{0,1},{1,2},{4,5},{5,6},{8,9},{9,10},{12,13},{13,14},{16,17},{17,1... | collective-permute-start | bytes 1572872 | tf_op jit(solution)/shard_map/ppermute | solution.py:135
  176.8 12.5 %collective-permute-start.12 = (bf16[8,64,512]{2,1,0:T(8,128)(2,1)S(1)}, bf16[8,64,512]{2,1,0:T(8,128)(2,1)S(1)}, u32[]{:S(2)}, u32[]{:S(2)}) collective-permute-start(bf16[8,64,512]{2,1,0:T(8,128)(2,1)S(1)} %get-tuple-element.22), channel_id=1, source_target_pairs={{3,2},{7,6},{11,10},{15,14},{19,18},{23,22},{27,26},{31,30}} | collective-permute-start | bytes 1572872 | tf_op jit(solution)/shard_map/ppermute | solution.py:136
  186.2 16.8 %collective-permute-start.27 = (bf16[8,64,512]{2,1,0:T(8,128)(2,1)S(1)}, bf16[8,64,512]{2,1,0:T(8,128)(2,1)S(1)}, u32[]{:S(2)}, u32[]{:S(2)}) collective-permute-start(bf16[8,64,512]{2,1,0:T(8,128)(2,1)S(1)} %get-tuple-element.26), channel_id=1, source_target_pairs={{3,2},{7,6},{11,10},{15,14},{19,18},{23,22},{27,26},{31,30}} | collective-permute-start | bytes 1572872 | tf_op jit(solution)/shard_map/ppermute | solution.py:136
  189.4 24.8 %collective-permute-start.13 = (bf16[8,64,512]{2,1,0:T(8,128)(2,1)S(1)}, bf16[8,64,512]{2,1,0:T(8,128)(2,1)S(1)}, u32[]{:S(2)}, u32[]{:S(2)}) collective-permute-start(bf16[8,64,512]{2,1,0:T(8,128)(2,1)S(1)} %add_convert_fusion.7), channel_id=1, source_target_pairs={{2,1},{3,2},{6,5},{7,6},{10,9},{11,10},{14,13},{15,14},{18,17},{19... | collective-permute-start | bytes 1572872 | tf_op jit(solution)/shard_map/ppermute | solution.py:136
  203.1 22.3 %collective-permute-start.28 = (bf16[8,64,512]{2,1,0:T(8,128)(2,1)S(1)}, bf16[8,64,512]{2,1,0:T(8,128)(2,1)S(1)}, u32[]{:S(2)}, u32[]{:S(2)}) collective-permute-start(bf16[8,64,512]{2,1,0:T(8,128)(2,1)S(1)} %add_convert_fusion.2), channel_id=1, source_target_pairs={{2,1},{3,2},{6,5},{7,6},{10,9},{11,10},{14,13},{15,14},{18,17},{19... | collective-permute-start | bytes 1572872 | tf_op jit(solution)/shard_map/ppermute | solution.py:136
  205.1 23.2 %collective-permute-start.11 = (bf16[8,64,512]{2,1,0:T(8,128)(2,1)S(1)}, bf16[8,64,512]{2,1,0:T(8,128)(2,1)S(1)}, u32[]{:S(2)}, u32[]{:S(2)}) collective-permute-start(bf16[8,64,512]{2,1,0:T(8,128)(2,1)S(1)} %get-tuple-element.21), channel_id=1, source_target_pairs={{0,1},{1,2},{2,3},{4,5},{5,6},{6,7},{8,9},{9,10},{10,11},{12,13},{... | collective-permute-start | bytes 1572872 | tf_op jit(solution)/shard_map/ppermute | solution.py:135
  214.4 22.3 %collective-permute-start.14 = (bf16[8,64,512]{2,1,0:T(8,128)(2,1)S(1)}, bf16[8,64,512]{2,1,0:T(8,128)(2,1)S(1)}, u32[]{:S(2)}, u32[]{:S(2)}) collective-permute-start(bf16[8,64,512]{2,1,0:T(8,128)(2,1)S(1)} %add_convert_fusion.6), channel_id=1, source_target_pairs={{1,0},{2,1},{3,2},{5,4},{6,5},{7,6},{9,8},{10,9},{11,10},{13,12},{... | collective-permute-start | bytes 1572872 | tf_op jit(solution)/shard_map/ppermute | solution.py:136
  216.3 24.9 %collective-permute-start.26 = (bf16[8,64,512]{2,1,0:T(8,128)(2,1)S(1)}, bf16[8,64,512]{2,1,0:T(8,128)(2,1)S(1)}, u32[]{:S(2)}, u32[]{:S(2)}) collective-permute-start(bf16[8,64,512]{2,1,0:T(8,128)(2,1)S(1)} %get-tuple-element.25), channel_id=1, source_target_pairs={{0,1},{1,2},{2,3},{4,5},{5,6},{6,7},{8,9},{9,10},{10,11},{12,13},{... | collective-permute-start | bytes 1572872 | tf_op jit(solution)/shard_map/ppermute | solution.py:135
  226.4 18.8 %collective-permute-start.29 = (bf16[8,64,512]{2,1,0:T(8,128)(2,1)}, bf16[8,64,512]{2,1,0:T(8,128)(2,1)S(1)}, u32[]{:S(2)}, u32[]{:S(2)}) collective-permute-start(bf16[8,64,512]{2,1,0:T(8,128)(2,1)} %add_convert_fusion.1), channel_id=1, source_target_pairs={{1,0},{2,1},{3,2},{5,4},{6,5},{7,6},{9,8},{10,9},{11,10},{13,12},{... | collective-permute-start | bytes 1572872 | tf_op jit(solution)/shard_map/ppermute | solution.py:136
  237.7 13.2 %all-to-all-start.1 = ((bf16[8,64,512]{2,1,0:T(8,128)(2,1)}), bf16[8,64,512]{2,1,0:T(8,128)(2,1)S(1)}, u32[]{:S(2)}, u32[]{:S(2)}) async-start(bf16[8,64,512]{2,1,0:T(8,128)(2,1)} %add_convert_fusion.5), calls=%async_computation.1 | async-start | bytes 1048576 | tf_op jit(solution)/shard_map/all_to_all | solution.py:186
  250.9 13.2 %all-to-all-start.3 = ((bf16[8,64,512]{2,1,0:T(8,128)(2,1)}), bf16[8,64,512]{2,1,0:T(8,128)(2,1)S(1)}, u32[]{:S(2)}, u32[]{:S(2)}) async-start(bf16[8,64,512]{2,1,0:T(8,128)(2,1)} %add_convert_fusion), calls=%async_computation.3 | async-start | bytes 1048576 | tf_op jit(solution)/shard_map/all_to_all | solution.py:186

commit v2 on v0

v2 whole, which is shorter than its diff:
```python
import functools

import jax
import jax.numpy as jnp
from jax import lax
from jax.experimental import pallas as pl
from jax.experimental.pallas import tpu as pltpu
from jax.sharding import PartitionSpec as P

F32, BF16, I32 = jnp.float32, jnp.bfloat16, jnp.int32
SHARES = (4, 4)
VMEM_LIMIT = 28 * 1024 * 1024
TILE = 512
ANY = pl.BlockSpec(memory_space=pl.ANY)


def tile_of(total):
    return TILE if total % TILE == 0 else total


def forward_kernel(slots, grows, code, weights, *rest):
    before, sources, out = rest[:grows], rest[grows : grows + len(slots)], rest[-1]
    codes = code[...]
    total = before[0][...] if grows else jnp.zeros(out.shape, F32)
    for slot, source in zip(slots, sources):
        docs, part, width = source.shape
        rows = source[...].reshape(docs * part, width)
        scores = jnp.dot(rows, weights[...], preferred_element_type=F32)
        scores = scores.reshape(docs, part, scores.shape[1])
        ids = lax.broadcasted_iota(I32, scores.shape, 1) + slot * part
        hit = ids == codes[:, None, :]
        total += jnp.sum(jnp.where(hit, scores, 0.0), axis=1)
    out[...] = total


def backward_kernel(slots, waits, code, weights, logits, pooled, bias, *rest):
    outs = rest[waits:]
    step = pl.program_id(0)
    x = logits[...] + bias[...]
    soft = jnp.maximum(x, 0.0) + jnp.log1p(jnp.exp(-jnp.abs(x)))
    factor = pooled[...] * jax.nn.sigmoid(x) / (1.0 + soft)
    delta = factor.astype(BF16).astype(F32)
    codes = code[...]
    for slot, out in zip(slots, outs):
        docs, part, width = out.shape
        ids = lax.broadcasted_iota(I32, (docs, part, codes.shape[1]), 1) + slot * part
        hit = ids == codes[:, None, :]
        spread = jnp.where(hit, delta[:, None, :], 0.0).astype(BF16)
        spread = spread.reshape(docs * part, codes.shape[1])
        grown = jnp.dot(spread, weights[...], preferred_element_type=F32)
        grown = grown.reshape(docs, part, width)

        @pl.when(step == 0)
        def _():
            out[...] = grown

        @pl.when(step > 0)
        def _():
            out[...] += grown


def forward(code, weights_t, slots, sources, before, waits):
    docs, part, width = sources[0].shape
    entries = weights_t.shape[1]
    tile = tile_of(entries)
    logit = pl.BlockSpec((docs, tile), lambda t: (0, t))
    rows = pl.BlockSpec((docs, part, width), lambda t: (0, 0, 0))
    flops = 2 * docs * part * width * entries * len(slots)
    before = [] if before is None else [before]
    return pl.pallas_call(
        functools.partial(forward_kernel, slots, len(before)),
        out_shape=jax.ShapeDtypeStruct((docs, entries), F32),
        grid=(entries // tile,),
        in_specs=[logit, pl.BlockSpec((width, tile), lambda t: (0, t))]
        + [logit] * len(before)
        + [rows] * len(slots)
        + [ANY] * len(waits),
        out_specs=logit,
        compiler_params=pltpu.CompilerParams(vmem_limit_bytes=VMEM_LIMIT),
        cost_estimate=pl.CostEstimate(flops=flops, bytes_accessed=6 << 20, transcendentals=0),
        name="forward",
    )(code, weights_t, *before, *sources, *waits)


def backward(code, weights, logits, pooled, bias, slots, part, waits):
    docs, entries = code.shape
    width = weights.shape[1]
    tile = tile_of(entries)
    whole = pl.BlockSpec((docs, tile), lambda t: (0, t))
    flops = 2 * docs * part * width * entries * len(slots)
    return pl.pallas_call(
        functools.partial(backward_kernel, slots, len(waits)),
        out_shape=[jax.ShapeDtypeStruct((docs, part, width), F32)] * len(slots),
        grid=(entries // tile,),
        in_specs=[
            whole,
            pl.BlockSpec((tile, width), lambda t: (t, 0)),
            whole,
            whole,
            pl.BlockSpec((1, tile), lambda t: (0, t)),
        ]
        + [ANY] * len(waits),
        out_specs=[pl.BlockSpec((docs, part, width), lambda t: (0, 0, 0))] * len(slots),
        compiler_params=pltpu.CompilerParams(vmem_limit_bytes=VMEM_LIMIT),
        cost_estimate=pl.CostEstimate(flops=flops, bytes_accessed=6 << 20, transcendentals=0),
        name="backward",
    )(code, weights, logits, pooled, bias, *waits)


def together(*values):
    return lax.optimization_barrier(values)


def exchange(value, axis, bit):
    return lax.ppermute(value, axis, [(i, i ^ bit) for i in range(lax.axis_size(axis))])


def on_device(hidden, head_weight, head_bias, argmax, lengths, query_terms, score_grad):
    blocks, size = lax.axis_size("seq"), lax.axis_size("dp")
    z = lax.axis_index("seq")
    tok_rows = hidden.shape[1]
    entries, width = head_weight.shape
    parts = [tok_rows * share // 8 for share in SHARES]
    firsts = [sum(parts[:i]) for i in range(len(parts))]
    count = len(parts)
    near = tuple(range(2, blocks, 2)) + (1,)
    far = tuple(range(3, blocks, 2))
    bits = [1 << i for i in range(blocks.bit_length() - 1)]

    def swap(x):
        return lax.all_to_all(x, "dp", split_axis=0, concat_axis=0, tiled=True)

    sents = []
    for part, first in zip(parts, firsts):
        sent = hidden[:, first : first + part]
        sents.append(sent.reshape(-1, part, size, width).transpose(2, 0, 1, 3).reshape(-1, part, width))

    held = [dict() for _ in range(count)]
    partials, logits = [None] * count, [None] * count
    grads = [dict() for _ in range(count)]
    clock = []

    def tie(*values):
        out = together(*values, *clock)
        clock[:] = out[len(values) :]
        return out[: len(values)]

    def gather_near(c):
        for bit in reversed(bits):
            for slot in sorted(held[c]) if bit > 1 else (0,):
                held[c][slot ^ bit] = exchange(held[c][slot], "seq", bit)

    def gather_far(c):
        for slot in far:
            held[c][slot] = exchange(held[c][slot ^ 1], "seq", 1)

    def run_forward(c, slots, *others):
        sources = [held[c][slot] for slot in slots]
        waits = tuple(clock) + others
        partials[c] = forward(codes[c], weights_t, slots, sources, partials[c], waits)
        clock[:] = [partials[c]]

    def run_backward(c, slots, *others):
        waits = tuple(clock) + others
        found = backward(
            codes[c], head_weight, logits[c], pooled, bias, slots, parts[c], waits
        )
        grads[c].update(zip(slots, found))
        clock[:] = [found[0]]

    def reduce_far(c):
        for slot in reversed(far):
            grads[c][slot] = exchange(grads[c][slot].astype(BF16), "seq", 1)

    def reduce_near(c):
        grads[c][1] = exchange(grads[c][1].astype(BF16), "seq", 1)
        for slot in far:
            grads[c][slot ^ 1] = grads[c][slot ^ 1] + grads[c].pop(slot).astype(F32)
        for bit in bits[1:]:
            for slot in range(blocks - bit, 0, -2 * bit):
                moved = exchange(grads[c].pop(slot).astype(BF16), "seq", bit)
                if slot == bit:
                    grads[c][slot] = moved
                else:
                    grads[c][slot ^ bit] = grads[c][slot ^ bit] + moved.astype(F32)

    def run_sum(value, *between):
        step = 1
        while step < size:
            value = value + exchange(value, "dp", step)
            if between:
                between[0](value)
                between = between[1:]
            step *= 2
        return value

    held[0][0] = swap(sents[0])
    gather_near(0)

    head_weight, saved_all, queries, scores, held[0][0] = together(
        head_weight, argmax, query_terms, score_grad, held[0][0]
    )
    saved = lax.dynamic_slice_in_dim(saved_all, z * entries, entries, 1)
    block = saved // tok_rows
    inner = saved - block * tok_rows
    kept = (block < blocks) & (saved < lengths[:, None])
    codes = []
    for part, first in zip(parts, firsts):
        here = kept & (inner >= first) & (inner < first + part)
        codes.append(jnp.where(here, (block ^ z) * part + inner - first, -1))
    bias = head_bias.astype(F32)[None, :]
    queries = lax.dynamic_slice_in_dim(queries, z * entries, entries, 1)
    pooled = jnp.einsum("jd,jv->dv", scores, queries, preferred_element_type=F32)
    pooled = run_sum(pooled)
    weights_t = head_weight.T
    run_forward(0, (0,))
    for c in range(1, count):
        sents[c], pooled = together(sents[c], pooled)
        held[c][0] = swap(sents[c])
    arrived = [held[0][slot] for slot in near]
    arrived = tie(*arrived, *[held[c][0] for c in range(1, count)])
    held[0].update(zip(near, arrived))
    for c in range(1, count):
        held[c][0] = arrived[len(near) + c - 1]
    gather_far(0)

    for c in range(1, count + 1):
        more = c < count
        if more:
            gather_near(c)
        run_forward(c - 1, near)
        run_forward(c - 1, far, *([grads[c - 2][slot] for slot in far] if c > 1 else ()))
        if c > 1:
            reduce_near(c - 2)
        between = []
        if more:
            between.append(lambda value: run_forward(c, (0,), value))
        elif count > 1:
            between.append(lambda value: run_backward(c - 2, (0,), value))
        logits[c - 1] = run_sum(partials[c - 1], *between)
        if more:
            arrived = tie(*[held[c][slot] for slot in near])
            held[c].update(zip(near, arrived))
            gather_far(c)
        run_backward(c - 1, far)
        reduce_far(c - 1)
        moving = [grads[c - 2][bit] for bit in bits] if c > 1 else ()
        run_backward(c - 1, near, *moving)
    reduce_near(count - 1)
    run_backward(count - 1, (0,))

    results = []
    for c in range(count):
        total = grads[c].pop(0)
        for moved in grads[c].values():
            total = total + moved.astype(F32)
        back = swap(total.astype(BF16))
        back = back.reshape(size, -1, parts[c], width).transpose(1, 2, 0, 3)
        results.append(back.reshape(-1, parts[c], size * width))
    return jnp.concatenate(results, axis=1)


def solution(mesh):
    return jax.shard_map(
        on_device,
        mesh=mesh,
        in_specs=(
            P("dp", "seq", None),
            P("seq", "dp"),
            P("seq"),
            P(),
            P(),
            P("dp", None),
            P("dp", None),
        ),
        out_specs=P("dp", "seq", None),
        check_vma=False,
    )
```

time: 2200 us -> 203 us (0.09)
  local copies, waits for them, and re-layouts: 2080 us -> 16.1 us
  waiting for transfers between devices: 1.47 us -> 77.3 us
  Pallas kernels: 0 us -> 63.1 us
  blocking collectives: 42.3 us -> 0 us
  other arithmetic: 40.8 us -> 6.79 us
  starting transfers between devices: 5.25 us -> 38.7 us
    gather x23 -> x0, local copies, waits for them, and re-layouts: 2060 us -> none  [the longest x15 1500 us: on_device(): jnp.searchsorted(row, targets, side='left')]
    pallas_call x0 -> x12, Pallas kernels: none -> 63.1 us  [the longest x6 34.8 us: backward(): pl.pallas_call(functools.partial(backward_kernel, slots, len(waits)), out...]
    ppermute x0 -> x21, waiting for transfers between devices: none -> 57.9 us  [exchange(): lax.ppermute(value, axis, [(i, i ^ bit) for i in range(lax.axis_size(axis...]
    all_gather x2 -> x0, blocking collectives: 24.3 us -> none  [the longest x1 14 us: on_device(): lax.all_gather(head_bias, 'seq', axis=0, tiled=True)]
    unnamed x6 -> x0, other arithmetic: 24.1 us -> none
    ppermute x0 -> x21, starting transfers between devices: none -> 22.9 us  [exchange(): lax.ppermute(value, axis, [(i, i ^ bit) for i in range(lax.axis_size(axis...]
  transfers between devices with their start and end apart: 4 -> 25, of which waited for: 0 -> 16; matrix products, arithmetic and copies ran while one was open for 93% -> 6% of each run, Pallas kernels for 0% -> 29%
where the time goes in v2:
time: 203 us
  waiting for transfers between devices  77.3 us (38%)
  Pallas kernels  63.1 us (31%)
  starting transfers between devices  38.7 us (19%)
  local copies, waits for them, and re-layouts  16.1 us (8%)
  other arithmetic  6.79 us (3%)
    ppermute x21, waiting for transfers between devices, exchange(): lax.ppermute(value, axis, [(i, i ^ bit) for i in range(lax.axis_size(axis...  57.9 us
    pallas_call x6, Pallas kernels, backward(): pl.pallas_call(functools.partial(backward_kernel, slots, len(waits)), out...  34.8 us
    pallas_call x6, Pallas kernels, forward(): pl.pallas_call(functools.partial(forward_kernel, slots, len(before)), out...  28.2 us
    ppermute x21, starting transfers between devices, exchange(): lax.ppermute(value, axis, [(i, i ^ bit) for i in range(lax.axis_size(axis...  22.9 us
    all_to_all x4, waiting for transfers between devices, swap(): return lax.all_to_all(x, 'dp', split_axis=0, concat_axis=0, tiled=True)  19.4 us
    all_to_all x4, starting transfers between devices, swap(): return lax.all_to_all(x, 'dp', split_axis=0, concat_axis=0, tiled=True)  15.8 us
    unnamed x16, local copies, waits for them, and re-layouts  6.58 us
    optimization_barrier x1, local copies, waits for them, and re-layouts, together(): return lax.optimization_barrier(values)  6.42 us
  transfers between devices with their start and end apart: 25, of which 16 were waited for; matrix products, arithmetic and copies ran while one was open for 6% of the time, Pallas kernels for 29%

profile of v2, /device:TPU:0, one launch (start us, length us, event | category | flops | bytes accessed | tf_op | source)
XLA Modules:
  0.0 202.5 jit_solution(196885689809059301)
XLA Ops:
  0.0 1.3 fusion.5
  1.3 0.8 copy.21
  2.2 5.3 %all-to-all-start = ((bf16[8,64,512]{2,1,0:T(8,128)(2,1)}), bf16[8,64,512]{2,1,0:T(8,128)(2,1)S(1)}, u32[]{:S(2)}, u32[]{:S(2)}) async-start(bf16[8,64,512]{2,1,0:T(8,128)(2,1)} %bitcast.30), calls=%async_computation | async-start | bytes 1048576 | tf_op jit(solution)/shard_map/all_to_all | solution.py:131
  7.5 9.7 %all-to-all-done.rest_0_ = bf16[8,64,512]{2,1,0:T(8,128)(2,1)S(1)} async-done(((bf16[8,64,512]{2,1,0:T(8,128)(2,1)}), bf16[8,64,512]{2,1,0:T(8,128)(2,1)S(1)}, u32[]{:S(2)}, u32[]{:S(2)}) %all-to-all-start) | async-done | bytes 524320 | tf_op jit(solution)/shard_map/all_to_all | solution.py:131
  17.2 0.2 fusion.2
  17.5 1.3 collective-permute-done.2
  18.8 0.6 collective-permute-start.3
  19.5 5.0 %collective-permute-done.3 = f32[8,4096]{1,0:T(8,128)S(1)} collective-permute-done((f32[8,4096]{1,0:T(8,128)S(1)}, f32[8,4096]{1,0:T(8,128)S(1)}, u32[]{:S(2)}, u32[]{:S(2)}) %collective-permute-start.3) | collective-permute-done | bytes 131104 | tf_op jit(solution)/shard_map/ppermute | solution.py:115
  24.5 0.6 collective-permute-start.4
  25.1 0.8 copy.20
  25.9 2.6 %collective-permute-start = (bf16[8,64,512]{2,1,0:T(8,128)(2,1)S(1)}, bf16[8,64,512]{2,1,0:T(8,128)(2,1)S(1)}, u32[]{:S(2)}, u32[]{:S(2)}) collective-permute-start(bf16[8,64,512]{2,1,0:T(8,128)(2,1)S(1)} %all-to-all-done.rest_0_), channel_id=1, source_target_pairs={{0,2},{1,3},{2,0},{3,1},{4,6},{5,7},{6,4},{7,5},{8,10},{9,11},{10,... | collective-permute-start | bytes 1572872 | tf_op jit(solution)/shard_map/ppermute | solution.py:115
  28.5 1.6 collective-permute-start.1
  30.1 3.5 %all-to-all-start.1 = ((bf16[8,64,512]{2,1,0:T(8,128)(2,1)}), bf16[8,64,512]{2,1,0:T(8,128)(2,1)S(1)}, u32[]{:S(2)}, u32[]{:S(2)}) async-start(bf16[8,64,512]{2,1,0:T(8,128)(2,1)} %bitcast.28), calls=%async_computation.1 | async-start | bytes 1048576 | tf_op jit(solution)/shard_map/all_to_all | solution.py:131
  33.7 1.1 and_select_fusion
  34.8 6.4 %copy.10 = bf16[4096,512]{0,1:T(8,128)(2,1)} copy(bf16[4096,512]{1,0:T(8,128)(2,1)} %weights.5) | data formatting | bytes 8388608 | tf_op jit(solution)/shard_map/optimization_barrier | solution.py:111
  41.2 2.2 %copy-done.3 = bf16[4096,512]{0,1:T(8,128)(2,1)S(1)} copy-done((bf16[4096,512]{0,1:T(8,128)(2,1)S(1)}, bf16[4096,512]{0,1:T(8,128)(2,1)}, u32[]{:S(2)}) %copy-start.3) | copy-done | bytes 4194328
  43.4 4.0 %forward.6.rest_0_.rest_3_ = f32[8,4096]{1,0:T(8,128)S(1)} custom-call(s32[8,4096]{1,0:T(8,128)S(1)} %get-tuple-element.43.code, bf16[512,4096]{1,0:T(8,128)(2,1)S(1)} %bitcast.31, bf16[8,64,512]{2,1,0:T(8,128)(2,1)S(1)} %all-to-all-done.rest_0_), custom_call_target="tpu_custom_call" | custom-call | flops 2147483648 | bytes 6291456 | tf_op jit(solution)/shard_map/forward/pallas_call | solution.py:70
  47.4 3.7 %collective-permute-done.rest_1_ = bf16[8,64,512]{2,1,0:T(8,128)(2,1)S(1)} collective-permute-done((bf16[8,64,512]{2,1,0:T(8,128)(2,1)S(1)}, bf16[8,64,512]{2,1,0:T(8,128)(2,1)S(1)}, u32[]{:S(2)}, u32[]{:S(2)}) %collective-permute-start) | collective-permute-done | bytes 524320 | tf_op jit(solution)/shard_map/ppermute | solution.py:115
  51.1 0.2 collective-permute-done.1.rest_2_
  51.3 1.4 collective-permute-start.5
  52.7 2.3 %collective-permute-start.9 = (bf16[8,64,512]{2,1,0:T(8,128)(2,1)S(1)}, bf16[8,64,512]{2,1,0:T(8,128)(2,1)S(1)}, u32[]{:S(2)}, u32[]{:S(2)}) collective-permute-start(bf16[8,64,512]{2,1,0:T(8,128)(2,1)S(1)} %all-to-all-done.1.rest_0_), channel_id=1, source_target_pairs={{0,2},{1,3},{2,0},{3,1},{4,6},{5,7},{6,4},{7,5},{8,10},{9,11},{10,... | collective-permute-start | bytes 1572872 | tf_op jit(solution)/shard_map/ppermute | solution.py:115
  55.0 0.1 collective-permute-start.10
  55.1 2.2 %copy-done.4 = bf16[4096,512]{0,1:T(8,128)(2,1)S(1)} copy-done((bf16[4096,512]{0,1:T(8,128)(2,1)S(1)}, bf16[4096,512]{0,1:T(8,128)(2,1)}, u32[]{:S(2)}) %copy-start.4) | copy-done | bytes 4194328
  57.3 6.2 %forward.7.rest_0_.rest_2_ = f32[8,4096]{1,0:T(8,128)S(1)} custom-call(s32[8,4096]{1,0:T(8,128)S(1)} %get-tuple-element.43.code, bf16[512,4096]{1,0:T(8,128)(2,1)S(1)} %bitcast.32, f32[8,4096]{1,0:T(8,128)S(1)} %forward.6.rest_0_.rest_3_, bf16[8,64,512]{2,1,0:T(8,128)(2,1)S(1)} %collective-permute-done.rest_1_, ...), custom_call_target="tpu_custom_call" | custom-call | flops 4294967296 | bytes 6291456 | tf_op jit(solution)/shard_map/forward/pallas_call | solution.py:70
  63.5 13.7 %collective-permute-done.5.rest_1_ = bf16[8,64,512]{2,1,0:T(8,128)(2,1)S(1)} collective-permute-done((bf16[8,64,512]{2,1,0:T(8,128)(2,1)S(1)}, bf16[8,64,512]{2,1,0:T(8,128)(2,1)S(1)}, u32[]{:S(2)}, u32[]{:S(2)}) %collective-permute-start.5) | collective-permute-done | bytes 524320 | tf_op jit(solution)/shard_map/ppermute | solution.py:115
  77.1 4.0 %forward.8.rest_1_ = f32[8,4096]{1,0:T(8,128)S(1)} custom-call(s32[8,4096]{1,0:T(8,128)S(1)} %get-tuple-element.43.code, bf16[512,4096]{1,0:T(8,128)(2,1)S(1)} %bitcast.33, f32[8,4096]{1,0:T(8,128)S(1)} %forward.7.rest_0_.rest_2_, bf16[8,64,512]{2,1,0:T(8,128)(2,1)S(1)} %collective-permute-done.5.rest_1_, f32[8,4096]{1,0:T(8,128)S(1)} %forward.7.rest_0_.rest_2_), custom_call_target="tpu_custom_call" | custom-call | flops 2147483648 | bytes 6291456 | tf_op jit(solution)/shard_map/forward/pallas_call | solution.py:70
  81.2 1.3 collective-permute-done.6
  82.5 0.6 collective-permute-start.7
  83.2 5.0 %collective-permute-done.7 = f32[8,4096]{1,0:T(8,128)S(1)} collective-permute-done((f32[8,4096]{1,0:T(8,128)S(1)}, f32[8,4096]{1,0:T(8,128)S(1)}, u32[]{:S(2)}, u32[]{:S(2)}) %collective-permute-start.7) | collective-permute-done | bytes 131104 | tf_op jit(solution)/shard_map/ppermute | solution.py:115
  88.2 1.5 collective-permute-start.8
  89.7 4.0 %forward.9.rest_0_ = f32[8,4096]{1,0:T(8,128)S(1)} custom-call(s32[8,4096]{1,0:T(8,128)S(1)} %get-tuple-element.44.code, bf16[512,4096]{1,0:T(8,128)(2,1)S(1)} %bitcast.34, bf16[8,64,512]{2,1,0:T(8,128)(2,1)S(1)} %all-to-all-done.1.rest_0_, f32[8,4096]{1,0:T(8,128)S(1)} %forward.8.rest_1_, f32[8,4096]{1,0:T(8,128)S(1)} %add.60.rest_2_), custom_call_target="tpu_custom_call" | custom-call | flops 2147483648 | bytes 6291456 | tf_op jit(solution)/shard_map/forward/pallas_call | solution.py:70
  93.7 0.1 collective-permute-start.11
  93.8 4.4 %backward.6.rest_0_ = f32[8,64,512]{2,1,0:T(8,128)S(1)} custom-call(s32[8,4096]{1,0:T(8,128)S(1)} %get-tuple-element.43.code, bf16[4096,512]{1,0:T(8,128)(2,1)S(1)} %copy-done.1, f32[8,4096]{1,0:T(8,128)S(1)} %add.62.logits, f32[8,4096]{1,0:T(8,128)S(1)} %add.59.pooled, f32[1,4096]{1,0:T(1,128)S(1)} %bitcast.37, f32[8,4096]{1,0:T(8,128)S(1)} %forward.9.rest_0_), custom_call_target="tpu_custom_call" | custom-call | flops 2147483648 | bytes 6291456 | tf_op jit(solution)/shard_map/backward/pallas_call | solution.py:91
  98.3 2.1 %collective-permute-start.12 = (bf16[8,64,512]{2,1,0:T(8,128)(2,1)S(1)}, bf16[8,64,512]{2,1,0:T(8,128)(2,1)S(1)}, u32[]{:S(2)}, u32[]{:S(2)}) collective-permute-start(bf16[8,64,512]{2,1,0:T(8,128)(2,1)S(1)} %convert_element_type.43), channel_id=1, source_target_pairs={{0,1},{1,0},{2,3},{3,2},{4,5},{5,4},{6,7},{7,6},{8,9},{9,8},{10,11... | collective-permute-start | bytes 1572872 | tf_op jit(solution)/shard_map/ppermute | solution.py:115
  100.4 8.6 %backward.7 = (f32[8,64,512]{2,1,0:T(8,128)S(1)}, f32[8,64,512]{2,1,0:T(8,128)S(1)}) custom-call(s32[8,4096]{1,0:T(8,128)S(1)} %get-tuple-element.43.code, bf16[4096,512]{1,0:T(8,128)(2,1)S(1)} %copy-done.1, f32[8,4096]{1,0:T(8,128)S(1)} %add.62.logits, f32[8,4096]{1,0:T(8,128)S(1)} %add.59.pooled, f32[1,4096]{1,0:T(1,128)S(1)} %bitcast.38, ...), custom_call_target="tpu_custom_call" | custom-call | flops 4294967296 | bytes 6291456 | tf_op jit(solution)/shard_map/backward/pallas_call | solution.py:91
  109.0 6.2 %forward.10.rest_0_.rest_2_ = f32[8,4096]{1,0:T(8,128)S(1)} custom-call(s32[8,4096]{1,0:T(8,128)S(1)} %get-tuple-element.44.code, bf16[512,4096]{1,0:T(8,128)(2,1)S(1)} %bitcast.35, f32[8,4096]{1,0:T(8,128)S(1)} %forward.9.rest_0_, bf16[8,64,512]{2,1,0:T(8,128)(2,1)S(1)} %collective-permute-done.9.rest_1_, ...), custom_call_target="tpu_custom_call" | custom-call | flops 4294967296 | bytes 6291456 | tf_op jit(solution)/shard_map/forward/pallas_call | solution.py:70
  115.2 2.7 %collective-permute-done.12.rest_3_ = bf16[8,64,512]{2,1,0:T(8,128)(2,1)S(1)} collective-permute-done((bf16[8,64,512]{2,1,0:T(8,128)(2,1)S(1)}, bf16[8,64,512]{2,1,0:T(8,128)(2,1)S(1)}, u32[]{:S(2)}, u32[]{:S(2)}) %collective-permute-start.12) | collective-permute-done | bytes 524320 | tf_op jit(solution)/shard_map/ppermute | solution.py:115
  117.9 4.0 %forward.11.rest_0_ = f32[8,4096]{1,0:T(8,128)S(1)} custom-call(s32[8,4096]{1,0:T(8,128)S(1)} %get-tuple-element.44.code, bf16[512,4096]{1,0:T(8,128)(2,1)S(1)} %bitcast.36, f32[8,4096]{1,0:T(8,128)S(1)} %forward.10.rest_0_.rest_2_, bf16[8,64,512]{2,1,0:T(8,128)(2,1)S(1)} %collective-permute-done.11.rest_1_, f32[8,4096]{1,0:T(8,128)S(1)} %forward.10.rest_0_.rest_2_, ...), custom_call_target="tpu_custom_call" | custom-call | flops 2147483648 | bytes 6291456 | tf_op jit(solution)/shard_map/forward/pallas_call | solution.py:70
  122.0 0.3 collective-permute-start.14
  122.4 0.9 collective-permute-done.13
  123.3 0.6 collective-permute-start.16
  123.9 0.2 add_convert_fusion.3
  124.1 2.8 %collective-permute-start.15 = (bf16[8,64,512]{2,1,0:T(8,128)(2,1)S(1)}, bf16[8,64,512]{2,1,0:T(8,128)(2,1)S(1)}, u32[]{:S(2)}, u32[]{:S(2)}) collective-permute-start(bf16[8,64,512]{2,1,0:T(8,128)(2,1)S(1)} %add_convert_fusion.3), channel_id=1, source_target_pairs={{0,2},{1,3},{2,0},{3,1},{4,6},{5,7},{6,4},{7,5},{8,10},{9,11},{10,... | collective-permute-start | bytes 1572872 | tf_op jit(solution)/shard_map/ppermute | solution.py:115
  126.9 2.0 %collective-permute-done.16 = f32[8,4096]{1,0:T(8,128)S(1)} collective-permute-done((f32[8,4096]{1,0:T(8,128)S(1)}, f32[8,4096]{1,0:T(8,128)S(1)}, u32[]{:S(2)}, u32[]{:S(2)}) %collective-permute-start.16) | collective-permute-done | bytes 131104 | tf_op jit(solution)/shard_map/ppermute | solution.py:115
  128.9 0.6 collective-permute-start.17
  129.6 4.4 %backward.8.rest_0_ = f32[8,64,512]{2,1,0:T(8,128)S(1)} custom-call(s32[8,4096]{1,0:T(8,128)S(1)} %get-tuple-element.43.code, bf16[4096,512]{1,0:T(8,128)(2,1)S(1)} %copy-done.1, f32[8,4096]{1,0:T(8,128)S(1)} %add.62.logits, f32[8,4096]{1,0:T(8,128)S(1)} %add.59.pooled, f32[1,4096]{1,0:T(1,128)S(1)} %bitcast.39, f32[8,4096]{1,0:T(8,128)S(1)} %forward.11.rest_0_, ...), custom_call_target="tpu_custom_call" | custom-call | flops 2147483648 | bytes 6291456 | tf_op jit(solution)/shard_map/backward/pallas_call | solution.py:91
  134.0 4.4 %backward.9.rest_0_ = f32[8,64,512]{2,1,0:T(8,128)S(1)} custom-call(s32[8,4096]{1,0:T(8,128)S(1)} %get-tuple-element.44.code, bf16[4096,512]{1,0:T(8,128)(2,1)S(1)} %copy-done.1, f32[8,4096]{1,0:T(8,128)S(1)} %add.68.logits, f32[8,4096]{1,0:T(8,128)S(1)} %add.59.pooled, f32[1,4096]{1,0:T(1,128)S(1)} %bitcast.40, f32[8,64,512]{2,1,0:T(8,128)S(1)} %backward.8.rest_0_), custom_call_target="tpu_custom_call" | custom-call | flops 2147483648 | bytes 6291456 | tf_op jit(solution)/shard_map/backward/pallas_call | solution.py:91
  138.5 1.0 collective-permute-start.19
  139.5 7.7 %collective-permute-done.14.rest_1_ = bf16[8,64,512]{2,1,0:T(8,128)(2,1)S(1)} collective-permute-done((bf16[8,64,512]{2,1,0:T(8,128)(2,1)S(1)}, bf16[8,64,512]{2,1,0:T(8,128)(2,1)S(1)}, u32[]{:S(2)}, u32[]{:S(2)}) %collective-permute-start.14) | collective-permute-done | bytes 524320 | tf_op jit(solution)/shard_map/ppermute | solution.py:115
  147.2 3.1 %collective-permute-done.15.rest_2_ = bf16[8,64,512]{2,1,0:T(8,128)(2,1)S(1)} collective-permute-done((bf16[8,64,512]{2,1,0:T(8,128)(2,1)S(1)}, bf16[8,64,512]{2,1,0:T(8,128)(2,1)S(1)}, u32[]{:S(2)}, u32[]{:S(2)}) %collective-permute-start.15) | collective-permute-done | bytes 524320 | tf_op jit(solution)/shard_map/ppermute | solution.py:115
  150.3 8.6 %backward.10 = (f32[8,64,512]{2,1,0:T(8,128)S(1)}, f32[8,64,512]{2,1,0:T(8,128)S(1)}) custom-call(s32[8,4096]{1,0:T(8,128)S(1)} %get-tuple-element.44.code, bf16[4096,512]{1,0:T(8,128)(2,1)S(1)} %copy-done.1, f32[8,4096]{1,0:T(8,128)S(1)} %add.68.logits, f32[8,4096]{1,0:T(8,128)S(1)} %add.59.pooled, f32[1,4096]{1,0:T(1,128)S(1)} %bitcast.41, ...), custom_call_target="tpu_custom_call" | custom-call | flops 4294967296 | bytes 6291456 | tf_op jit(solution)/shard_map/backward/pallas_call | solution.py:91
  159.0 0.4 collective-permute-start.18
  159.4 1.0 add_convert_fusion.1
  160.3 3.4 %collective-permute-start.20 = (bf16[8,64,512]{2,1,0:T(8,128)(2,1)}, bf16[8,64,512]{2,1,0:T(8,128)(2,1)}, u32[]{:S(2)}, u32[]{:S(2)}) collective-permute-start(bf16[8,64,512]{2,1,0:T(8,128)(2,1)} %add_convert_fusion.1), channel_id=1, source_target_pairs={{0,2},{1,3},{2,0},{3,1},{4,6},{5,7},{6,4},{7,5},{8,10},{9,11},{10,... | collective-permute-start | bytes 1572872 | tf_op jit(solution)/shard_map/ppermute | solution.py:115
  163.8 1.0 add_convert_fusion.2
  164.8 3.5 %all-to-all-start.2 = ((bf16[8,64,512]{2,1,0:T(8,128)(2,1)}), bf16[8,64,512]{2,1,0:T(8,128)(2,1)S(1)}, u32[]{:S(2)}, u32[]{:S(2)}) async-start(bf16[8,64,512]{2,1,0:T(8,128)(2,1)} %add_convert_fusion.2), calls=%async_computation.2 | async-start | bytes 1048576 | tf_op jit(solution)/shard_map/all_to_all | solution.py:131
  168.3 2.2 %copy-done.2 = bf16[4096,512]{1,0:T(8,128)(2,1)S(1)} copy-done((bf16[4096,512]{1,0:T(8,128)(2,1)S(1)}, bf16[4096,512]{1,0:T(8,128)(2,1)}, u32[]{:S(2)}) %copy-start.2) | copy-done | bytes 4194328
  170.5 4.4 %backward.11 = f32[8,64,512]{2,1,0:T(8,128)S(1)} custom-call(s32[8,4096]{1,0:T(8,128)S(1)} %get-tuple-element.44.code, bf16[4096,512]{1,0:T(8,128)(2,1)S(1)} %copy-done.2, f32[8,4096]{1,0:T(8,128)S(1)} %add.68.logits, f32[8,4096]{1,0:T(8,128)S(1)} %add.59.pooled, f32[1,4096]{1,0:T(1,128)S(1)} %bitcast.42, f32[8,64,512]{2,1,0:T(8,128)S(1)} %get-tuple-element.39.rest_0_), custom_call_target="tpu_custom_call" | custom-call | flops 2147483648 | bytes 6291456 | tf_op jit(solution)/shard_map/backward/pallas_call | solution.py:91
  174.9 5.4 %collective-permute-done.18 = bf16[8,64,512]{2,1,0:T(8,128)(2,1)S(1)} collective-permute-done((bf16[8,64,512]{2,1,0:T(8,128)(2,1)S(1)}, bf16[8,64,512]{2,1,0:T(8,128)(2,1)S(1)}, u32[]{:S(2)}, u32[]{:S(2)}) %collective-permute-start.18) | collective-permute-done | bytes 524320 | tf_op jit(solution)/shard_map/ppermute | solution.py:115
  180.3 5.8 %collective-permute-done.20 = bf16[8,64,512]{2,1,0:T(8,128)(2,1)} collective-permute-done((bf16[8,64,512]{2,1,0:T(8,128)(2,1)}, bf16[8,64,512]{2,1,0:T(8,128)(2,1)}, u32[]{:S(2)}, u32[]{:S(2)}) %collective-permute-start.20) | collective-permute-done | bytes 524320 | tf_op jit(solution)/shard_map/ppermute | solution.py:115
  186.2 2.1 %add_convert_fusion = bf16[8,64,512]{2,1,0:T(8,128)(2,1)} fusion(bf16[8,64,512]{2,1,0:T(8,128)(2,1)} %collective-permute-done.20, f32[8,64,512]{2,1,0:T(8,128)S(1)} %backward.11, bf16[8,64,512]{2,1,0:T(8,128)(2,1)S(1)} %collective-permute-done.18), kind=kLoop, calls=%fused_computation.1 | loop fusion | flops 1310720 | bytes 2621440 | tf_op jit(solution)/shard_map/convert_element_type | solution.py:257
  188.2 3.5 %all-to-all-start.3 = ((bf16[8,64,512]{2,1,0:T(8,128)(2,1)}), bf16[8,64,512]{2,1,0:T(8,128)(2,1)S(1)}, u32[]{:S(2)}, u32[]{:S(2)}) async-start(bf16[8,64,512]{2,1,0:T(8,128)(2,1)} %add_convert_fusion), calls=%async_computation.3 | async-start | bytes 1048576 | tf_op jit(solution)/shard_map/all_to_all | solution.py:131
  191.8 9.6 %all-to-all-done.3 = bf16[8,64,512]{2,1,0:T(8,128)(2,1)S(1)} async-done(((bf16[8,64,512]{2,1,0:T(8,128)(2,1)}), bf16[8,64,512]{2,1,0:T(8,128)(2,1)S(1)}, u32[]{:S(2)}, u32[]{:S(2)}) %all-to-all-start.3) | async-done | bytes 524320 | tf_op jit(solution)/shard_map/all_to_all | solution.py:131
  201.4 1.1 pad_maximum_fusion
  (41 shorter events, 0.8 us)
Async XLA Ops:
  0.0 17.2 %copy-start = (bf16[4,16384]{1,0:T(4,128)(2,1)S(1)}, bf16[4,16384]{1,0:T(4,128)(2,1)}, u32[]{:S(2)}) copy-start(bf16[4,16384]{1,0:T(4,128)(2,1)} %param.12) | copy-start | bytes 393220
  0.0 17.2 %copy-start.6 = (bf16[4,8]{1,0:T(4,128)(2,1)S(1)}, bf16[4,8]{1,0:T(4,128)(2,1)}, u32[]{:S(2)}) copy-start(bf16[4,8]{1,0:T(4,128)(2,1)} %param.13) | copy-start | bytes 196
  2.2 31.5 %copy-start.7 = (s32[8]{0:T(128)S(1)}, s32[8]{0:T(128)}, u32[]{:S(2)}) copy-start(s32[8]{0:T(128)} %param.11) | copy-start | bytes 100
  2.2 15.0 %all-to-all-start = ((bf16[8,64,512]{2,1,0:T(8,128)(2,1)}), bf16[8,64,512]{2,1,0:T(8,128)(2,1)S(1)}, u32[]{:S(2)}, u32[]{:S(2)}) async-start(bf16[8,64,512]{2,1,0:T(8,128)(2,1)} %bitcast.30), calls=%async_computation | async-start | bytes 1048576 | tf_op jit(solution)/shard_map/all_to_all | solution.py:131
  17.4 1.4 collective-permute-start.2
  18.8 5.6 %collective-permute-start.3 = (f32[8,4096]{1,0:T(8,128)S(1)}, f32[8,4096]{1,0:T(8,128)S(1)}, u32[]{:S(2)}, u32[]{:S(2)}) collective-permute-start(f32[8,4096]{1,0:T(8,128)S(1)} %add.57), channel_id=1, source_target_pairs={{0,8},{4,12},{8,0},{12,4},{16,24},{20,28},{24,16},{28,20},{1,9},{5... | collective-permute-start | bytes 393224 | tf_op jit(solution)/shard_map/ppermute | solution.py:115
  24.5 5.6 %collective-permute-start.4 = (f32[8,4096]{1,0:T(8,128)S(1)}, f32[8,4096]{1,0:T(8,128)S(1)}, u32[]{:S(2)}, u32[]{:S(2)}) collective-permute-start(f32[8,4096]{1,0:T(8,128)S(1)} %add.58), channel_id=1, source_target_pairs={{0,16},{4,20},{8,24},{12,28},{16,0},{20,4},{24,8},{28,12},{1,17},{... | collective-permute-start | bytes 393224 | tf_op jit(solution)/shard_map/ppermute | solution.py:115
  25.9 25.1 %collective-permute-start = (bf16[8,64,512]{2,1,0:T(8,128)(2,1)S(1)}, bf16[8,64,512]{2,1,0:T(8,128)(2,1)S(1)}, u32[]{:S(2)}, u32[]{:S(2)}) collective-permute-start(bf16[8,64,512]{2,1,0:T(8,128)(2,1)S(1)} %all-to-all-done.rest_0_), channel_id=1, source_target_pairs={{0,2},{1,3},{2,0},{3,1},{4,6},{5,7},{6,4},{7,5},{8,10},{9,11},{10,... | collective-permute-start | bytes 1572872 | tf_op jit(solution)/shard_map/ppermute | solution.py:115
  28.5 22.7 %collective-permute-start.1 = (bf16[8,64,512]{2,1,0:T(8,128)(2,1)S(1)}, bf16[8,64,512]{2,1,0:T(8,128)(2,1)S(1)}, u32[]{:S(2)}, u32[]{:S(2)}) collective-permute-start(bf16[8,64,512]{2,1,0:T(8,128)(2,1)S(1)} %all-to-all-done.rest_0_), channel_id=1, source_target_pairs={{0,1},{1,0},{2,3},{3,2},{4,5},{5,4},{6,7},{7,6},{8,9},{9,8},{10,11... | collective-permute-start | bytes 1572872 | tf_op jit(solution)/shard_map/ppermute | solution.py:115
  30.1 21.1 %all-to-all-start.1 = ((bf16[8,64,512]{2,1,0:T(8,128)(2,1)}), bf16[8,64,512]{2,1,0:T(8,128)(2,1)S(1)}, u32[]{:S(2)}, u32[]{:S(2)}) async-start(bf16[8,64,512]{2,1,0:T(8,128)(2,1)} %bitcast.28), calls=%async_computation.1 | async-start | bytes 1048576 | tf_op jit(solution)/shard_map/all_to_all | solution.py:131
  41.2 2.2 %copy-start.3 = (bf16[4096,512]{0,1:T(8,128)(2,1)S(1)}, bf16[4096,512]{0,1:T(8,128)(2,1)}, u32[]{:S(2)}) copy-start(bf16[4096,512]{0,1:T(8,128)(2,1)} %copy.10) | copy-start | bytes 12582916
  51.3 25.9 %collective-permute-start.5 = (bf16[8,64,512]{2,1,0:T(8,128)(2,1)S(1)}, bf16[8,64,512]{2,1,0:T(8,128)(2,1)S(1)}, u32[]{:S(2)}, u32[]{:S(2)}) collective-permute-start(bf16[8,64,512]{2,1,0:T(8,128)(2,1)S(1)} %collective-permute-done.rest_1_), channel_id=1, source_target_pairs={{0,1},{1,0},{2,3},{3,2},{4,5},{5,4},{6,7},{7,6},{8,9},{9,8},{10,11... | collective-permute-start | bytes 1572872 | tf_op jit(solution)/shard_map/ppermute | solution.py:115
  52.7 41.0 %collective-permute-start.9 = (bf16[8,64,512]{2,1,0:T(8,128)(2,1)S(1)}, bf16[8,64,512]{2,1,0:T(8,128)(2,1)S(1)}, u32[]{:S(2)}, u32[]{:S(2)}) collective-permute-start(bf16[8,64,512]{2,1,0:T(8,128)(2,1)S(1)} %all-to-all-done.1.rest_0_), channel_id=1, source_target_pairs={{0,2},{1,3},{2,0},{3,1},{4,6},{5,7},{6,4},{7,5},{8,10},{9,11},{10,... | collective-permute-start | bytes 1572872 | tf_op jit(solution)/shard_map/ppermute | solution.py:115
  55.0 38.7 %collective-permute-start.10 = (bf16[8,64,512]{2,1,0:T(8,128)(2,1)S(1)}, bf16[8,64,512]{2,1,0:T(8,128)(2,1)S(1)}, u32[]{:S(2)}, u32[]{:S(2)}) collective-permute-start(bf16[8,64,512]{2,1,0:T(8,128)(2,1)S(1)} %all-to-all-done.1.rest_0_), channel_id=1, source_target_pairs={{0,1},{1,0},{2,3},{3,2},{4,5},{5,4},{6,7},{7,6},{8,9},{9,8},{10,11... | collective-permute-start | bytes 1572872 | tf_op jit(solution)/shard_map/ppermute | solution.py:115
  55.1 2.2 %copy-start.4 = (bf16[4096,512]{0,1:T(8,128)(2,1)S(1)}, bf16[4096,512]{0,1:T(8,128)(2,1)}, u32[]{:S(2)}) copy-start(bf16[4096,512]{0,1:T(8,128)(2,1)} %copy.10) | copy-start | bytes 12582916
  63.5 19.7 %copy-start.5 = (bf16[4096]{0:T(1024)(128)(2,1)S(1)}, bf16[4096]{0:T(1024)(128)(2,1)}, u32[]{:S(2)}) copy-start(bf16[4096]{0:T(1024)(128)(2,1)} %param.9) | copy-start | bytes 24580
  81.1 1.4 collective-permute-start.6
  82.5 5.6 %collective-permute-start.7 = (f32[8,4096]{1,0:T(8,128)S(1)}, f32[8,4096]{1,0:T(8,128)S(1)}, u32[]{:S(2)}, u32[]{:S(2)}) collective-permute-start(f32[8,4096]{1,0:T(8,128)S(1)} %add.60.rest_2_), channel_id=1, source_target_pairs={{0,8},{4,12},{8,0},{12,4},{16,24},{20,28},{24,16},{28,20},{1,9},{5... | collective-permute-start | bytes 393224 | tf_op jit(solution)/shard_map/ppermute | solution.py:115
  88.2 5.6 %collective-permute-start.8 = (f32[8,4096]{1,0:T(8,128)S(1)}, f32[8,4096]{1,0:T(8,128)S(1)}, u32[]{:S(2)}, u32[]{:S(2)}) collective-permute-start(f32[8,4096]{1,0:T(8,128)S(1)} %add.61), channel_id=1, source_target_pairs={{0,16},{4,20},{8,24},{12,28},{16,0},{20,4},{24,8},{28,12},{1,17},{... | collective-permute-start | bytes 393224 | tf_op jit(solution)/shard_map/ppermute | solution.py:115
  89.7 4.1 %copy-start.1 = (bf16[4096,512]{1,0:T(8,128)(2,1)S(1)}, bf16[4096,512]{1,0:T(8,128)(2,1)}, u32[]{:S(2)}) copy-start(bf16[4096,512]{1,0:T(8,128)(2,1)} %weights.5) | copy-start | bytes 12582916
  93.7 21.5 %collective-permute-start.11 = (bf16[8,64,512]{2,1,0:T(8,128)(2,1)S(1)}, bf16[8,64,512]{2,1,0:T(8,128)(2,1)S(1)}, u32[]{:S(2)}, u32[]{:S(2)}) collective-permute-start(bf16[8,64,512]{2,1,0:T(8,128)(2,1)S(1)} %collective-permute-done.9.rest_1_), channel_id=1, source_target_pairs={{0,1},{1,0},{2,3},{3,2},{4,5},{5,4},{6,7},{7,6},{8,9},{9,8},{10,11... | collective-permute-start | bytes 1572872 | tf_op jit(solution)/shard_map/ppermute | solution.py:115
  98.3 19.5 %collective-permute-start.12 = (bf16[8,64,512]{2,1,0:T(8,128)(2,1)S(1)}, bf16[8,64,512]{2,1,0:T(8,128)(2,1)S(1)}, u32[]{:S(2)}, u32[]{:S(2)}) collective-permute-start(bf16[8,64,512]{2,1,0:T(8,128)(2,1)S(1)} %convert_element_type.43), channel_id=1, source_target_pairs={{0,1},{1,0},{2,3},{3,2},{4,5},{5,4},{6,7},{7,6},{8,9},{9,8},{10,11... | collective-permute-start | bytes 1572872 | tf_op jit(solution)/shard_map/ppermute | solution.py:115
  121.9 1.4 collective-permute-start.13
  122.0 25.2 %collective-permute-start.14 = (bf16[8,64,512]{2,1,0:T(8,128)(2,1)S(1)}, bf16[8,64,512]{2,1,0:T(8,128)(2,1)S(1)}, u32[]{:S(2)}, u32[]{:S(2)}) collective-permute-start(bf16[8,64,512]{2,1,0:T(8,128)(2,1)S(1)} %convert_element_type.44), channel_id=1, source_target_pairs={{0,1},{1,0},{2,3},{3,2},{4,5},{5,4},{6,7},{7,6},{8,9},{9,8},{10,11... | collective-permute-start | bytes 1572872 | tf_op jit(solution)/shard_map/ppermute | solution.py:115
  123.3 5.6 %collective-permute-start.16 = (f32[8,4096]{1,0:T(8,128)S(1)}, f32[8,4096]{1,0:T(8,128)S(1)}, u32[]{:S(2)}, u32[]{:S(2)}) collective-permute-start(f32[8,4096]{1,0:T(8,128)S(1)} %add.63.rest_1_), channel_id=1, source_target_pairs={{0,8},{4,12},{8,0},{12,4},{16,24},{20,28},{24,16},{28,20},{1,9},{5... | collective-permute-start | bytes 393224 | tf_op jit(solution)/shard_map/ppermute | solution.py:115
  124.1 26.2 %collective-permute-start.15 = (bf16[8,64,512]{2,1,0:T(8,128)(2,1)S(1)}, bf16[8,64,512]{2,1,0:T(8,128)(2,1)S(1)}, u32[]{:S(2)}, u32[]{:S(2)}) collective-permute-start(bf16[8,64,512]{2,1,0:T(8,128)(2,1)S(1)} %add_convert_fusion.3), channel_id=1, source_target_pairs={{0,2},{1,3},{2,0},{3,1},{4,6},{5,7},{6,4},{7,5},{8,10},{9,11},{10,... | collective-permute-start | bytes 1572872 | tf_op jit(solution)/shard_map/ppermute | solution.py:115
  128.9 5.0 %collective-permute-start.17 = (f32[8,4096]{1,0:T(8,128)S(1)}, f32[8,4096]{1,0:T(8,128)S(1)}, u32[]{:S(2)}, u32[]{:S(2)}) collective-permute-start(f32[8,4096]{1,0:T(8,128)S(1)} %add.67), channel_id=1, source_target_pairs={{0,16},{4,20},{8,24},{12,28},{16,0},{20,4},{24,8},{28,12},{1,17},{... | collective-permute-start | bytes 393224 | tf_op jit(solution)/shard_map/ppermute | solution.py:115
  138.5 20.9 %collective-permute-start.19 = (bf16[8,64,512]{2,1,0:T(8,128)(2,1)S(1)}, bf16[8,64,512]{2,1,0:T(8,128)(2,1)S(1)}, u32[]{:S(2)}, u32[]{:S(2)}) collective-permute-start(bf16[8,64,512]{2,1,0:T(8,128)(2,1)S(1)} %convert_element_type.52), channel_id=1, source_target_pairs={{0,1},{1,0},{2,3},{3,2},{4,5},{5,4},{6,7},{7,6},{8,9},{9,8},{10,11... | collective-permute-start | bytes 1572872 | tf_op jit(solution)/shard_map/ppermute | solution.py:115
  159.0 21.4 %collective-permute-start.18 = (bf16[8,64,512]{2,1,0:T(8,128)(2,1)S(1)}, bf16[8,64,512]{2,1,0:T(8,128)(2,1)S(1)}, u32[]{:S(2)}, u32[]{:S(2)}) collective-permute-start(bf16[8,64,512]{2,1,0:T(8,128)(2,1)S(1)} %convert_element_type.50), channel_id=1, source_target_pairs={{0,1},{1,0},{2,3},{3,2},{4,5},{5,4},{6,7},{7,6},{8,9},{9,8},{10,11... | collective-permute-start | bytes 1572872 | tf_op jit(solution)/shard_map/ppermute | solution.py:115
  160.3 25.8 %collective-permute-start.20 = (bf16[8,64,512]{2,1,0:T(8,128)(2,1)}, bf16[8,64,512]{2,1,0:T(8,128)(2,1)}, u32[]{:S(2)}, u32[]{:S(2)}) collective-permute-start(bf16[8,64,512]{2,1,0:T(8,128)(2,1)} %add_convert_fusion.1), channel_id=1, source_target_pairs={{0,2},{1,3},{2,0},{3,1},{4,6},{5,7},{6,4},{7,5},{8,10},{9,11},{10,... | collective-permute-start | bytes 1572872 | tf_op jit(solution)/shard_map/ppermute | solution.py:115
  164.8 23.4 %all-to-all-start.2 = ((bf16[8,64,512]{2,1,0:T(8,128)(2,1)}), bf16[8,64,512]{2,1,0:T(8,128)(2,1)S(1)}, u32[]{:S(2)}, u32[]{:S(2)}) async-start(bf16[8,64,512]{2,1,0:T(8,128)(2,1)} %add_convert_fusion.2), calls=%async_computation.2 | async-start | bytes 1048576 | tf_op jit(solution)/shard_map/all_to_all | solution.py:131
  168.3 2.2 %copy-start.2 = (bf16[4096,512]{1,0:T(8,128)(2,1)S(1)}, bf16[4096,512]{1,0:T(8,128)(2,1)}, u32[]{:S(2)}) copy-start(bf16[4096,512]{1,0:T(8,128)(2,1)} %weights.5) | copy-start | bytes 12582916
  188.2 13.2 %all-to-all-start.3 = ((bf16[8,64,512]{2,1,0:T(8,128)(2,1)}), bf16[8,64,512]{2,1,0:T(8,128)(2,1)S(1)}, u32[]{:S(2)}, u32[]{:S(2)}) async-start(bf16[8,64,512]{2,1,0:T(8,128)(2,1)} %add_convert_fusion), calls=%async_computation.3 | async-start | bytes 1048576 | tf_op jit(solution)/shard_map/all_to_all | solution.py:131

commit v3 on v2

--- a/solution.py
+++ b/solution.py
@@ -18,10 +18,10 @@
     return TILE if total % TILE == 0 else total
 
 
-def forward_kernel(slots, grows, code, weights, *rest):
+def forward_kernel(slots, grows, joined, code, weights, *rest):
     before, sources, out = rest[:grows], rest[grows : grows + len(slots)], rest[-1]
     codes = code[...]
-    total = before[0][...] if grows else jnp.zeros(out.shape, F32)
+    total = before[0][...] if grows else jnp.zeros(codes.shape, F32)
     for slot, source in zip(slots, sources):
         docs, part, width = source.shape
         rows = source[...].reshape(docs * part, width)
@@ -30,7 +30,11 @@
         ids = lax.broadcasted_iota(I32, scores.shape, 1) + slot * part
         hit = ids == codes[:, None, :]
         total += jnp.sum(jnp.where(hit, scores, 0.0), axis=1)
-    out[...] = total
+    if joined:
+        out[pl.ds(0, codes.shape[0]), :] = total
+        out[pl.ds(codes.shape[0], codes.shape[0]), :] = rest[grows + len(slots)][...]
+    else:
+        out[...] = total
 
 
 def backward_kernel(slots, waits, code, weights, logits, pooled, bias, *rest):
@@ -59,7 +63,7 @@
             out[...] += grown
 
 
-def forward(code, weights_t, slots, sources, before, waits):
+def forward(code, weights_t, slots, sources, before, join, waits):
     docs, part, width = sources[0].shape
     entries = weights_t.shape[1]
     tile = tile_of(entries)
@@ -67,19 +71,21 @@
     rows = pl.BlockSpec((docs, part, width), lambda t: (0, 0, 0))
     flops = 2 * docs * part * width * entries * len(slots)
     before = [] if before is None else [before]
+    high = docs * (1 + len(join))
     return pl.pallas_call(
-        functools.partial(forward_kernel, slots, len(before)),
-        out_shape=jax.ShapeDtypeStruct((docs, entries), F32),
+        functools.partial(forward_kernel, slots, len(before), len(join)),
+        out_shape=jax.ShapeDtypeStruct((high, entries), F32),
         grid=(entries // tile,),
         in_specs=[logit, pl.BlockSpec((width, tile), lambda t: (0, t))]
         + [logit] * len(before)
         + [rows] * len(slots)
+        + [logit] * len(join)
         + [ANY] * len(waits),
-        out_specs=logit,
+        out_specs=pl.BlockSpec((high, tile), lambda t: (0, t)),
         compiler_params=pltpu.CompilerParams(vmem_limit_bytes=VMEM_LIMIT),
         cost_estimate=pl.CostEstimate(flops=flops, bytes_accessed=6 << 20, transcendentals=0),
         name="forward",
-    )(code, weights_t, *before, *sources, *waits)
+    )(code, weights_t, *before, *sources, *join, *waits)
 
 
 def backward(code, weights, logits, pooled, bias, slots, part, waits):
@@ -96,7 +102,7 @@
             whole,
             pl.BlockSpec((tile, width), lambda t: (t, 0)),
             whole,
-            whole,
+            pl.BlockSpec((docs, tile), lambda t: (1, t)),
             pl.BlockSpec((1, tile), lambda t: (0, t)),
         ]
         + [ANY] * len(waits),
@@ -123,7 +129,8 @@
     parts = [tok_rows * share // 8 for share in SHARES]
     firsts = [sum(parts[:i]) for i in range(len(parts))]
     count = len(parts)
-    near = tuple(range(2, blocks, 2)) + (1,)
+    even = tuple(range(2, blocks, 2))
+    near = even + (1,)
     far = tuple(range(3, blocks, 2))
     bits = [1 << i for i in range(blocks.bit_length() - 1)]
 
@@ -157,13 +164,14 @@
     def run_forward(c, slots, *others):
         sources = [held[c][slot] for slot in slots]
         waits = tuple(clock) + others
-        partials[c] = forward(codes[c], weights_t, slots, sources, partials[c], waits)
+        join = (pooled,) if c == 0 and slots == far else ()
+        partials[c] = forward(codes[c], weights_t, slots, sources, partials[c], join, waits)
         clock[:] = [partials[c]]
 
     def run_backward(c, slots, *others):
         waits = tuple(clock) + others
         found = backward(
-            codes[c], head_weight, logits[c], pooled, bias, slots, parts[c], waits
+            codes[c], head_weight, logits[c], logits[0], bias, slots, parts[c], waits
         )
         grads[c].update(zip(slots, found))
         clock[:] = [found[0]]
@@ -184,8 +192,8 @@
                 else:
                     grads[c][slot ^ bit] = grads[c][slot ^ bit] + moved.astype(F32)
 
-    def run_sum(value, *between):
-        step = 1
+    def run_sum(value, *between, start=1):
+        step = start
         while step < size:
             value = value + exchange(value, "dp", step)
             if between:
@@ -208,14 +216,13 @@
     for part, first in zip(parts, firsts):
         here = kept & (inner >= first) & (inner < first + part)
         codes.append(jnp.where(here, (block ^ z) * part + inner - first, -1))
+    sents[1:], codes = together(sents[1:], codes)
     bias = head_bias.astype(F32)[None, :]
     queries = lax.dynamic_slice_in_dim(queries, z * entries, entries, 1)
     pooled = jnp.einsum("jd,jv->dv", scores, queries, preferred_element_type=F32)
-    pooled = run_sum(pooled)
     weights_t = head_weight.T
     run_forward(0, (0,))
     for c in range(1, count):
-        sents[c], pooled = together(sents[c], pooled)
         held[c][0] = swap(sents[c])
     arrived = [held[0][slot] for slot in near]
     arrived = tie(*arrived, *[held[c][0] for c in range(1, count)])
@@ -229,23 +236,29 @@
         if more:
             gather_near(c)
         run_forward(c - 1, near)
-        run_forward(c - 1, far, *([grads[c - 2][slot] for slot in far] if c > 1 else ()))
-        if c > 1:
-            reduce_near(c - 2)
+        run_forward(c - 1, far)
         between = []
         if more:
             between.append(lambda value: run_forward(c, (0,), value))
         elif count > 1:
             between.append(lambda value: run_backward(c - 2, (0,), value))
-        logits[c - 1] = run_sum(partials[c - 1], *between)
+        value = partials[c - 1]
+        if c > 1:
+            value = value + exchange(value, "dp", 1)
+            value, *got = together(value, *[grads[c - 2][slot] for slot in far])
+            grads[c - 2].update(zip(far, got))
+            reduce_near(c - 2)
+            logits[c - 1] = run_sum(value, *between, start=2)
+        else:
+            logits[c - 1] = run_sum(value, *between)
         if more:
             arrived = tie(*[held[c][slot] for slot in near])
             held[c].update(zip(near, arrived))
             gather_far(c)
         run_backward(c - 1, far)
         reduce_far(c - 1)
-        moving = [grads[c - 2][bit] for bit in bits] if c > 1 else ()
-        run_backward(c - 1, near, *moving)
+        run_backward(c - 1, even, *((grads[c - 2][1],) if c > 1 else ()))
+        run_backward(c - 1, (1,), *([grads[c - 2][bit] for bit in bits[1:]] if c > 1 else ()))
     reduce_near(count - 1)
     run_backward(count - 1, (0,))
 

time: 203 us -> 193 us (0.951)
  waiting for transfers between devices: 77.3 us -> 62.7 us
  starting transfers between devices: 38.7 us -> 43 us
    ppermute x21 -> x18, waiting for transfers between devices: 57.9 us -> 44.1 us  [exchange(): lax.ppermute(value, axis, [(i, i ^ bit) for i in range(lax.axis_size(axis...]
    all_to_all x4, starting transfers between devices: 15.8 us -> 18.6 us  [swap(): return lax.all_to_all(x, 'dp', split_axis=0, concat_axis=0, tiled=True)]
    ppermute x21 -> x18, starting transfers between devices: 22.9 us -> 24.4 us  [exchange(): lax.ppermute(value, axis, [(i, i ^ bit) for i in range(lax.axis_size(axis...]
    pallas_call x6 -> x8, Pallas kernels: 34.8 us -> 35.3 us  [backward(): pl.pallas_call(functools.partial(backward_kernel, slots, len(waits)), out...]
  transfers between devices with their start and end apart: 25 -> 22, of which waited for: 16 -> 15; matrix products, arithmetic and copies ran while one was open for 6% -> 7% of each run, Pallas kernels for 29% -> 31%
where the time goes in v3:
time: 193 us
  Pallas kernels  63.6 us (33%)
  waiting for transfers between devices  62.7 us (32%)
  starting transfers between devices  43 us (22%)
  local copies, waits for them, and re-layouts  16.1 us (8%)
  other arithmetic  6.76 us (4%)
    ppermute x18, waiting for transfers between devices, exchange(): lax.ppermute(value, axis, [(i, i ^ bit) for i in range(lax.axis_size(axis...  44.1 us
    pallas_call x8, Pallas kernels, backward(): pl.pallas_call(functools.partial(backward_kernel, slots, len(waits)), out...  35.3 us
    pallas_call x6, Pallas kernels, forward(): pl.pallas_call(functools.partial(forward_kernel, slots, len(before), len(...  28.3 us
    ppermute x18, starting transfers between devices, exchange(): lax.ppermute(value, axis, [(i, i ^ bit) for i in range(lax.axis_size(axis...  24.4 us
    all_to_all x4, starting transfers between devices, swap(): return lax.all_to_all(x, 'dp', split_axis=0, concat_axis=0, tiled=True)  18.6 us
    all_to_all x4, waiting for transfers between devices, swap(): return lax.all_to_all(x, 'dp', split_axis=0, concat_axis=0, tiled=True)  18.6 us
    unnamed x16, local copies, waits for them, and re-layouts  6.59 us
    optimization_barrier x1, local copies, waits for them, and re-layouts, together(): return lax.optimization_barrier(values)  6.42 us
  transfers between devices with their start and end apart: 22, of which 15 were waited for; matrix products, arithmetic and copies ran while one was open for 7% of the time, Pallas kernels for 31%

profile of v3, /device:TPU:0, one launch (start us, length us, event | category | flops | bytes accessed | tf_op | source)
XLA Modules:
  0.0 192.7 jit_solution(11146311705274255008)
XLA Ops:
  0.0 1.3 fusion.5
  1.3 0.8 copy.20
  2.2 5.2 %all-to-all-start = ((bf16[8,64,512]{2,1,0:T(8,128)(2,1)}), bf16[8,64,512]{2,1,0:T(8,128)(2,1)S(1)}, u32[]{:S(2)}, u32[]{:S(2)}) async-start(bf16[8,64,512]{2,1,0:T(8,128)(2,1)} %bitcast.28), calls=%async_computation | async-start | bytes 1048576 | tf_op jit(solution)/shard_map/all_to_all | solution.py:138
  7.3 0.8 copy.21
  8.2 8.9 %all-to-all-done.rest_0_ = bf16[8,64,512]{2,1,0:T(8,128)(2,1)S(1)} async-done(((bf16[8,64,512]{2,1,0:T(8,128)(2,1)}), bf16[8,64,512]{2,1,0:T(8,128)(2,1)S(1)}, u32[]{:S(2)}, u32[]{:S(2)}) %all-to-all-start) | async-done | bytes 524320 | tf_op jit(solution)/shard_map/all_to_all | solution.py:138
  17.1 1.6 collective-permute-start.1
  18.6 2.6 %collective-permute-start = (bf16[8,64,512]{2,1,0:T(8,128)(2,1)S(1)}, bf16[8,64,512]{2,1,0:T(8,128)(2,1)S(1)}, u32[]{:S(2)}, u32[]{:S(2)}) collective-permute-start(bf16[8,64,512]{2,1,0:T(8,128)(2,1)S(1)} %all-to-all-done.rest_0_), channel_id=1, source_target_pairs={{0,2},{1,3},{2,0},{3,1},{4,6},{5,7},{6,4},{7,5},{8,10},{9,11},{10,... | collective-permute-start | bytes 1572872 | tf_op jit(solution)/shard_map/ppermute | solution.py:121
  21.2 1.1 add_select_fusion.1
  22.3 3.5 %all-to-all-start.1 = ((bf16[8,64,512]{2,1,0:T(8,128)(2,1)}), bf16[8,64,512]{2,1,0:T(8,128)(2,1)S(1)}, u32[]{:S(2)}, u32[]{:S(2)}) async-start(bf16[8,64,512]{2,1,0:T(8,128)(2,1)} %bitcast.30), calls=%async_computation.1 | async-start | bytes 1048576 | tf_op jit(solution)/shard_map/all_to_all | solution.py:138
  25.9 6.4 %copy.11 = bf16[4096,512]{0,1:T(8,128)(2,1)} copy(bf16[4096,512]{1,0:T(8,128)(2,1)} %weights.7) | data formatting | bytes 8388608 | tf_op jit(solution)/shard_map/optimization_barrier | solution.py:117
  32.3 2.2 %copy-done.3 = bf16[4096,512]{0,1:T(8,128)(2,1)S(1)} copy-done((bf16[4096,512]{0,1:T(8,128)(2,1)S(1)}, bf16[4096,512]{0,1:T(8,128)(2,1)}, u32[]{:S(2)}) %copy-start.3) | copy-done | bytes 4194328
  34.5 4.0 %forward.6.rest_0_.rest_3_ = f32[8,4096]{1,0:T(8,128)S(1)} custom-call(s32[8,4096]{1,0:T(8,128)S(1)} %get-tuple-element.23.code, bf16[512,4096]{1,0:T(8,128)(2,1)S(1)} %bitcast.31, bf16[8,64,512]{2,1,0:T(8,128)(2,1)S(1)} %all-to-all-done.rest_0_), custom_call_target="tpu_custom_call" | custom-call | flops 2147483648 | bytes 6291456 | tf_op jit(solution)/shard_map/forward/pallas_call | solution.py:75
  38.4 1.1 collective-permute-done.1.rest_2_
  39.5 2.5 %collective-permute-done.rest_1_ = bf16[8,64,512]{2,1,0:T(8,128)(2,1)S(1)} collective-permute-done((bf16[8,64,512]{2,1,0:T(8,128)(2,1)S(1)}, bf16[8,64,512]{2,1,0:T(8,128)(2,1)S(1)}, u32[]{:S(2)}, u32[]{:S(2)}) %collective-permute-start) | collective-permute-done | bytes 524320 | tf_op jit(solution)/shard_map/ppermute | solution.py:121
  42.0 0.3 collective-permute-start.2
  42.3 0.2 fusion.2.rest_2_
  42.5 2.2 %copy-done.4 = bf16[4096,512]{0,1:T(8,128)(2,1)S(1)} copy-done((bf16[4096,512]{0,1:T(8,128)(2,1)S(1)}, bf16[4096,512]{0,1:T(8,128)(2,1)}, u32[]{:S(2)}) %copy-start.4) | copy-done | bytes 4194328
  44.7 6.2 %forward.7.rest_0_.rest_3_ = f32[8,4096]{1,0:T(8,128)S(1)} custom-call(s32[8,4096]{1,0:T(8,128)S(1)} %get-tuple-element.23.code, bf16[512,4096]{1,0:T(8,128)(2,1)S(1)} %bitcast.32, f32[8,4096]{1,0:T(8,128)S(1)} %forward.6.rest_0_.rest_3_, bf16[8,64,512]{2,1,0:T(8,128)(2,1)S(1)} %collective-permute-done.rest_1_, ...), custom_call_target="tpu_custom_call" | custom-call | flops 4294967296 | bytes 6291456 | tf_op jit(solution)/shard_map/forward/pallas_call | solution.py:75
  50.9 2.0 %collective-permute-done.2.rest_1_ = bf16[8,64,512]{2,1,0:T(8,128)(2,1)S(1)} collective-permute-done((bf16[8,64,512]{2,1,0:T(8,128)(2,1)S(1)}, bf16[8,64,512]{2,1,0:T(8,128)(2,1)S(1)}, u32[]{:S(2)}, u32[]{:S(2)}) %collective-permute-start.2) | collective-permute-done | bytes 524320 | tf_op jit(solution)/shard_map/ppermute | solution.py:121
  52.9 4.0 %forward.8.rest_1_ = f32[16,4096]{1,0:T(8,128)S(1)} custom-call(s32[8,4096]{1,0:T(8,128)S(1)} %get-tuple-element.23.code, bf16[512,4096]{1,0:T(8,128)(2,1)S(1)} %bitcast.33, f32[8,4096]{1,0:T(8,128)S(1)} %forward.7.rest_0_.rest_3_, bf16[8,64,512]{2,1,0:T(8,128)(2,1)S(1)} %collective-permute-done.2.rest_1_, f32[8,4096]{1,0:T(8,128)S(1)} %fusion.2.rest_2_, ...), custom_call_target="tpu_custom_call" | custom-call | flops 2147483648 | bytes 6291456 | tf_op jit(solution)/shard_map/forward/pallas_call | solution.py:75
  56.9 0.1 collective-permute-start.3
  57.0 0.4 collective-permute-start.7
  57.4 2.9 %collective-permute-start.6 = (bf16[8,64,512]{2,1,0:T(8,128)(2,1)S(1)}, bf16[8,64,512]{2,1,0:T(8,128)(2,1)S(1)}, u32[]{:S(2)}, u32[]{:S(2)}) collective-permute-start(bf16[8,64,512]{2,1,0:T(8,128)(2,1)S(1)} %all-to-all-done.1.rest_0_), channel_id=1, source_target_pairs={{0,2},{1,3},{2,0},{3,1},{4,6},{5,7},{6,4},{7,5},{8,10},{9,11},{10,... | collective-permute-start | bytes 1572872 | tf_op jit(solution)/shard_map/ppermute | solution.py:121
  60.3 4.8 %collective-permute-start.4 = (f32[16,4096]{1,0:T(8,128)S(1)}, f32[16,4096]{1,0:T(8,128)S(1)}, u32[]{:S(2)}, u32[]{:S(2)}) collective-permute-start(f32[16,4096]{1,0:T(8,128)S(1)} %add.48.rest_2_), channel_id=1, source_target_pairs={{0,8},{4,12},{8,0},{12,4},{16,24},{20,28},{24,16},{28,20},{1,9},{5... | collective-permute-start | bytes 786440 | tf_op jit(solution)/shard_map/ppermute | solution.py:121
  65.1 6.4 %collective-permute-done.4 = f32[16,4096]{1,0:T(8,128)S(1)} collective-permute-done((f32[16,4096]{1,0:T(8,128)S(1)}, f32[16,4096]{1,0:T(8,128)S(1)}, u32[]{:S(2)}, u32[]{:S(2)}) %collective-permute-start.4) | collective-permute-done | bytes 262176 | tf_op jit(solution)/shard_map/ppermute | solution.py:121
  71.5 0.1 collective-permute-start.5
  71.6 4.0 %forward.9.rest_0_ = f32[8,4096]{1,0:T(8,128)S(1)} custom-call(s32[8,4096]{1,0:T(8,128)S(1)} %get-tuple-element.32.code, bf16[512,4096]{1,0:T(8,128)(2,1)S(1)} %bitcast.34, bf16[8,64,512]{2,1,0:T(8,128)(2,1)S(1)} %all-to-all-done.1.rest_0_, f32[16,4096]{1,0:T(8,128)S(1)} %forward.8.rest_1_, f32[16,4096]{1,0:T(8,128)S(1)} %add.48.rest_2_), custom_call_target="tpu_custom_call" | custom-call | flops 2147483648 | bytes 6291456 | tf_op jit(solution)/shard_map/forward/pallas_call | solution.py:75
  75.6 6.7 %collective-permute-done.7.rest_2_ = bf16[8,64,512]{2,1,0:T(8,128)(2,1)S(1)} collective-permute-done((bf16[8,64,512]{2,1,0:T(8,128)(2,1)S(1)}, bf16[8,64,512]{2,1,0:T(8,128)(2,1)S(1)}, u32[]{:S(2)}, u32[]{:S(2)}) %collective-permute-start.7) | collective-permute-done | bytes 524320 | tf_op jit(solution)/shard_map/ppermute | solution.py:121
  82.3 1.5 collective-permute-done.6.rest_1_
  83.8 0.3 collective-permute-start.8
  84.2 4.4 %backward.8.rest_0_ = f32[8,64,512]{2,1,0:T(8,128)S(1)} custom-call(s32[8,4096]{1,0:T(8,128)S(1)} %get-tuple-element.23.code, bf16[4096,512]{1,0:T(8,128)(2,1)S(1)} %copy-done.1, f32[16,4096]{1,0:T(8,128)S(1)} %add.50.logits.pooled, f32[16,4096]{1,0:T(8,128)S(1)} %add.50.logits.pooled, f32[1,4096]{1,0:T(1,128)S(1)} %bitcast.37, f32[8,4096]{1,0:T(8,128)S(1)} %forward.9.rest_0_), custom_call_target="tpu_custom_call" | custom-call | flops 2147483648 | bytes 6291456 | tf_op jit(solution)/shard_map/backward/pallas_call | solution.py:97
  88.7 4.4 %backward.9.rest_0_ = f32[8,64,512]{2,1,0:T(8,128)S(1)} custom-call(s32[8,4096]{1,0:T(8,128)S(1)} %get-tuple-element.23.code, bf16[4096,512]{1,0:T(8,128)(2,1)S(1)} %copy-done.1, f32[16,4096]{1,0:T(8,128)S(1)} %add.50.logits.pooled, f32[16,4096]{1,0:T(8,128)S(1)} %add.50.logits.pooled, f32[1,4096]{1,0:T(1,128)S(1)} %bitcast.38, ...), custom_call_target="tpu_custom_call" | custom-call | flops 2147483648 | bytes 6291456 | tf_op jit(solution)/shard_map/backward/pallas_call | solution.py:97
  93.1 1.8 collective-permute-start.10
  94.9 4.4 %backward.10.rest_3_ = f32[8,64,512]{2,1,0:T(8,128)S(1)} custom-call(s32[8,4096]{1,0:T(8,128)S(1)} %get-tuple-element.23.code, bf16[4096,512]{1,0:T(8,128)(2,1)S(1)} %copy-done.1, f32[16,4096]{1,0:T(8,128)S(1)} %add.50.logits.pooled, f32[16,4096]{1,0:T(8,128)S(1)} %add.50.logits.pooled, f32[1,4096]{1,0:T(1,128)S(1)} %bitcast.39, ...), custom_call_target="tpu_custom_call" | custom-call | flops 2147483648 | bytes 6291456 | tf_op jit(solution)/shard_map/backward/pallas_call | solution.py:97
  99.3 6.2 %forward.10.rest_0_.rest_2_ = f32[8,4096]{1,0:T(8,128)S(1)} custom-call(s32[8,4096]{1,0:T(8,128)S(1)} %get-tuple-element.32.code, bf16[512,4096]{1,0:T(8,128)(2,1)S(1)} %bitcast.35, f32[8,4096]{1,0:T(8,128)S(1)} %forward.9.rest_0_, bf16[8,64,512]{2,1,0:T(8,128)(2,1)S(1)} %collective-permute-done.6.rest_1_, ...), custom_call_target="tpu_custom_call" | custom-call | flops 4294967296 | bytes 6291456 | tf_op jit(solution)/shard_map/forward/pallas_call | solution.py:75
  105.5 4.0 %forward.11.rest_0_ = f32[8,4096]{1,0:T(8,128)S(1)} custom-call(s32[8,4096]{1,0:T(8,128)S(1)} %get-tuple-element.32.code, bf16[512,4096]{1,0:T(8,128)(2,1)S(1)} %bitcast.36, f32[8,4096]{1,0:T(8,128)S(1)} %forward.10.rest_0_.rest_2_, bf16[8,64,512]{2,1,0:T(8,128)(2,1)S(1)} %collective-permute-done.8.rest_1_, f32[8,4096]{1,0:T(8,128)S(1)} %forward.10.rest_0_.rest_2_), custom_call_target="tpu_custom_call" | custom-call | flops 2147483648 | bytes 6291456 | tf_op jit(solution)/shard_map/forward/pallas_call | solution.py:75
  109.5 0.1 collective-permute-start.9
  109.7 0.4 collective-permute-start.12
  110.0 0.9 collective-permute-done.9
  110.9 5.0 %collective-permute-start.11 = (f32[8,4096]{1,0:T(8,128)S(1)}, f32[8,4096]{1,0:T(8,128)S(1)}, u32[]{:S(2)}, u32[]{:S(2)}) collective-permute-start(f32[8,4096]{1,0:T(8,128)S(1)} %add.51), channel_id=1, source_target_pairs={{0,8},{4,12},{8,0},{12,4},{16,24},{20,28},{24,16},{28,20},{1,9},{5... | collective-permute-start | bytes 393224 | tf_op jit(solution)/shard_map/ppermute | solution.py:121
  116.0 0.2 add_convert_fusion.3
  116.1 1.5 collective-permute-start.13
  117.7 2.1 %collective-permute-done.11 = f32[8,4096]{1,0:T(8,128)S(1)} collective-permute-done((f32[8,4096]{1,0:T(8,128)S(1)}, f32[8,4096]{1,0:T(8,128)S(1)}, u32[]{:S(2)}, u32[]{:S(2)}) %collective-permute-start.11) | collective-permute-done | bytes 131104 | tf_op jit(solution)/shard_map/ppermute | solution.py:121
  119.8 0.2 collective-permute-start.14
  120.0 4.4 %backward.11.rest_0_ = f32[8,64,512]{2,1,0:T(8,128)S(1)} custom-call(s32[8,4096]{1,0:T(8,128)S(1)} %get-tuple-element.23.code, bf16[4096,512]{1,0:T(8,128)(2,1)S(1)} %copy-done.1, f32[16,4096]{1,0:T(8,128)S(1)} %add.50.logits.pooled, f32[16,4096]{1,0:T(8,128)S(1)} %add.50.logits.pooled, f32[1,4096]{1,0:T(1,128)S(1)} %bitcast.40, ...), custom_call_target="tpu_custom_call" | custom-call | flops 2147483648 | bytes 6291456 | tf_op jit(solution)/shard_map/backward/pallas_call | solution.py:97
  124.4 0.5 collective-permute-done.14
  124.9 4.4 %backward.12.rest_0_ = f32[8,64,512]{2,1,0:T(8,128)S(1)} custom-call(s32[8,4096]{1,0:T(8,128)S(1)} %get-tuple-element.32.code, bf16[4096,512]{1,0:T(8,128)(2,1)S(1)} %copy-done.1, f32[8,4096]{1,0:T(8,128)S(1)} %add.56.logits, f32[16,4096]{1,0:T(8,128)S(1)} %add.50.logits.pooled, f32[1,4096]{1,0:T(1,128)S(1)} %bitcast.41, f32[8,64,512]{2,1,0:T(8,128)S(1)} %backward.11.rest_0_), custom_call_target="tpu_custom_call" | custom-call | flops 2147483648 | bytes 6291456 | tf_op jit(solution)/shard_map/backward/pallas_call | solution.py:97
  129.4 1.0 collective-permute-start.16
  130.5 4.4 %backward.13.rest_0_ = f32[8,64,512]{2,1,0:T(8,128)S(1)} custom-call(s32[8,4096]{1,0:T(8,128)S(1)} %get-tuple-element.32.code, bf16[4096,512]{1,0:T(8,128)(2,1)S(1)} %copy-done.1, f32[8,4096]{1,0:T(8,128)S(1)} %add.56.logits, f32[16,4096]{1,0:T(8,128)S(1)} %add.50.logits.pooled, f32[1,4096]{1,0:T(1,128)S(1)} %bitcast.42, ...), custom_call_target="tpu_custom_call" | custom-call | flops 2147483648 | bytes 6291456 | tf_op jit(solution)/shard_map/backward/pallas_call | solution.py:97
  134.9 7.3 %collective-permute-done.13.rest_1_ = bf16[8,64,512]{2,1,0:T(8,128)(2,1)S(1)} collective-permute-done((bf16[8,64,512]{2,1,0:T(8,128)(2,1)S(1)}, bf16[8,64,512]{2,1,0:T(8,128)(2,1)S(1)}, u32[]{:S(2)}, u32[]{:S(2)}) %collective-permute-start.13) | collective-permute-done | bytes 524320 | tf_op jit(solution)/shard_map/ppermute | solution.py:121
  142.2 4.4 %backward.14.rest_0_ = f32[8,64,512]{2,1,0:T(8,128)S(1)} custom-call(s32[8,4096]{1,0:T(8,128)S(1)} %get-tuple-element.32.code, bf16[4096,512]{1,0:T(8,128)(2,1)S(1)} %copy-done.1, f32[8,4096]{1,0:T(8,128)S(1)} %add.56.logits, f32[16,4096]{1,0:T(8,128)S(1)} %add.50.logits.pooled, f32[1,4096]{1,0:T(1,128)S(1)} %bitcast.43, ...), custom_call_target="tpu_custom_call" | custom-call | flops 2147483648 | bytes 6291456 | tf_op jit(solution)/shard_map/backward/pallas_call | solution.py:97
  146.8 1.8 collective-permute-done.16
  148.6 1.0 add_convert_fusion.1
  149.5 1.3 collective-permute-start.17
  150.8 1.0 add_convert_fusion.2
  151.8 4.1 %all-to-all-start.2 = ((bf16[8,64,512]{2,1,0:T(8,128)(2,1)}), bf16[8,64,512]{2,1,0:T(8,128)(2,1)S(1)}, u32[]{:S(2)}, u32[]{:S(2)}) async-start(bf16[8,64,512]{2,1,0:T(8,128)(2,1)} %add_convert_fusion.2), calls=%async_computation.2 | async-start | bytes 1048576 | tf_op jit(solution)/shard_map/all_to_all | solution.py:138
  155.9 2.2 %copy-done.2 = bf16[4096,512]{1,0:T(8,128)(2,1)S(1)} copy-done((bf16[4096,512]{1,0:T(8,128)(2,1)S(1)}, bf16[4096,512]{1,0:T(8,128)(2,1)}, u32[]{:S(2)}) %copy-start.2) | copy-done | bytes 4194328
  158.1 4.4 %backward.15 = f32[8,64,512]{2,1,0:T(8,128)S(1)} custom-call(s32[8,4096]{1,0:T(8,128)S(1)} %get-tuple-element.32.code, bf16[4096,512]{1,0:T(8,128)(2,1)S(1)} %copy-done.2, f32[8,4096]{1,0:T(8,128)S(1)} %add.56.logits, f32[16,4096]{1,0:T(8,128)S(1)} %add.50.logits.pooled, f32[1,4096]{1,0:T(1,128)S(1)} %bitcast.44, f32[8,64,512]{2,1,0:T(8,128)S(1)} %backward.14.rest_0_), custom_call_target="tpu_custom_call" | custom-call | flops 2147483648 | bytes 6291456 | tf_op jit(solution)/shard_map/backward/pallas_call | solution.py:97
  162.5 5.9 %collective-permute-done.15 = bf16[8,64,512]{2,1,0:T(8,128)(2,1)S(1)} collective-permute-done((bf16[8,64,512]{2,1,0:T(8,128)(2,1)S(1)}, bf16[8,64,512]{2,1,0:T(8,128)(2,1)S(1)}, u32[]{:S(2)}, u32[]{:S(2)}) %collective-permute-start.15) | collective-permute-done | bytes 524320 | tf_op jit(solution)/shard_map/ppermute | solution.py:121
  168.4 5.5 %collective-permute-done.17 = bf16[8,64,512]{2,1,0:T(8,128)(2,1)} collective-permute-done((bf16[8,64,512]{2,1,0:T(8,128)(2,1)}, bf16[8,64,512]{2,1,0:T(8,128)(2,1)}, u32[]{:S(2)}, u32[]{:S(2)}) %collective-permute-start.17) | collective-permute-done | bytes 524320 | tf_op jit(solution)/shard_map/ppermute | solution.py:121
  173.9 2.1 %add_convert_fusion = bf16[8,64,512]{2,1,0:T(8,128)(2,1)} fusion(bf16[8,64,512]{2,1,0:T(8,128)(2,1)} %collective-permute-done.17, f32[8,64,512]{2,1,0:T(8,128)S(1)} %backward.15, bf16[8,64,512]{2,1,0:T(8,128)(2,1)S(1)} %collective-permute-done.15), kind=kLoop, calls=%fused_computation.1 | loop fusion | flops 1310720 | bytes 2621440 | tf_op jit(solution)/shard_map/convert_element_type | solution.py:270
  175.9 5.9 %all-to-all-start.3 = ((bf16[8,64,512]{2,1,0:T(8,128)(2,1)}), bf16[8,64,512]{2,1,0:T(8,128)(2,1)S(1)}, u32[]{:S(2)}, u32[]{:S(2)}) async-start(bf16[8,64,512]{2,1,0:T(8,128)(2,1)} %add_convert_fusion), calls=%async_computation.3 | async-start | bytes 1048576 | tf_op jit(solution)/shard_map/all_to_all | solution.py:138
  181.9 9.7 %all-to-all-done.3 = bf16[8,64,512]{2,1,0:T(8,128)(2,1)S(1)} async-done(((bf16[8,64,512]{2,1,0:T(8,128)(2,1)}), bf16[8,64,512]{2,1,0:T(8,128)(2,1)S(1)}, u32[]{:S(2)}, u32[]{:S(2)}) %all-to-all-start.3) | async-done | bytes 524320 | tf_op jit(solution)/shard_map/all_to_all | solution.py:138
  191.6 1.1 pad_maximum_fusion
  (34 shorter events, 0.6 us)
Async XLA Ops:
  0.0 42.3 %copy-start = (bf16[4,16384]{1,0:T(4,128)(2,1)S(1)}, bf16[4,16384]{1,0:T(4,128)(2,1)}, u32[]{:S(2)}) copy-start(bf16[4,16384]{1,0:T(4,128)(2,1)} %param.12) | copy-start | bytes 393220
  1.3 19.9 %copy-start.7 = (s32[8]{0:T(128)S(1)}, s32[8]{0:T(128)}, u32[]{:S(2)}) copy-start(s32[8]{0:T(128)} %param.11) | copy-start | bytes 100
  2.2 14.9 %all-to-all-start = ((bf16[8,64,512]{2,1,0:T(8,128)(2,1)}), bf16[8,64,512]{2,1,0:T(8,128)(2,1)S(1)}, u32[]{:S(2)}, u32[]{:S(2)}) async-start(bf16[8,64,512]{2,1,0:T(8,128)(2,1)} %bitcast.28), calls=%async_computation | async-start | bytes 1048576 | tf_op jit(solution)/shard_map/all_to_all | solution.py:138
  17.1 22.4 %collective-permute-start.1 = (bf16[8,64,512]{2,1,0:T(8,128)(2,1)S(1)}, bf16[8,64,512]{2,1,0:T(8,128)(2,1)S(1)}, u32[]{:S(2)}, u32[]{:S(2)}) collective-permute-start(bf16[8,64,512]{2,1,0:T(8,128)(2,1)S(1)} %all-to-all-done.rest_0_), channel_id=1, source_target_pairs={{0,1},{1,0},{2,3},{3,2},{4,5},{5,4},{6,7},{7,6},{8,9},{9,8},{10,11... | collective-permute-start | bytes 1572872 | tf_op jit(solution)/shard_map/ppermute | solution.py:121
  18.6 23.3 %collective-permute-start = (bf16[8,64,512]{2,1,0:T(8,128)(2,1)S(1)}, bf16[8,64,512]{2,1,0:T(8,128)(2,1)S(1)}, u32[]{:S(2)}, u32[]{:S(2)}) collective-permute-start(bf16[8,64,512]{2,1,0:T(8,128)(2,1)S(1)} %all-to-all-done.rest_0_), channel_id=1, source_target_pairs={{0,2},{1,3},{2,0},{3,1},{4,6},{5,7},{6,4},{7,5},{8,10},{9,11},{10,... | collective-permute-start | bytes 1572872 | tf_op jit(solution)/shard_map/ppermute | solution.py:121
  22.3 16.1 %all-to-all-start.1 = ((bf16[8,64,512]{2,1,0:T(8,128)(2,1)}), bf16[8,64,512]{2,1,0:T(8,128)(2,1)S(1)}, u32[]{:S(2)}, u32[]{:S(2)}) async-start(bf16[8,64,512]{2,1,0:T(8,128)(2,1)} %bitcast.30), calls=%async_computation.1 | async-start | bytes 1048576 | tf_op jit(solution)/shard_map/all_to_all | solution.py:138
  32.3 2.2 %copy-start.3 = (bf16[4096,512]{0,1:T(8,128)(2,1)S(1)}, bf16[4096,512]{0,1:T(8,128)(2,1)}, u32[]{:S(2)}) copy-start(bf16[4096,512]{0,1:T(8,128)(2,1)} %copy.11) | copy-start | bytes 12582916
  34.5 7.9 %copy-start.6 = (bf16[4,8]{1,0:T(4,128)(2,1)S(1)}, bf16[4,8]{1,0:T(4,128)(2,1)}, u32[]{:S(2)}) copy-start(bf16[4,8]{1,0:T(4,128)(2,1)} %param.13) | copy-start | bytes 196
  42.0 10.9 %collective-permute-start.2 = (bf16[8,64,512]{2,1,0:T(8,128)(2,1)S(1)}, bf16[8,64,512]{2,1,0:T(8,128)(2,1)S(1)}, u32[]{:S(2)}, u32[]{:S(2)}) collective-permute-start(bf16[8,64,512]{2,1,0:T(8,128)(2,1)S(1)} %collective-permute-done.rest_1_), channel_id=1, source_target_pairs={{0,1},{1,0},{2,3},{3,2},{4,5},{5,4},{6,7},{7,6},{8,9},{9,8},{10,11... | collective-permute-start | bytes 1572872 | tf_op jit(solution)/shard_map/ppermute | solution.py:121
  42.5 2.2 %copy-start.4 = (bf16[4096,512]{0,1:T(8,128)(2,1)S(1)}, bf16[4096,512]{0,1:T(8,128)(2,1)}, u32[]{:S(2)}) copy-start(bf16[4096,512]{0,1:T(8,128)(2,1)} %copy.11) | copy-start | bytes 12582916
  50.9 20.7 %copy-start.5 = (bf16[4096]{0:T(1024)(128)(2,1)S(1)}, bf16[4096]{0:T(1024)(128)(2,1)}, u32[]{:S(2)}) copy-start(bf16[4096]{0:T(1024)(128)(2,1)} %param.9) | copy-start | bytes 24580
  56.9 3.4 %collective-permute-start.3 = (f32[16,4096]{1,0:T(8,128)S(1)}, f32[16,4096]{1,0:T(8,128)S(1)}, u32[]{:S(2)}, u32[]{:S(2)}) collective-permute-start(f32[16,4096]{1,0:T(8,128)S(1)} %forward.8.rest_1_), channel_id=1, source_target_pairs={{0,4},{4,0},{8,12},{12,8},{16,20},{20,16},{24,28},{28,24},{1,5},{5... | collective-permute-start | bytes 786440 | tf_op jit(solution)/shard_map/ppermute | solution.py:121
  57.0 25.3 %collective-permute-start.7 = (bf16[8,64,512]{2,1,0:T(8,128)(2,1)S(1)}, bf16[8,64,512]{2,1,0:T(8,128)(2,1)S(1)}, u32[]{:S(2)}, u32[]{:S(2)}) collective-permute-start(bf16[8,64,512]{2,1,0:T(8,128)(2,1)S(1)} %all-to-all-done.1.rest_0_), channel_id=1, source_target_pairs={{0,1},{1,0},{2,3},{3,2},{4,5},{5,4},{6,7},{7,6},{8,9},{9,8},{10,11... | collective-permute-start | bytes 1572872 | tf_op jit(solution)/shard_map/ppermute | solution.py:121
  57.4 26.5 %collective-permute-start.6 = (bf16[8,64,512]{2,1,0:T(8,128)(2,1)S(1)}, bf16[8,64,512]{2,1,0:T(8,128)(2,1)S(1)}, u32[]{:S(2)}, u32[]{:S(2)}) collective-permute-start(bf16[8,64,512]{2,1,0:T(8,128)(2,1)S(1)} %all-to-all-done.1.rest_0_), channel_id=1, source_target_pairs={{0,2},{1,3},{2,0},{3,1},{4,6},{5,7},{6,4},{7,5},{8,10},{9,11},{10,... | collective-permute-start | bytes 1572872 | tf_op jit(solution)/shard_map/ppermute | solution.py:121
  60.3 11.1 %collective-permute-start.4 = (f32[16,4096]{1,0:T(8,128)S(1)}, f32[16,4096]{1,0:T(8,128)S(1)}, u32[]{:S(2)}, u32[]{:S(2)}) collective-permute-start(f32[16,4096]{1,0:T(8,128)S(1)} %add.48.rest_2_), channel_id=1, source_target_pairs={{0,8},{4,12},{8,0},{12,4},{16,24},{20,28},{24,16},{28,20},{1,9},{5... | collective-permute-start | bytes 786440 | tf_op jit(solution)/shard_map/ppermute | solution.py:121
  71.5 12.7 %collective-permute-start.5 = (f32[16,4096]{1,0:T(8,128)S(1)}, f32[16,4096]{1,0:T(8,128)S(1)}, u32[]{:S(2)}, u32[]{:S(2)}) collective-permute-start(f32[16,4096]{1,0:T(8,128)S(1)} %add.49), channel_id=1, source_target_pairs={{0,16},{4,20},{8,24},{12,28},{16,0},{20,4},{24,8},{28,12},{1,17},{... | collective-permute-start | bytes 786440 | tf_op jit(solution)/shard_map/ppermute | solution.py:121
  71.6 12.6 %copy-start.1 = (bf16[4096,512]{1,0:T(8,128)(2,1)S(1)}, bf16[4096,512]{1,0:T(8,128)(2,1)}, u32[]{:S(2)}) copy-start(bf16[4096,512]{1,0:T(8,128)(2,1)} %weights.7) | copy-start | bytes 12582916
  83.8 21.7 %collective-permute-start.8 = (bf16[8,64,512]{2,1,0:T(8,128)(2,1)S(1)}, bf16[8,64,512]{2,1,0:T(8,128)(2,1)S(1)}, u32[]{:S(2)}, u32[]{:S(2)}) collective-permute-start(bf16[8,64,512]{2,1,0:T(8,128)(2,1)S(1)} %collective-permute-done.6.rest_1_), channel_id=1, source_target_pairs={{0,1},{1,0},{2,3},{3,2},{4,5},{5,4},{6,7},{7,6},{8,9},{9,8},{10,11... | collective-permute-start | bytes 1572872 | tf_op jit(solution)/shard_map/ppermute | solution.py:121
  93.1 17.8 %collective-permute-start.10 = (bf16[8,64,512]{2,1,0:T(8,128)(2,1)S(1)}, bf16[8,64,512]{2,1,0:T(8,128)(2,1)S(1)}, u32[]{:S(2)}, u32[]{:S(2)}) collective-permute-start(bf16[8,64,512]{2,1,0:T(8,128)(2,1)S(1)} %convert_element_type.43), channel_id=1, source_target_pairs={{0,1},{1,0},{2,3},{3,2},{4,5},{5,4},{6,7},{7,6},{8,9},{9,8},{10,11... | collective-permute-start | bytes 1572872 | tf_op jit(solution)/shard_map/ppermute | solution.py:121
  109.5 1.4 collective-permute-start.9
  109.7 20.8 %collective-permute-start.12 = (bf16[8,64,512]{2,1,0:T(8,128)(2,1)S(1)}, bf16[8,64,512]{2,1,0:T(8,128)(2,1)S(1)}, u32[]{:S(2)}, u32[]{:S(2)}) collective-permute-start(bf16[8,64,512]{2,1,0:T(8,128)(2,1)S(1)} %convert_element_type.44), channel_id=1, source_target_pairs={{0,1},{1,0},{2,3},{3,2},{4,5},{5,4},{6,7},{7,6},{8,9},{9,8},{10,11... | collective-permute-start | bytes 1572872 | tf_op jit(solution)/shard_map/ppermute | solution.py:121
  110.9 8.8 %collective-permute-start.11 = (f32[8,4096]{1,0:T(8,128)S(1)}, f32[8,4096]{1,0:T(8,128)S(1)}, u32[]{:S(2)}, u32[]{:S(2)}) collective-permute-start(f32[8,4096]{1,0:T(8,128)S(1)} %add.51), channel_id=1, source_target_pairs={{0,8},{4,12},{8,0},{12,4},{16,24},{20,28},{24,16},{28,20},{1,9},{5... | collective-permute-start | bytes 393224 | tf_op jit(solution)/shard_map/ppermute | solution.py:121
  116.1 26.1 %collective-permute-start.13 = (bf16[8,64,512]{2,1,0:T(8,128)(2,1)S(1)}, bf16[8,64,512]{2,1,0:T(8,128)(2,1)S(1)}, u32[]{:S(2)}, u32[]{:S(2)}) collective-permute-start(bf16[8,64,512]{2,1,0:T(8,128)(2,1)S(1)} %add_convert_fusion.3), channel_id=1, source_target_pairs={{0,2},{1,3},{2,0},{3,1},{4,6},{5,7},{6,4},{7,5},{8,10},{9,11},{10,... | collective-permute-start | bytes 1572872 | tf_op jit(solution)/shard_map/ppermute | solution.py:121
  119.8 5.1 %collective-permute-start.14 = (f32[8,4096]{1,0:T(8,128)S(1)}, f32[8,4096]{1,0:T(8,128)S(1)}, u32[]{:S(2)}, u32[]{:S(2)}) collective-permute-start(f32[8,4096]{1,0:T(8,128)S(1)} %add.52.rest_1_), channel_id=1, source_target_pairs={{0,16},{4,20},{8,24},{12,28},{16,0},{20,4},{24,8},{28,12},{1,17},{... | collective-permute-start | bytes 393224 | tf_op jit(solution)/shard_map/ppermute | solution.py:121
  129.4 19.1 %collective-permute-start.16 = (bf16[8,64,512]{2,1,0:T(8,128)(2,1)S(1)}, bf16[8,64,512]{2,1,0:T(8,128)(2,1)S(1)}, u32[]{:S(2)}, u32[]{:S(2)}) collective-permute-start(bf16[8,64,512]{2,1,0:T(8,128)(2,1)S(1)} %convert_element_type.52), channel_id=1, source_target_pairs={{0,1},{1,0},{2,3},{3,2},{4,5},{5,4},{6,7},{7,6},{8,9},{9,8},{10,11... | collective-permute-start | bytes 1572872 | tf_op jit(solution)/shard_map/ppermute | solution.py:121
  146.7 21.7 %collective-permute-start.15 = (bf16[8,64,512]{2,1,0:T(8,128)(2,1)S(1)}, bf16[8,64,512]{2,1,0:T(8,128)(2,1)S(1)}, u32[]{:S(2)}, u32[]{:S(2)}) collective-permute-start(bf16[8,64,512]{2,1,0:T(8,128)(2,1)S(1)} %convert_element_type.50), channel_id=1, source_target_pairs={{0,1},{1,0},{2,3},{3,2},{4,5},{5,4},{6,7},{7,6},{8,9},{9,8},{10,11... | collective-permute-start | bytes 1572872 | tf_op jit(solution)/shard_map/ppermute | solution.py:121
  149.5 24.4 %collective-permute-start.17 = (bf16[8,64,512]{2,1,0:T(8,128)(2,1)}, bf16[8,64,512]{2,1,0:T(8,128)(2,1)}, u32[]{:S(2)}, u32[]{:S(2)}) collective-permute-start(bf16[8,64,512]{2,1,0:T(8,128)(2,1)} %add_convert_fusion.1), channel_id=1, source_target_pairs={{0,2},{1,3},{2,0},{3,1},{4,6},{5,7},{6,4},{7,5},{8,10},{9,11},{10,... | collective-permute-start | bytes 1572872 | tf_op jit(solution)/shard_map/ppermute | solution.py:121
  151.8 24.1 %all-to-all-start.2 = ((bf16[8,64,512]{2,1,0:T(8,128)(2,1)}), bf16[8,64,512]{2,1,0:T(8,128)(2,1)S(1)}, u32[]{:S(2)}, u32[]{:S(2)}) async-start(bf16[8,64,512]{2,1,0:T(8,128)(2,1)} %add_convert_fusion.2), calls=%async_computation.2 | async-start | bytes 1048576 | tf_op jit(solution)/shard_map/all_to_all | solution.py:138
  155.9 2.2 %copy-start.2 = (bf16[4096,512]{1,0:T(8,128)(2,1)S(1)}, bf16[4096,512]{1,0:T(8,128)(2,1)}, u32[]{:S(2)}) copy-start(bf16[4096,512]{1,0:T(8,128)(2,1)} %weights.7) | copy-start | bytes 12582916
  175.9 15.6 %all-to-all-start.3 = ((bf16[8,64,512]{2,1,0:T(8,128)(2,1)}), bf16[8,64,512]{2,1,0:T(8,128)(2,1)S(1)}, u32[]{:S(2)}, u32[]{:S(2)}) async-start(bf16[8,64,512]{2,1,0:T(8,128)(2,1)} %add_convert_fusion), calls=%async_computation.3 | async-start | bytes 1048576 | tf_op jit(solution)/shard_map/all_to_all | solution.py:138

commit v4 on v3

v4 whole, which is shorter than its diff:
```python
import functools

import jax
import jax.numpy as jnp
from jax import lax
from jax.experimental import pallas as pl
from jax.experimental.pallas import tpu as pltpu
from jax.sharding import PartitionSpec as P

F32, BF16, I32 = jnp.float32, jnp.bfloat16, jnp.int32
SHARES = (4, 4)
VMEM_LIMIT = 28 * 1024 * 1024
TILE = 1024
ANY = pl.BlockSpec(memory_space=pl.ANY)
FAR = pl.BlockSpec(memory_space=pltpu.HBM)
SCALAR = pl.BlockSpec(memory_space=pltpu.SMEM)


def tile_of(total):
    return TILE if total % TILE == 0 else total


def columns(side, k, half):
    at = side[0] if k == 0 else 1 - side[0]
    return pl.ds(pl.multiple_of(at * half, half), half)


def weights_of_step(side, sources, buffer, arrived):
    tile, half = buffer.shape[0] // arrived.shape[1], buffer.shape[1] // 2
    step = pl.program_id(0)

    def copy(k, t):
        where_at = pl.ds(t * tile, tile)
        target = buffer.at[where_at, columns(side, k, half)]
        return pltpu.make_async_copy(sources[k].at[where_at], target, arrived.at[k, t])

    @pl.when(step == 0)
    def _():
        for t in range(arrived.shape[1]):
            for k in range(2):
                copy(k, t).start()

    for k in range(2):
        copy(k, step).wait()
    return buffer[pl.ds(pl.multiple_of(step * tile, tile), tile), :]


def score(rows, weights):
    return lax.dot_general(rows, weights, (((1,), (1,)), ((), ())), preferred_element_type=F32)


def forward_kernel(slots, grows, joined, side, code, mine, other, *rest):
    before, sources = rest[:grows], rest[grows : grows + len(slots)]
    out, buffer, arrived = rest[-3:]
    weights = weights_of_step(side, (mine, other), buffer, arrived)
    codes = code[...]
    total = before[0][...] if grows else jnp.zeros(codes.shape, F32)
    for slot, source in zip(slots, sources):
        docs, part, width = source.shape
        scores = score(source[...].reshape(docs * part, width), weights)
        scores = scores.reshape(docs, part, scores.shape[1])
        ids = lax.broadcasted_iota(I32, scores.shape, 1) + slot * part
        hit = ids == codes[:, None, :]
        total += jnp.sum(jnp.where(hit, scores, 0.0), axis=1)
    if joined:
        out[pl.ds(0, codes.shape[0]), :] = total
        out[pl.ds(codes.shape[0], codes.shape[0]), :] = rest[grows + len(slots)][...]
    else:
        out[...] = total


def backward_kernel(slots, waits, side, code, mine, other, logits, joined, bias, *rest):
    outs, buffer, arrived = rest[waits:-2], rest[-2], rest[-1]
    weights = weights_of_step(side, (mine, other), buffer, arrived)
    step = pl.program_id(0)
    docs = code.shape[0]
    x = logits[pl.ds(0, docs), :] + bias[...]
    soft = jnp.maximum(x, 0.0) + jnp.log1p(jnp.exp(-jnp.abs(x)))
    factor = joined[pl.ds(docs, docs), :] * jax.nn.sigmoid(x) / (1.0 + soft)
    delta = factor.astype(BF16).astype(F32)
    codes = code[...]
    for slot, out in zip(slots, outs):
        docs, part, width = out.shape
        ids = lax.broadcasted_iota(I32, (docs, part, codes.shape[1]), 1) + slot * part
        hit = ids == codes[:, None, :]
        spread = jnp.where(hit, delta[:, None, :], 0.0).astype(BF16)
        spread = spread.reshape(docs * part, codes.shape[1])
        grown = jnp.dot(spread, weights, preferred_element_type=F32)
        grown = grown.reshape(docs, part, width)

        @pl.when(step == 0)
        def _():
            out[...] = grown

        @pl.when(step > 0)
        def _():
            out[...] += grown


def forward(side, code, mine, other, slots, sources, before, join, waits):
    docs, part, width = sources[0].shape
    entries = mine.shape[0]
    tile = tile_of(entries)
    logit = pl.BlockSpec((docs, tile), lambda t: (0, t))
    rows = pl.BlockSpec((docs, part, width), lambda t: (0, 0, 0))
    flops = 2 * docs * part * width * entries * len(slots)
    before = [] if before is None else [before]
    high = docs * (1 + len(join))
    return pl.pallas_call(
        functools.partial(forward_kernel, slots, len(before), len(join)),
        out_shape=jax.ShapeDtypeStruct((high, entries), F32),
        grid=(entries // tile,),
        in_specs=[SCALAR, logit, FAR, FAR]
        + [logit] * len(before)
        + [rows] * len(slots)
        + [logit] * len(join)
        + [ANY] * len(waits),
        out_specs=pl.BlockSpec((high, tile), lambda t: (0, t)),
        scratch_shapes=[
            pltpu.VMEM((entries, width), BF16),
            pltpu.SemaphoreType.DMA((2, entries // tile)),
        ],
        compiler_params=pltpu.CompilerParams(vmem_limit_bytes=VMEM_LIMIT),
        cost_estimate=pl.CostEstimate(flops=flops, bytes_accessed=6 << 20, transcendentals=0),
        name="forward",
    )(side, code, mine, other, *before, *sources, *join, *waits)


def backward(side, code, mine, other, logits, joined, bias, slots, part, waits):
    docs, entries = code.shape
    width = 2 * mine.shape[1]
    tile = tile_of(entries)
    whole = pl.BlockSpec((docs, tile), lambda t: (0, t))
    flops = 2 * docs * part * width * entries * len(slots)
    return pl.pallas_call(
        functools.partial(backward_kernel, slots, len(waits)),
        out_shape=[jax.ShapeDtypeStruct((docs, part, width), F32)] * len(slots),
        grid=(entries // tile,),
        in_specs=[
            SCALAR,
            whole,
            FAR,
            FAR,
            pl.BlockSpec((logits.shape[0], tile), lambda t: (0, t)),
            pl.BlockSpec((2 * docs, tile), lambda t: (0, t)),
            pl.BlockSpec((1, tile), lambda t: (0, t)),
        ]
        + [ANY] * len(waits),
        out_specs=[pl.BlockSpec((docs, part, width), lambda t: (0, 0, 0))] * len(slots),
        scratch_shapes=[
            pltpu.VMEM((entries, width), BF16),
            pltpu.SemaphoreType.DMA((2, entries // tile)),
        ],
        compiler_params=pltpu.CompilerParams(vmem_limit_bytes=VMEM_LIMIT),
        cost_estimate=pl.CostEstimate(flops=flops, bytes_accessed=6 << 20, transcendentals=0),
        name="backward",
    )(side, code, mine, other, logits, joined, bias, *waits)


def together(*values):
    return lax.optimization_barrier(values)


def exchange(value, axis, bit):
    return lax.ppermute(value, axis, [(i, i ^ bit) for i in range(lax.axis_size(axis))])


def on_device(hidden, head_weight, head_bias, argmax, lengths, query_terms, score_grad):
    blocks, size = lax.axis_size("seq"), lax.axis_size("dp")
    z = lax.axis_index("seq")
    core = lax.axis_index("dp") % 2
    side = jnp.reshape(core, (1,)).astype(I32)
    pairs = size // 2
    groups = [list(range(side, size, 2)) for side in (0, 1)]
    tok_rows = hidden.shape[1]
    entries, width = head_weight.shape
    parts = [tok_rows * share // 8 for share in SHARES]
    firsts = [sum(parts[:i]) for i in range(len(parts))]
    count = len(parts)
    even = tuple(range(2, blocks, 2))
    near = even + (1,)
    far = tuple(range(3, blocks, 2))
    bits = [1 << i for i in range(blocks.bit_length() - 1)]

    def swap(x):
        return lax.all_to_all(
            x, "dp", split_axis=0, concat_axis=0, axis_index_groups=groups, tiled=True
        )

    def own_docs(x):
        x = x.reshape((pairs, 2, x.shape[0] // size) + x.shape[1:])
        x = lax.dynamic_index_in_dim(x, core, 1, keepdims=False)
        return x.reshape((-1,) + x.shape[2:])

    sents = []
    for part, first in zip(parts, firsts):
        sent = hidden[:, first : first + part]
        sent = sent.reshape(-1, part, pairs, 2 * width).transpose(2, 0, 1, 3)
        sents.append(sent.reshape(-1, part, 2 * width))

    held = [dict() for _ in range(count)]
    partials, logits = [None] * count, [None] * count
    grads = [dict() for _ in range(count)]
    clock = []

    def tie(*values):
        out = together(*values, *clock)
        clock[:] = out[len(values) :]
        return out[: len(values)]

    def gather_near(c):
        for bit in reversed(bits):
            for slot in sorted(held[c]) if bit > 1 else (0,):
                held[c][slot ^ bit] = exchange(held[c][slot], "seq", bit)

    def gather_far(c):
        for slot in far:
            held[c][slot] = exchange(held[c][slot ^ 1], "seq", 1)

    def run_forward(c, slots, *others):
        sources = [held[c][slot] for slot in slots]
        waits = tuple(clock) + others
        join = (pooled,) if c == 0 and slots == far else ()
        partials[c] = forward(side, codes[c], mine, other, slots, sources, partials[c], join, waits)
        clock[:] = [partials[c]]

    def run_backward(c, slots, *others):
        waits = tuple(clock) + others
        found = backward(
            side, codes[c], mine, other, logits[c], logits[0], bias, slots, parts[c], waits
        )
        grads[c].update(zip(slots, found))
        clock[:] = [found[0]]

    def reduce_far(c):
        for slot in reversed(far):
            grads[c][slot] = exchange(grads[c][slot].astype(BF16), "seq", 1)

    def reduce_near(c):
        grads[c][1] = exchange(grads[c][1].astype(BF16), "seq", 1)
        for slot in far:
            grads[c][slot ^ 1] = grads[c][slot ^ 1] + grads[c].pop(slot).astype(F32)
        for bit in bits[1:]:
            for slot in range(blocks - bit, 0, -2 * bit):
                moved = exchange(grads[c].pop(slot).astype(BF16), "seq", bit)
                if slot == bit:
                    grads[c][slot] = moved
                else:
                    grads[c][slot ^ bit] = grads[c][slot ^ bit] + moved.astype(F32)

    def run_sum(value, *between, start=2):
        step = start
        while step < size:
            value = value + exchange(value, "dp", step)
            if between:
                between[0](value)
                between = between[1:]
            step *= 2
        return value

    other = exchange(head_weight, "dp", 1)
    held[0][0] = swap(sents[0])
    gather_near(0)

    mine, saved_all, queries, scores, held[0][0] = together(
        head_weight, argmax, query_terms, score_grad, held[0][0]
    )
    saved = own_docs(lax.dynamic_slice_in_dim(saved_all, z * entries, entries, 1))
    block = saved // tok_rows
    inner = saved - block * tok_rows
    kept = (block < blocks) & (saved < own_docs(lengths)[:, None])
    codes = []
    for part, first in zip(parts, firsts):
        here = kept & (inner >= first) & (inner < first + part)
        codes.append(jnp.where(here, (block ^ z) * part + inner - first, -1))
    bias = head_bias.astype(F32)[None, :]
    queries = lax.dynamic_slice_in_dim(queries, z * entries, entries, 1)
    pooled = jnp.einsum("jd,jv->dv", scores, queries, preferred_element_type=F32)
    pooled = pooled.reshape((pairs, 2, -1, entries))
    kept_part = lax.dynamic_index_in_dim(pooled, core, 1, keepdims=False)
    sent_part = lax.dynamic_index_in_dim(pooled, 1 - core, 1, keepdims=False)
    pooled = (kept_part + exchange(sent_part, "dp", 1)).reshape(-1, entries)
    run_forward(0, (0,))
    sents[1:] = tie(*sents[1:])
    for c in range(1, count):
        held[c][0] = swap(sents[c])
    arrived = [held[0][slot] for slot in near]
    arrived = tie(*arrived, *[held[c][0] for c in range(1, count)])
    held[0].update(zip(near, arrived))
    for c in range(1, count):
        held[c][0] = arrived[len(near) + c - 1]
    gather_far(0)

    for c in range(1, count + 1):
        more = c < count
        if more:
            gather_near(c)
        if c == 1:
            run_forward(0, near)
        run_forward(c - 1, far)
        value = partials[c - 1]
        if c > 1:
            value = value + exchange(value, "dp", 2)
            value, *got = together(value, *[grads[c - 2][slot] for slot in far])
            grads[c - 2].update(zip(far, got))
            reduce_near(c - 2)
            logits[c - 1] = run_sum(value, start=4)
        else:
            logits[c - 1] = run_sum(value)
        run_backward(c - 1, far)
        reduce_far(c - 1)
        if more:
            arrived = tie(*[held[c][slot] for slot in near])
            held[c].update(zip(near, arrived))
            gather_far(c)
            run_forward(c, (0,) + near)
            run_backward(c - 1, near)
        else:
            run_backward(c - 1, even, *((grads[c - 2][1],) if c > 1 else ()))
            run_backward(c - 1, (1,), *([grads[c - 2][bit] for bit in bits[1:]] if c > 1 else ()))
    reduce_near(count - 1)
    for c in range(count):
        run_backward(c, (0,))

    results = []
    for c in range(count):
        total = grads[c].pop(0)
        for moved in grads[c].values():
            total = total + moved.astype(F32)
        back = swap(total.astype(BF16))
        back = back.reshape(pairs, -1, parts[c], 2 * width).transpose(1, 2, 0, 3)
        results.append(back.reshape(-1, parts[c], size * width))
    return jnp.concatenate(results, axis=1)


def solution(mesh):
    return jax.shard_map(
        on_device,
        mesh=mesh,
        in_specs=(
            P("dp", "seq", None),
            P("seq", "dp"),
            P("seq"),
            P(),
            P(),
            P("dp", None),
            P("dp", None),
        ),
        out_specs=P("dp", "seq", None),
        check_vma=False,
    )
```

time: 193 us -> 185 us (0.959)
  local copies, waits for them, and re-layouts: 16.1 us -> 10.3 us
  starting transfers between devices: 43 us -> 37.4 us
  Pallas kernels: 63.6 us -> 66.1 us
    optimization_barrier x1 -> x0, local copies, waits for them, and re-layouts: 6.42 us -> none  [together(): return lax.optimization_barrier(values)]
    ppermute x18, waiting for transfers between devices: 44.1 us -> 49.5 us  [exchange(): lax.ppermute(value, axis, [(i, i ^ bit) for i in range(lax.axis_size(axis...]
    all_to_all x4, waiting for transfers between devices: 18.6 us -> 14.1 us  [swap(): lax.all_to_all(x, 'dp', split_axis=0, concat_axis=0, axis_index_groups=gr...]
    ppermute x18, starting transfers between devices: 24.4 us -> 21.5 us  [exchange(): lax.ppermute(value, axis, [(i, i ^ bit) for i in range(lax.axis_size(axis...]
    all_to_all x4, starting transfers between devices: 18.6 us -> 15.9 us  [swap(): lax.all_to_all(x, 'dp', split_axis=0, concat_axis=0, axis_index_groups=gr...]
    pallas_call x8 -> x7, Pallas kernels: 35.3 us -> 36.7 us  [backward(): pl.pallas_call(functools.partial(backward_kernel, slots, len(waits)), out...]
    pallas_call x6 -> x5, Pallas kernels: 28.3 us -> 29.4 us  [forward(): pl.pallas_call(functools.partial(forward_kernel, slots, len(before), len(...]
    unnamed x16 -> x17, local copies, waits for them, and re-layouts: 6.59 us -> 6.63 us
  transfers between devices with their start and end apart: 22 -> 22, of which waited for: 15 -> 11; matrix products, arithmetic and copies ran while one was open for 7% -> 5% of each run, Pallas kernels for 31% -> 36%
where the time goes in v4:
time: 185 us
  Pallas kernels  66.1 us (36%)
  waiting for transfers between devices  63.6 us (34%)
  starting transfers between devices  37.4 us (20%)
  local copies, waits for them, and re-layouts  10.3 us (6%)
  other arithmetic  5.91 us (3%)
    ppermute x18, waiting for transfers between devices, exchange(): lax.ppermute(value, axis, [(i, i ^ bit) for i in range(lax.axis_size(axis...  49.5 us
    pallas_call x7, Pallas kernels, backward(): pl.pallas_call(functools.partial(backward_kernel, slots, len(waits)), out...  36.7 us
    pallas_call x5, Pallas kernels, forward(): pl.pallas_call(functools.partial(forward_kernel, slots, len(before), len(...  29.4 us
    ppermute x18, starting transfers between devices, exchange(): lax.ppermute(value, axis, [(i, i ^ bit) for i in range(lax.axis_size(axis...  21.5 us
    all_to_all x4, starting transfers between devices, swap(): lax.all_to_all(x, 'dp', split_axis=0, concat_axis=0, axis_index_groups=gr...  15.9 us
    all_to_all x4, waiting for transfers between devices, swap(): lax.all_to_all(x, 'dp', split_axis=0, concat_axis=0, axis_index_groups=gr...  14.1 us
    unnamed x17, local copies, waits for them, and re-layouts  6.63 us
  transfers between devices with their start and end apart: 22, of which 11 were waited for; matrix products, arithmetic and copies ran while one was open for 5% of the time, Pallas kernels for 36%

profile of v4, /device:TPU:0, one launch (start us, length us, event | category | flops | bytes accessed | tf_op | source)
XLA Modules:
  0.0 184.6 jit_solution(15704630105198429504)
XLA Ops:
  0.0 0.5 collective-permute-start
  0.5 1.3 fusion.9
  1.7 0.9 copy.47
  2.6 4.8 %all-to-all-start = ((bf16[4,64,1024]{2,1,0:T(8,128)(2,1)}), bf16[4,64,1024]{2,1,0:T(8,128)(2,1)S(1)}, u32[]{:S(2)}, u32[]{:S(2)}) async-start(bf16[4,64,1024]{2,1,0:T(8,128)(2,1)} %bitcast.72), calls=%async_computation | async-start | bytes 1048576 | tf_op jit(solution)/shard_map/all_to_all | solution.py:186
  7.4 0.1 reshape.49
  7.5 0.8 copy.46
  8.3 0.2 dynamic-slice_reduce_fusion
  8.5 7.5 %all-to-all-done.rest_0_ = bf16[4,64,1024]{2,1,0:T(8,128)(2,1)S(1)} async-done(((bf16[4,64,1024]{2,1,0:T(8,128)(2,1)}), bf16[4,64,1024]{2,1,0:T(8,128)(2,1)S(1)}, u32[]{:S(2)}, u32[]{:S(2)}) %all-to-all-start) | async-done | bytes 524320 | tf_op jit(solution)/shard_map/all_to_all | solution.py:186
  16.0 0.1 reshape.47
  16.1 1.0 fusion.6
  17.1 0.1 reshape.52
  17.2 1.6 collective-permute-start.2
  18.8 2.6 %collective-permute-start.1 = (bf16[4,64,1024]{2,1,0:T(8,128)(2,1)S(1)}, bf16[4,64,1024]{2,1,0:T(8,128)(2,1)S(1)}, u32[]{:S(2)}, u32[]{:S(2)}) collective-permute-start(bf16[4,64,1024]{2,1,0:T(8,128)(2,1)S(1)} %all-to-all-done.rest_0_), channel_id=1, source_target_pairs={{0,2},{1,3},{2,0},{3,1},{4,6},{5,7},{6,4},{7,5},{8,10},{9,11},{10,... | collective-permute-start | bytes 1572872 | tf_op jit(solution)/shard_map/ppermute | solution.py:165
  21.5 0.2 and_select_fusion
  21.7 2.2 %copy-done.1 = bf16[4096,512]{1,0:T(8,128)(2,1)S(1)} copy-done((bf16[4096,512]{1,0:T(8,128)(2,1)S(1)}, bf16[4096,512]{1,0:T(8,128)(2,1)}, u32[]{:S(2)}) %copy-start.1) | copy-done | bytes 4194328
  23.9 4.6 %forward.5.rest_0_.rest_3_ = f32[4,4096]{1,0:T(4,128)S(1)} custom-call(s32[1]{0:T(128)} %bitcast.side, s32[4,4096]{1,0:T(4,128)S(1)} %get-tuple-element.45.code, bf16[4096,512]{1,0:T(8,128)(2,1)S(1)} %copy-done.1, bf16[4096,512]{1,0:T(8,128)(2,1)} %collective-permute-done.other, bf16[4,64,1024]{2,1,0:T(8,128)(2,1)S(1)} %all-to-all-done.rest_0_), custom_call_target="tpu_custom_call" | custom-call | flops 2147483648 | bytes 6291456 | tf_op jit(solution)/shard_map/forward/pallas_call | solution.py:109
  28.5 3.5 %all-to-all-start.1 = ((bf16[4,64,1024]{2,1,0:T(8,128)(2,1)}), bf16[4,64,1024]{2,1,0:T(8,128)(2,1)S(1)}, u32[]{:S(2)}, u32[]{:S(2)}) async-start(bf16[4,64,1024]{2,1,0:T(8,128)(2,1)} %bitcast.70), calls=%async_computation.1 | async-start | bytes 1048576 | tf_op jit(solution)/shard_map/all_to_all | solution.py:186
  32.0 0.1 constant_dynamic-slice_fusion.1
  32.2 0.1 collective-permute-start.4
  32.3 9.2 %collective-permute-done.2.rest_2_ = bf16[4,64,1024]{2,1,0:T(8,128)(2,1)S(1)} collective-permute-done((bf16[4,64,1024]{2,1,0:T(8,128)(2,1)S(1)}, bf16[4,64,1024]{2,1,0:T(8,128)(2,1)S(1)}, u32[]{:S(2)}, u32[]{:S(2)}) %collective-permute-start.2) | collective-permute-done | bytes 524320 | tf_op jit(solution)/shard_map/ppermute | solution.py:165
  41.5 2.5 %collective-permute-done.1.rest_1_ = bf16[4,64,1024]{2,1,0:T(8,128)(2,1)S(1)} collective-permute-done((bf16[4,64,1024]{2,1,0:T(8,128)(2,1)S(1)}, bf16[4,64,1024]{2,1,0:T(8,128)(2,1)S(1)}, u32[]{:S(2)}, u32[]{:S(2)}) %collective-permute-start.1) | collective-permute-done | bytes 524320 | tf_op jit(solution)/shard_map/ppermute | solution.py:165
  44.0 0.3 collective-permute-start.3
  44.4 1.8 collective-permute-start.8
  46.1 1.1 collective-permute-start.7
  47.2 2.2 %copy-done.2 = bf16[4096,512]{1,0:T(8,128)(2,1)S(1)} copy-done((bf16[4096,512]{1,0:T(8,128)(2,1)S(1)}, bf16[4096,512]{1,0:T(8,128)(2,1)}, u32[]{:S(2)}) %copy-start.2) | copy-done | bytes 4194328
  49.4 6.7 %forward.6.rest_0_.rest_3_ = f32[4,4096]{1,0:T(4,128)S(1)} custom-call(s32[1]{0:T(128)} %bitcast.side, s32[4,4096]{1,0:T(4,128)S(1)} %get-tuple-element.45.code, bf16[4096,512]{1,0:T(8,128)(2,1)S(1)} %copy-done.2, bf16[4096,512]{1,0:T(8,128)(2,1)} %collective-permute-done.other, f32[4,4096]{1,0:T(4,128)S(1)} %forward.5.rest_0_.rest_3_, ...), custom_call_target="tpu_custom_call" | custom-call | flops 4294967296 | bytes 6291456 | tf_op jit(solution)/shard_map/forward/pallas_call | solution.py:109
  56.2 12.6 %collective-permute-done.3.rest_1_ = bf16[4,64,1024]{2,1,0:T(8,128)(2,1)S(1)} collective-permute-done((bf16[4,64,1024]{2,1,0:T(8,128)(2,1)S(1)}, bf16[4,64,1024]{2,1,0:T(8,128)(2,1)S(1)}, u32[]{:S(2)}, u32[]{:S(2)}) %collective-permute-start.3) | collective-permute-done | bytes 524320 | tf_op jit(solution)/shard_map/ppermute | solution.py:165
  68.7 4.5 %forward.7.rest_0_ = f32[8,4096]{1,0:T(8,128)S(1)} custom-call(s32[1]{0:T(128)} %bitcast.side, s32[4,4096]{1,0:T(4,128)S(1)} %get-tuple-element.45.code, bf16[4096,512]{1,0:T(8,128)(2,1)S(1)} %copy-done.2, bf16[4096,512]{1,0:T(8,128)(2,1)} %collective-permute-done.other, f32[4,4096]{1,0:T(4,128)S(1)} %forward.6.rest_0_.rest_3_, ...), custom_call_target="tpu_custom_call" | custom-call | flops 2147483648 | bytes 6291456 | tf_op jit(solution)/shard_map/forward/pallas_call | solution.py:109
  73.3 1.5 collective-permute-start.5
  74.8 3.5 %collective-permute-done.5 = f32[8,4096]{1,0:T(8,128)S(1)} collective-permute-done((f32[8,4096]{1,0:T(8,128)S(1)}, f32[8,4096]{1,0:T(8,128)S(1)}, u32[]{:S(2)}, u32[]{:S(2)}) %collective-permute-start.5) | collective-permute-done | bytes 131104 | tf_op jit(solution)/shard_map/ppermute | solution.py:165
  78.3 1.6 collective-permute-start.6
  79.9 3.5 %collective-permute-done.6 = f32[8,4096]{1,0:T(8,128)S(1)} collective-permute-done((f32[8,4096]{1,0:T(8,128)S(1)}, f32[8,4096]{1,0:T(8,128)S(1)}, u32[]{:S(2)}, u32[]{:S(2)}) %collective-permute-start.6) | collective-permute-done | bytes 131104 | tf_op jit(solution)/shard_map/ppermute | solution.py:165
  83.4 4.9 %backward.7.rest_3_ = f32[4,64,1024]{2,1,0:T(8,128)S(1)} custom-call(s32[1]{0:T(128)} %bitcast.side, s32[4,4096]{1,0:T(4,128)S(1)} %get-tuple-element.45.code, bf16[4096,512]{1,0:T(8,128)(2,1)S(1)} %copy-done.2, bf16[4096,512]{1,0:T(8,128)(2,1)} %collective-permute-done.other, f32[8,4096]{1,0:T(8,128)S(1)} %add.66.logits.joined, ...), custom_call_target="tpu_custom_call" | custom-call | flops 2147483648 | bytes 6291456 | tf_op jit(solution)/shard_map/backward/pallas_call | solution.py:135
  88.5 0.1 collective-permute-start.11
  88.5 2.0 %collective-permute-start.9 = (bf16[4,64,1024]{2,1,0:T(8,128)(2,1)S(1)}, bf16[4,64,1024]{2,1,0:T(8,128)(2,1)S(1)}, u32[]{:S(2)}, u32[]{:S(2)}) collective-permute-start(bf16[4,64,1024]{2,1,0:T(8,128)(2,1)S(1)} %collective-permute-done.7.rest_1_), channel_id=1, source_target_pairs={{0,1},{1,0},{2,3},{3,2},{4,5},{5,4},{6,7},{7,6},{8,9},{9,8},{10,11... | collective-permute-start | bytes 1572872 | tf_op jit(solution)/shard_map/ppermute | solution.py:165
  90.5 8.9 %forward.8.rest_0_ = f32[4,4096]{1,0:T(4,128)S(1)} custom-call(s32[1]{0:T(128)} %bitcast.side, s32[4,4096]{1,0:T(4,128)S(1)} %get-tuple-element.46.code, bf16[4096,512]{1,0:T(8,128)(2,1)S(1)} %copy-done.3, bf16[4096,512]{1,0:T(8,128)(2,1)} %collective-permute-done.other, bf16[4,64,1024]{2,1,0:T(8,128)(2,1)S(1)} %all-to-all-done.1.rest_0_, ...), custom_call_target="tpu_custom_call" | custom-call | flops 6442450944 | bytes 6291456 | tf_op jit(solution)/shard_map/forward/pallas_call | solution.py:109
  99.5 8.0 %backward.8 = (f32[4,64,1024]{2,1,0:T(8,128)S(1)}, f32[4,64,1024]{2,1,0:T(8,128)S(1)}) custom-call(s32[1]{0:T(128)} %bitcast.side, s32[4,4096]{1,0:T(4,128)S(1)} %get-tuple-element.45.code, bf16[4096,512]{1,0:T(8,128)(2,1)S(1)} %copy-done.3, bf16[4096,512]{1,0:T(8,128)(2,1)} %collective-permute-done.other, f32[8,4096]{1,0:T(8,128)S(1)} %add.66.logits.joined, ...), custom_call_target="tpu_custom_call" | custom-call | flops 4294967296 | bytes 6291456 | tf_op jit(solution)/shard_map/backward/pallas_call | solution.py:135
  107.5 4.5 %forward.9.rest_0_ = f32[4,4096]{1,0:T(4,128)S(1)} custom-call(s32[1]{0:T(128)} %bitcast.side, s32[4,4096]{1,0:T(4,128)S(1)} %get-tuple-element.46.code, bf16[4096,512]{1,0:T(8,128)(2,1)S(1)} %copy-done.3, bf16[4096,512]{1,0:T(8,128)(2,1)} %collective-permute-done.other, f32[4,4096]{1,0:T(4,128)S(1)} %forward.8.rest_0_, ...), custom_call_target="tpu_custom_call" | custom-call | flops 2147483648 | bytes 6291456 | tf_op jit(solution)/shard_map/forward/pallas_call | solution.py:109
  112.0 1.5 collective-permute-start.10
  113.6 0.1 collective-permute-start.13
  113.8 2.6 %collective-permute-done.10 = f32[4,4096]{1,0:T(4,128)S(1)} collective-permute-done((f32[4,4096]{1,0:T(4,128)S(1)}, f32[4,4096]{1,0:T(4,128)S(1)}, u32[]{:S(2)}, u32[]{:S(2)}) %collective-permute-start.10) | collective-permute-done | bytes 65568 | tf_op jit(solution)/shard_map/ppermute | solution.py:165
  116.4 1.6 collective-permute-start.12
  118.0 0.1 add_convert_fusion.3
  118.1 1.7 collective-permute-start.14
  119.8 1.0 collective-permute-done.12
  120.8 4.8 %backward.9.rest_0_ = f32[4,64,1024]{2,1,0:T(8,128)S(1)} custom-call(s32[1]{0:T(128)} %bitcast.side, s32[4,4096]{1,0:T(4,128)S(1)} %get-tuple-element.46.code, bf16[4096,512]{1,0:T(8,128)(2,1)S(1)} %copy-done.3, bf16[4096,512]{1,0:T(8,128)(2,1)} %collective-permute-done.other, f32[4,4096]{1,0:T(4,128)S(1)} %add.68.logits, f32[8,4096]{1,0:T(8,128)S(1)} %add.66.logits.joined, ...), custom_call_target="tpu_custom_call" | custom-call | flops 2147483648 | bytes 6291456 | tf_op jit(solution)/shard_map/backward/pallas_call | solution.py:135
  125.5 0.1 convert_element_type.52
  125.6 0.8 collective-permute-start.16
  126.4 8.8 %collective-permute-done.13.rest_1_ = bf16[4,64,1024]{2,1,0:T(8,128)(2,1)S(1)} collective-permute-done((bf16[4,64,1024]{2,1,0:T(8,128)(2,1)S(1)}, bf16[4,64,1024]{2,1,0:T(8,128)(2,1)S(1)}, u32[]{:S(2)}, u32[]{:S(2)}) %collective-permute-start.13) | collective-permute-done | bytes 524320 | tf_op jit(solution)/shard_map/ppermute | solution.py:165
  135.2 4.7 %backward.10.rest_0_ = f32[4,64,1024]{2,1,0:T(8,128)S(1)} custom-call(s32[1]{0:T(128)} %bitcast.side, s32[4,4096]{1,0:T(4,128)S(1)} %get-tuple-element.46.code, bf16[4096,512]{1,0:T(8,128)(2,1)S(1)} %copy-done.3, bf16[4096,512]{1,0:T(8,128)(2,1)} %collective-permute-done.other, f32[4,4096]{1,0:T(4,128)S(1)} %add.68.logits, f32[8,4096]{1,0:T(8,128)S(1)} %add.66.logits.joined, ...), custom_call_target="tpu_custom_call" | custom-call | flops 2147483648 | bytes 6291456 | tf_op jit(solution)/shard_map/backward/pallas_call | solution.py:135
  140.0 4.8 %backward.11.rest_0_ = f32[4,64,1024]{2,1,0:T(8,128)S(1)} custom-call(s32[1]{0:T(128)} %bitcast.side, s32[4,4096]{1,0:T(4,128)S(1)} %get-tuple-element.46.code, bf16[4096,512]{1,0:T(8,128)(2,1)S(1)} %copy-done.3, bf16[4096,512]{1,0:T(8,128)(2,1)} %collective-permute-done.other, f32[4,4096]{1,0:T(4,128)S(1)} %add.68.logits, f32[8,4096]{1,0:T(8,128)S(1)} %add.66.logits.joined, ...), custom_call_target="tpu_custom_call" | custom-call | flops 2147483648 | bytes 6291456 | tf_op jit(solution)/shard_map/backward/pallas_call | solution.py:135
  144.8 1.4 collective-permute-start.15
  146.3 5.8 %collective-permute-done.16 = bf16[4,64,1024]{2,1,0:T(8,128)(2,1)S(1)} collective-permute-done((bf16[4,64,1024]{2,1,0:T(8,128)(2,1)S(1)}, bf16[4,64,1024]{2,1,0:T(8,128)(2,1)S(1)}, u32[]{:S(2)}, u32[]{:S(2)}) %collective-permute-start.16) | collective-permute-done | bytes 524320 | tf_op jit(solution)/shard_map/ppermute | solution.py:165
  152.1 0.9 add_convert_fusion.1
  153.0 1.3 collective-permute-start.17
  154.4 4.8 %backward.12.rest_0_ = f32[4,64,1024]{2,1,0:T(8,128)S(1)} custom-call(s32[1]{0:T(128)} %bitcast.side, s32[4,4096]{1,0:T(4,128)S(1)} %get-tuple-element.45.code, bf16[4096,512]{1,0:T(8,128)(2,1)S(1)} %copy-done.3, bf16[4096,512]{1,0:T(8,128)(2,1)} %collective-permute-done.other, f32[8,4096]{1,0:T(8,128)S(1)} %add.66.logits.joined, ...), custom_call_target="tpu_custom_call" | custom-call | flops 2147483648 | bytes 6291456 | tf_op jit(solution)/shard_map/backward/pallas_call | solution.py:135
  159.2 1.1 add_convert_fusion.2
  160.2 3.5 %all-to-all-start.2 = ((bf16[4,64,1024]{2,1,0:T(8,128)(2,1)}), bf16[4,64,1024]{2,1,0:T(8,128)(2,1)S(1)}, u32[]{:S(2)}, u32[]{:S(2)}) async-start(bf16[4,64,1024]{2,1,0:T(8,128)(2,1)} %add_convert_fusion.2), calls=%async_computation.2 | async-start | bytes 1048576 | tf_op jit(solution)/shard_map/all_to_all | solution.py:186
  163.7 2.2 %copy-done.4 = bf16[4096,512]{1,0:T(8,128)(2,1)S(1)} copy-done((bf16[4096,512]{1,0:T(8,128)(2,1)S(1)}, bf16[4096,512]{1,0:T(8,128)(2,1)}, u32[]{:S(2)}) %copy-start.4) | copy-done | bytes 4194328
  165.9 4.7 %backward.13 = f32[4,64,1024]{2,1,0:T(8,128)S(1)} custom-call(s32[1]{0:T(128)} %bitcast.side, s32[4,4096]{1,0:T(4,128)S(1)} %get-tuple-element.46.code, bf16[4096,512]{1,0:T(8,128)(2,1)S(1)} %copy-done.4, bf16[4096,512]{1,0:T(8,128)(2,1)} %collective-permute-done.other, f32[4,4096]{1,0:T(4,128)S(1)} %add.68.logits, f32[8,4096]{1,0:T(8,128)S(1)} %add.66.logits.joined, ...), custom_call_target="tpu_custom_call" | custom-call | flops 2147483648 | bytes 6291456 | tf_op jit(solution)/shard_map/backward/pallas_call | solution.py:135
  170.7 2.1 %add_convert_fusion = bf16[4,64,1024]{2,1,0:T(8,128)(2,1)} fusion(bf16[4,64,1024]{2,1,0:T(8,128)(2,1)} %collective-permute-done.17, f32[4,64,1024]{2,1,0:T(8,128)S(1)} %backward.13, bf16[4,64,1024]{2,1,0:T(8,128)(2,1)S(1)} %collective-permute-done.15), kind=kLoop, calls=%fused_computation.1 | loop fusion | flops 1310720 | bytes 2621440 | tf_op jit(solution)/shard_map/convert_element_type | solution.py:330
  172.7 4.2 %all-to-all-start.3 = ((bf16[4,64,1024]{2,1,0:T(8,128)(2,1)}), bf16[4,64,1024]{2,1,0:T(8,128)(2,1)S(1)}, u32[]{:S(2)}, u32[]{:S(2)}) async-start(bf16[4,64,1024]{2,1,0:T(8,128)(2,1)} %add_convert_fusion), calls=%async_computation.3 | async-start | bytes 1048576 | tf_op jit(solution)/shard_map/all_to_all | solution.py:186
  176.9 6.5 %all-to-all-done.3 = bf16[4,64,1024]{2,1,0:T(8,128)(2,1)S(1)} async-done(((bf16[4,64,1024]{2,1,0:T(8,128)(2,1)}), bf16[4,64,1024]{2,1,0:T(8,128)(2,1)S(1)}, u32[]{:S(2)}, u32[]{:S(2)}) %all-to-all-start.3) | async-done | bytes 524320 | tf_op jit(solution)/shard_map/all_to_all | solution.py:186
  183.5 1.1 pad_maximum_fusion
  (38 shorter events, 0.6 us)
Async XLA Ops:
  0.0 16.0 %copy-start = (s32[8,16384]{1,0:T(8,128)S(1)}, s32[8,16384]{1,0:T(8,128)}, u32[]{:S(2)}) copy-start(s32[8,16384]{1,0:T(8,128)} %param.10) | copy-start | bytes 1572868
  0.0 7.4 %copy-start.7 = (s32[8]{0:T(128)S(1)}, s32[8]{0:T(128)}, u32[]{:S(2)}) copy-start(s32[8]{0:T(128)} %param.11) | copy-start | bytes 100
  0.0 21.7 %collective-permute-start = (bf16[4096,512]{1,0:T(8,128)(2,1)}, bf16[4096,512]{1,0:T(8,128)(2,1)}, u32[]{:S(2)}, u32[]{:S(2)}) collective-permute-start(bf16[4096,512]{1,0:T(8,128)(2,1)} %mine.11), channel_id=1, source_target_pairs={{0,4},{4,0},{8,12},{12,8},{16,20},{20,16},{24,28},{28,24},{1,5},{5... | collective-permute-start | bytes 12582920 | tf_op jit(solution)/shard_map/ppermute | solution.py:165
  1.7 14.4 %copy-start.6 = (bf16[4,8]{1,0:T(4,128)(2,1)S(1)}, bf16[4,8]{1,0:T(4,128)(2,1)}, u32[]{:S(2)}) copy-start(bf16[4,8]{1,0:T(4,128)(2,1)} %param.13) | copy-start | bytes 196
  2.6 13.4 %all-to-all-start = ((bf16[4,64,1024]{2,1,0:T(8,128)(2,1)}), bf16[4,64,1024]{2,1,0:T(8,128)(2,1)S(1)}, u32[]{:S(2)}, u32[]{:S(2)}) async-start(bf16[4,64,1024]{2,1,0:T(8,128)(2,1)} %bitcast.72), calls=%async_computation | async-start | bytes 1048576 | tf_op jit(solution)/shard_map/all_to_all | solution.py:186
  17.2 24.3 %collective-permute-start.2 = (bf16[4,64,1024]{2,1,0:T(8,128)(2,1)S(1)}, bf16[4,64,1024]{2,1,0:T(8,128)(2,1)S(1)}, u32[]{:S(2)}, u32[]{:S(2)}) collective-permute-start(bf16[4,64,1024]{2,1,0:T(8,128)(2,1)S(1)} %all-to-all-done.rest_0_), channel_id=1, source_target_pairs={{0,1},{1,0},{2,3},{3,2},{4,5},{5,4},{6,7},{7,6},{8,9},{9,8},{10,11... | collective-permute-start | bytes 1572872 | tf_op jit(solution)/shard_map/ppermute | solution.py:165
  18.8 25.2 %collective-permute-start.1 = (bf16[4,64,1024]{2,1,0:T(8,128)(2,1)S(1)}, bf16[4,64,1024]{2,1,0:T(8,128)(2,1)S(1)}, u32[]{:S(2)}, u32[]{:S(2)}) collective-permute-start(bf16[4,64,1024]{2,1,0:T(8,128)(2,1)S(1)} %all-to-all-done.rest_0_), channel_id=1, source_target_pairs={{0,2},{1,3},{2,0},{3,1},{4,6},{5,7},{6,4},{7,5},{8,10},{9,11},{10,... | collective-permute-start | bytes 1572872 | tf_op jit(solution)/shard_map/ppermute | solution.py:165
  21.7 2.2 %copy-start.1 = (bf16[4096,512]{1,0:T(8,128)(2,1)S(1)}, bf16[4096,512]{1,0:T(8,128)(2,1)}, u32[]{:S(2)}) copy-start(bf16[4096,512]{1,0:T(8,128)(2,1)} %mine.11) | copy-start | bytes 12582916
  28.5 15.5 %all-to-all-start.1 = ((bf16[4,64,1024]{2,1,0:T(8,128)(2,1)}), bf16[4,64,1024]{2,1,0:T(8,128)(2,1)S(1)}, u32[]{:S(2)}, u32[]{:S(2)}) async-start(bf16[4,64,1024]{2,1,0:T(8,128)(2,1)} %bitcast.70), calls=%async_computation.1 | async-start | bytes 1048576 | tf_op jit(solution)/shard_map/all_to_all | solution.py:186
  32.2 12.1 %collective-permute-start.4 = (f32[4,1,4096]{2,0,1:T(4,128)S(1)}, f32[4,1,4096]{2,0,1:T(4,128)S(1)}, u32[]{:S(2)}, u32[]{:S(2)}) collective-permute-start(f32[4,1,4096]{2,0,1:T(4,128)S(1)} %bitcast.87), channel_id=1, source_target_pairs={{0,4},{4,0},{8,12},{12,8},{16,20},{20,16},{24,28},{28,24},{1,5},{5... | collective-permute-start | bytes 196616 | tf_op jit(solution)/shard_map/ppermute | solution.py:165
  44.0 24.7 %collective-permute-start.3 = (bf16[4,64,1024]{2,1,0:T(8,128)(2,1)S(1)}, bf16[4,64,1024]{2,1,0:T(8,128)(2,1)S(1)}, u32[]{:S(2)}, u32[]{:S(2)}) collective-permute-start(bf16[4,64,1024]{2,1,0:T(8,128)(2,1)S(1)} %collective-permute-done.1.rest_1_), channel_id=1, source_target_pairs={{0,1},{1,0},{2,3},{3,2},{4,5},{5,4},{6,7},{7,6},{8,9},{9,8},{10,11... | collective-permute-start | bytes 1572872 | tf_op jit(solution)/shard_map/ppermute | solution.py:165
  44.4 44.0 %collective-permute-start.8 = (bf16[4,64,1024]{2,1,0:T(8,128)(2,1)S(1)}, bf16[4,64,1024]{2,1,0:T(8,128)(2,1)S(1)}, u32[]{:S(2)}, u32[]{:S(2)}) collective-permute-start(bf16[4,64,1024]{2,1,0:T(8,128)(2,1)S(1)} %all-to-all-done.1.rest_0_), channel_id=1, source_target_pairs={{0,1},{1,0},{2,3},{3,2},{4,5},{5,4},{6,7},{7,6},{8,9},{9,8},{10,11... | collective-permute-start | bytes 1572872 | tf_op jit(solution)/shard_map/ppermute | solution.py:165
  46.1 42.3 %collective-permute-start.7 = (bf16[4,64,1024]{2,1,0:T(8,128)(2,1)S(1)}, bf16[4,64,1024]{2,1,0:T(8,128)(2,1)S(1)}, u32[]{:S(2)}, u32[]{:S(2)}) collective-permute-start(bf16[4,64,1024]{2,1,0:T(8,128)(2,1)S(1)} %all-to-all-done.1.rest_0_), channel_id=1, source_target_pairs={{0,2},{1,3},{2,0},{3,1},{4,6},{5,7},{6,4},{7,5},{8,10},{9,11},{10,... | collective-permute-start | bytes 1572872 | tf_op jit(solution)/shard_map/ppermute | solution.py:165
  47.2 2.2 %copy-start.2 = (bf16[4096,512]{1,0:T(8,128)(2,1)S(1)}, bf16[4096,512]{1,0:T(8,128)(2,1)}, u32[]{:S(2)}) copy-start(bf16[4096,512]{1,0:T(8,128)(2,1)} %mine.11) | copy-start | bytes 12582916
  56.2 23.7 %copy-start.5 = (bf16[4096]{0:T(1024)(128)(2,1)S(1)}, bf16[4096]{0:T(1024)(128)(2,1)}, u32[]{:S(2)}) copy-start(bf16[4096]{0:T(1024)(128)(2,1)} %param.9) | copy-start | bytes 24580
  73.3 5.0 %collective-permute-start.5 = (f32[8,4096]{1,0:T(8,128)S(1)}, f32[8,4096]{1,0:T(8,128)S(1)}, u32[]{:S(2)}, u32[]{:S(2)}) collective-permute-start(f32[8,4096]{1,0:T(8,128)S(1)} %forward.7.rest_0_), channel_id=1, source_target_pairs={{0,8},{4,12},{8,0},{12,4},{16,24},{20,28},{24,16},{28,20},{1,9},{5... | collective-permute-start | bytes 393224 | tf_op jit(solution)/shard_map/ppermute | solution.py:165
  78.3 5.0 %collective-permute-start.6 = (f32[8,4096]{1,0:T(8,128)S(1)}, f32[8,4096]{1,0:T(8,128)S(1)}, u32[]{:S(2)}, u32[]{:S(2)}) collective-permute-start(f32[8,4096]{1,0:T(8,128)S(1)} %add.65), channel_id=1, source_target_pairs={{0,16},{4,20},{8,24},{12,28},{16,0},{20,4},{24,8},{28,12},{1,17},{... | collective-permute-start | bytes 393224 | tf_op jit(solution)/shard_map/ppermute | solution.py:165
  83.4 7.2 %copy-start.3 = (bf16[4096,512]{1,0:T(8,128)(2,1)S(1)}, bf16[4096,512]{1,0:T(8,128)(2,1)}, u32[]{:S(2)}) copy-start(bf16[4096,512]{1,0:T(8,128)(2,1)} %mine.11) | copy-start | bytes 12582916
  88.5 27.9 %collective-permute-start.11 = (bf16[4,64,1024]{2,1,0:T(8,128)(2,1)S(1)}, bf16[4,64,1024]{2,1,0:T(8,128)(2,1)S(1)}, u32[]{:S(2)}, u32[]{:S(2)}) collective-permute-start(bf16[4,64,1024]{2,1,0:T(8,128)(2,1)S(1)} %convert_element_type.43), channel_id=1, source_target_pairs={{0,1},{1,0},{2,3},{3,2},{4,5},{5,4},{6,7},{7,6},{8,9},{9,8},{10,11... | collective-permute-start | bytes 1572872 | tf_op jit(solution)/shard_map/ppermute | solution.py:165
  88.5 18.9 %collective-permute-start.9 = (bf16[4,64,1024]{2,1,0:T(8,128)(2,1)S(1)}, bf16[4,64,1024]{2,1,0:T(8,128)(2,1)S(1)}, u32[]{:S(2)}, u32[]{:S(2)}) collective-permute-start(bf16[4,64,1024]{2,1,0:T(8,128)(2,1)S(1)} %collective-permute-done.7.rest_1_), channel_id=1, source_target_pairs={{0,1},{1,0},{2,3},{3,2},{4,5},{5,4},{6,7},{7,6},{8,9},{9,8},{10,11... | collective-permute-start | bytes 1572872 | tf_op jit(solution)/shard_map/ppermute | solution.py:165
  112.0 4.3 %collective-permute-start.10 = (f32[4,4096]{1,0:T(4,128)S(1)}, f32[4,4096]{1,0:T(4,128)S(1)}, u32[]{:S(2)}, u32[]{:S(2)}) collective-permute-start(f32[4,4096]{1,0:T(4,128)S(1)} %forward.9.rest_0_), channel_id=1, source_target_pairs={{0,8},{4,12},{8,0},{12,4},{16,24},{20,28},{24,16},{28,20},{1,9},{5... | collective-permute-start | bytes 196616 | tf_op jit(solution)/shard_map/ppermute | solution.py:165
  113.6 21.6 %collective-permute-start.13 = (bf16[4,64,1024]{2,1,0:T(8,128)(2,1)S(1)}, bf16[4,64,1024]{2,1,0:T(8,128)(2,1)S(1)}, u32[]{:S(2)}, u32[]{:S(2)}) collective-permute-start(bf16[4,64,1024]{2,1,0:T(8,128)(2,1)S(1)} %convert_element_type.44), channel_id=1, source_target_pairs={{0,1},{1,0},{2,3},{3,2},{4,5},{5,4},{6,7},{7,6},{8,9},{9,8},{10,11... | collective-permute-start | bytes 1572872 | tf_op jit(solution)/shard_map/ppermute | solution.py:165
  116.4 4.3 %collective-permute-start.12 = (f32[4,4096]{1,0:T(4,128)S(1)}, f32[4,4096]{1,0:T(4,128)S(1)}, u32[]{:S(2)}, u32[]{:S(2)}) collective-permute-start(f32[4,4096]{1,0:T(4,128)S(1)} %add.67), channel_id=1, source_target_pairs={{0,16},{4,20},{8,24},{12,28},{16,0},{20,4},{24,8},{28,12},{1,17},{... | collective-permute-start | bytes 196616 | tf_op jit(solution)/shard_map/ppermute | solution.py:165
  118.1 21.9 %collective-permute-start.14 = (bf16[4,64,1024]{2,1,0:T(8,128)(2,1)S(1)}, bf16[4,64,1024]{2,1,0:T(8,128)(2,1)S(1)}, u32[]{:S(2)}, u32[]{:S(2)}) collective-permute-start(bf16[4,64,1024]{2,1,0:T(8,128)(2,1)S(1)} %add_convert_fusion.3), channel_id=1, source_target_pairs={{0,2},{1,3},{2,0},{3,1},{4,6},{5,7},{6,4},{7,5},{8,10},{9,11},{10,... | collective-permute-start | bytes 1572872 | tf_op jit(solution)/shard_map/ppermute | solution.py:165
  125.6 26.5 %collective-permute-start.16 = (bf16[4,64,1024]{2,1,0:T(8,128)(2,1)S(1)}, bf16[4,64,1024]{2,1,0:T(8,128)(2,1)S(1)}, u32[]{:S(2)}, u32[]{:S(2)}) collective-permute-start(bf16[4,64,1024]{2,1,0:T(8,128)(2,1)S(1)} %convert_element_type.52), channel_id=1, source_target_pairs={{0,1},{1,0},{2,3},{3,2},{4,5},{5,4},{6,7},{7,6},{8,9},{9,8},{10,11... | collective-permute-start | bytes 1572872 | tf_op jit(solution)/shard_map/ppermute | solution.py:165
  144.8 25.8 %collective-permute-start.15 = (bf16[4,64,1024]{2,1,0:T(8,128)(2,1)S(1)}, bf16[4,64,1024]{2,1,0:T(8,128)(2,1)S(1)}, u32[]{:S(2)}, u32[]{:S(2)}) collective-permute-start(bf16[4,64,1024]{2,1,0:T(8,128)(2,1)S(1)} %convert_element_type.50), channel_id=1, source_target_pairs={{0,1},{1,0},{2,3},{3,2},{4,5},{5,4},{6,7},{7,6},{8,9},{9,8},{10,11... | collective-permute-start | bytes 1572872 | tf_op jit(solution)/shard_map/ppermute | solution.py:165
  153.0 17.6 %collective-permute-start.17 = (bf16[4,64,1024]{2,1,0:T(8,128)(2,1)}, bf16[4,64,1024]{2,1,0:T(8,128)(2,1)}, u32[]{:S(2)}, u32[]{:S(2)}) collective-permute-start(bf16[4,64,1024]{2,1,0:T(8,128)(2,1)} %add_convert_fusion.1), channel_id=1, source_target_pairs={{0,2},{1,3},{2,0},{3,1},{4,6},{5,7},{6,4},{7,5},{8,10},{9,11},{10,... | collective-permute-start | bytes 1572872 | tf_op jit(solution)/shard_map/ppermute | solution.py:165
  160.2 12.5 %all-to-all-start.2 = ((bf16[4,64,1024]{2,1,0:T(8,128)(2,1)}), bf16[4,64,1024]{2,1,0:T(8,128)(2,1)S(1)}, u32[]{:S(2)}, u32[]{:S(2)}) async-start(bf16[4,64,1024]{2,1,0:T(8,128)(2,1)} %add_convert_fusion.2), calls=%async_computation.2 | async-start | bytes 1048576 | tf_op jit(solution)/shard_map/all_to_all | solution.py:186
  163.7 2.2 %copy-start.4 = (bf16[4096,512]{1,0:T(8,128)(2,1)S(1)}, bf16[4096,512]{1,0:T(8,128)(2,1)}, u32[]{:S(2)}) copy-start(bf16[4096,512]{1,0:T(8,128)(2,1)} %mine.11) | copy-start | bytes 12582916
  172.7 10.7 %all-to-all-start.3 = ((bf16[4,64,1024]{2,1,0:T(8,128)(2,1)}), bf16[4,64,1024]{2,1,0:T(8,128)(2,1)S(1)}, u32[]{:S(2)}, u32[]{:S(2)}) async-start(bf16[4,64,1024]{2,1,0:T(8,128)(2,1)} %add_convert_fusion), calls=%async_computation.3 | async-start | bytes 1048576 | tf_op jit(solution)/shard_map/all_to_all | solution.py:186

commit v5 on v4

--- a/solution.py
+++ b/solution.py
@@ -310,7 +310,7 @@
         run_backward(c - 1, far)
         reduce_far(c - 1)
         if more:
-            arrived = tie(*[held[c][slot] for slot in near])
+            arrived = together(*[held[c][slot] for slot in near])
             held[c].update(zip(near, arrived))
             gather_far(c)
             run_forward(c, (0,) + near)

time: 185 us -> 183 us (0.989)
  waiting for transfers between devices: 63.6 us -> 59.7 us
    ppermute x18, waiting for transfers between devices: 49.5 us -> 45.6 us  [exchange(): lax.ppermute(value, axis, [(i, i ^ bit) for i in range(lax.axis_size(axis...]
    ppermute x18, starting transfers between devices: 21.5 us -> 23.9 us  [exchange(): lax.ppermute(value, axis, [(i, i ^ bit) for i in range(lax.axis_size(axis...]
  transfers between devices with their start and end apart: 22 -> 22, of which waited for: 11 -> 12; matrix products, arithmetic and copies ran while one was open for 5% -> 5% of each run, Pallas kernels for 36% -> 36%
where the time goes in v5:
time: 183 us
  Pallas kernels  66.1 us (36%)
  waiting for transfers between devices  59.7 us (33%)
  starting transfers between devices  39.2 us (21%)
  local copies, waits for them, and re-layouts  10.3 us (6%)
  other arithmetic  5.9 us (3%)
    ppermute x18, waiting for transfers between devices, exchange(): lax.ppermute(value, axis, [(i, i ^ bit) for i in range(lax.axis_size(axis...  45.6 us
    pallas_call x7, Pallas kernels, backward(): pl.pallas_call(functools.partial(backward_kernel, slots, len(waits)), out...  36.7 us
    pallas_call x5, Pallas kernels, forward(): pl.pallas_call(functools.partial(forward_kernel, slots, len(before), len(...  29.4 us
    ppermute x18, starting transfers between devices, exchange(): lax.ppermute(value, axis, [(i, i ^ bit) for i in range(lax.axis_size(axis...  23.9 us
    all_to_all x4, starting transfers between devices, swap(): lax.all_to_all(x, 'dp', split_axis=0, concat_axis=0, axis_index_groups=gr...  15.3 us
    all_to_all x4, waiting for transfers between devices, swap(): lax.all_to_all(x, 'dp', split_axis=0, concat_axis=0, axis_index_groups=gr...  14.1 us
    unnamed x17, local copies, waits for them, and re-layouts  6.63 us
  transfers between devices with their start and end apart: 22, of which 12 were waited for; matrix products, arithmetic and copies ran while one was open for 5% of the time, Pallas kernels for 36%

profile of v5, /device:TPU:0, one launch (start us, length us, event | category | flops | bytes accessed | tf_op | source)
XLA Modules:
  0.0 182.6 jit_solution(1907919764633511650)
XLA Ops:
  0.0 0.5 collective-permute-start
  0.5 1.3 fusion.9
  1.7 0.9 copy.47
  2.6 4.8 %all-to-all-start = ((bf16[4,64,1024]{2,1,0:T(8,128)(2,1)}), bf16[4,64,1024]{2,1,0:T(8,128)(2,1)S(1)}, u32[]{:S(2)}, u32[]{:S(2)}) async-start(bf16[4,64,1024]{2,1,0:T(8,128)(2,1)} %bitcast.72), calls=%async_computation | async-start | bytes 1048576 | tf_op jit(solution)/shard_map/all_to_all | solution.py:186
  7.4 0.1 reshape.49
  7.5 0.8 copy.46
  8.3 0.2 dynamic-slice_reduce_fusion
  8.5 7.5 %all-to-all-done.rest_0_ = bf16[4,64,1024]{2,1,0:T(8,128)(2,1)S(1)} async-done(((bf16[4,64,1024]{2,1,0:T(8,128)(2,1)}), bf16[4,64,1024]{2,1,0:T(8,128)(2,1)S(1)}, u32[]{:S(2)}, u32[]{:S(2)}) %all-to-all-start) | async-done | bytes 524320 | tf_op jit(solution)/shard_map/all_to_all | solution.py:186
  16.0 0.1 reshape.47
  16.1 1.0 fusion.6
  17.1 0.1 reshape.52
  17.2 1.6 collective-permute-start.2
  18.8 2.6 %collective-permute-start.1 = (bf16[4,64,1024]{2,1,0:T(8,128)(2,1)S(1)}, bf16[4,64,1024]{2,1,0:T(8,128)(2,1)S(1)}, u32[]{:S(2)}, u32[]{:S(2)}) collective-permute-start(bf16[4,64,1024]{2,1,0:T(8,128)(2,1)S(1)} %all-to-all-done.rest_0_), channel_id=1, source_target_pairs={{0,2},{1,3},{2,0},{3,1},{4,6},{5,7},{6,4},{7,5},{8,10},{9,11},{10,... | collective-permute-start | bytes 1572872 | tf_op jit(solution)/shard_map/ppermute | solution.py:165
  21.5 0.2 and_select_fusion
  21.7 2.2 %copy-done.1 = bf16[4096,512]{1,0:T(8,128)(2,1)S(1)} copy-done((bf16[4096,512]{1,0:T(8,128)(2,1)S(1)}, bf16[4096,512]{1,0:T(8,128)(2,1)}, u32[]{:S(2)}) %copy-start.1) | copy-done | bytes 4194328
  23.9 4.6 %forward.5.rest_0_.rest_3_ = f32[4,4096]{1,0:T(4,128)S(1)} custom-call(s32[1]{0:T(128)} %bitcast.side, s32[4,4096]{1,0:T(4,128)S(1)} %get-tuple-element.43.code, bf16[4096,512]{1,0:T(8,128)(2,1)S(1)} %copy-done.1, bf16[4096,512]{1,0:T(8,128)(2,1)} %collective-permute-done.other, bf16[4,64,1024]{2,1,0:T(8,128)(2,1)S(1)} %all-to-all-done.rest_0_), custom_call_target="tpu_custom_call" | custom-call | flops 2147483648 | bytes 6291456 | tf_op jit(solution)/shard_map/forward/pallas_call | solution.py:109
  28.5 3.5 %all-to-all-start.1 = ((bf16[4,64,1024]{2,1,0:T(8,128)(2,1)}), bf16[4,64,1024]{2,1,0:T(8,128)(2,1)S(1)}, u32[]{:S(2)}, u32[]{:S(2)}) async-start(bf16[4,64,1024]{2,1,0:T(8,128)(2,1)} %bitcast.70), calls=%async_computation.1 | async-start | bytes 1048576 | tf_op jit(solution)/shard_map/all_to_all | solution.py:186
  32.0 0.1 constant_dynamic-slice_fusion.1
  32.2 0.1 collective-permute-start.4
  32.3 9.2 %collective-permute-done.2.rest_2_ = bf16[4,64,1024]{2,1,0:T(8,128)(2,1)S(1)} collective-permute-done((bf16[4,64,1024]{2,1,0:T(8,128)(2,1)S(1)}, bf16[4,64,1024]{2,1,0:T(8,128)(2,1)S(1)}, u32[]{:S(2)}, u32[]{:S(2)}) %collective-permute-start.2) | collective-permute-done | bytes 524320 | tf_op jit(solution)/shard_map/ppermute | solution.py:165
  41.5 2.5 %collective-permute-done.1.rest_1_ = bf16[4,64,1024]{2,1,0:T(8,128)(2,1)S(1)} collective-permute-done((bf16[4,64,1024]{2,1,0:T(8,128)(2,1)S(1)}, bf16[4,64,1024]{2,1,0:T(8,128)(2,1)S(1)}, u32[]{:S(2)}, u32[]{:S(2)}) %collective-permute-start.1) | collective-permute-done | bytes 524320 | tf_op jit(solution)/shard_map/ppermute | solution.py:165
  44.0 0.3 collective-permute-start.3
  44.4 1.8 collective-permute-start.8
  46.1 1.1 collective-permute-start.7
  47.2 2.2 %copy-done.2 = bf16[4096,512]{1,0:T(8,128)(2,1)S(1)} copy-done((bf16[4096,512]{1,0:T(8,128)(2,1)S(1)}, bf16[4096,512]{1,0:T(8,128)(2,1)}, u32[]{:S(2)}) %copy-start.2) | copy-done | bytes 4194328
  49.4 6.7 %forward.6.rest_0_.rest_3_ = f32[4,4096]{1,0:T(4,128)S(1)} custom-call(s32[1]{0:T(128)} %bitcast.side, s32[4,4096]{1,0:T(4,128)S(1)} %get-tuple-element.43.code, bf16[4096,512]{1,0:T(8,128)(2,1)S(1)} %copy-done.2, bf16[4096,512]{1,0:T(8,128)(2,1)} %collective-permute-done.other, f32[4,4096]{1,0:T(4,128)S(1)} %forward.5.rest_0_.rest_3_, ...), custom_call_target="tpu_custom_call" | custom-call | flops 4294967296 | bytes 6291456 | tf_op jit(solution)/shard_map/forward/pallas_call | solution.py:109
  56.2 12.6 %collective-permute-done.3.rest_1_ = bf16[4,64,1024]{2,1,0:T(8,128)(2,1)S(1)} collective-permute-done((bf16[4,64,1024]{2,1,0:T(8,128)(2,1)S(1)}, bf16[4,64,1024]{2,1,0:T(8,128)(2,1)S(1)}, u32[]{:S(2)}, u32[]{:S(2)}) %collective-permute-start.3) | collective-permute-done | bytes 524320 | tf_op jit(solution)/shard_map/ppermute | solution.py:165
  68.7 4.5 %forward.7.rest_0_ = f32[8,4096]{1,0:T(8,128)S(1)} custom-call(s32[1]{0:T(128)} %bitcast.side, s32[4,4096]{1,0:T(4,128)S(1)} %get-tuple-element.43.code, bf16[4096,512]{1,0:T(8,128)(2,1)S(1)} %copy-done.2, bf16[4096,512]{1,0:T(8,128)(2,1)} %collective-permute-done.other, f32[4,4096]{1,0:T(4,128)S(1)} %forward.6.rest_0_.rest_3_, ...), custom_call_target="tpu_custom_call" | custom-call | flops 2147483648 | bytes 6291456 | tf_op jit(solution)/shard_map/forward/pallas_call | solution.py:109
  73.3 1.5 collective-permute-start.5
  74.8 3.5 %collective-permute-done.5 = f32[8,4096]{1,0:T(8,128)S(1)} collective-permute-done((f32[8,4096]{1,0:T(8,128)S(1)}, f32[8,4096]{1,0:T(8,128)S(1)}, u32[]{:S(2)}, u32[]{:S(2)}) %collective-permute-start.5) | collective-permute-done | bytes 131104 | tf_op jit(solution)/shard_map/ppermute | solution.py:165
  78.3 1.6 collective-permute-start.6
  79.9 0.1 collective-permute-start.9
  80.0 3.4 %collective-permute-done.6 = f32[8,4096]{1,0:T(8,128)S(1)} collective-permute-done((f32[8,4096]{1,0:T(8,128)S(1)}, f32[8,4096]{1,0:T(8,128)S(1)}, u32[]{:S(2)}, u32[]{:S(2)}) %collective-permute-start.6) | collective-permute-done | bytes 131104 | tf_op jit(solution)/shard_map/ppermute | solution.py:165
  83.4 4.9 %backward.7.rest_3_ = f32[4,64,1024]{2,1,0:T(8,128)S(1)} custom-call(s32[1]{0:T(128)} %bitcast.side, s32[4,4096]{1,0:T(4,128)S(1)} %get-tuple-element.43.code, bf16[4096,512]{1,0:T(8,128)(2,1)S(1)} %copy-done.2, bf16[4096,512]{1,0:T(8,128)(2,1)} %collective-permute-done.other, f32[8,4096]{1,0:T(8,128)S(1)} %add.66.logits.joined, ...), custom_call_target="tpu_custom_call" | custom-call | flops 2147483648 | bytes 6291456 | tf_op jit(solution)/shard_map/backward/pallas_call | solution.py:135
  88.4 0.1 collective-permute-start.11
  88.5 9.0 %forward.8.rest_0_ = f32[4,4096]{1,0:T(4,128)S(1)} custom-call(s32[1]{0:T(128)} %bitcast.side, s32[4,4096]{1,0:T(4,128)S(1)} %get-tuple-element.44.code, bf16[4096,512]{1,0:T(8,128)(2,1)S(1)} %copy-done.3, bf16[4096,512]{1,0:T(8,128)(2,1)} %collective-permute-done.other, bf16[4,64,1024]{2,1,0:T(8,128)(2,1)S(1)} %all-to-all-done.1.rest_0_, ...), custom_call_target="tpu_custom_call" | custom-call | flops 6442450944 | bytes 6291456 | tf_op jit(solution)/shard_map/forward/pallas_call | solution.py:109
  97.5 8.0 %backward.8 = (f32[4,64,1024]{2,1,0:T(8,128)S(1)}, f32[4,64,1024]{2,1,0:T(8,128)S(1)}) custom-call(s32[1]{0:T(128)} %bitcast.side, s32[4,4096]{1,0:T(4,128)S(1)} %get-tuple-element.43.code, bf16[4096,512]{1,0:T(8,128)(2,1)S(1)} %copy-done.3, bf16[4096,512]{1,0:T(8,128)(2,1)} %collective-permute-done.other, f32[8,4096]{1,0:T(8,128)S(1)} %add.66.logits.joined, ...), custom_call_target="tpu_custom_call" | custom-call | flops 4294967296 | bytes 6291456 | tf_op jit(solution)/shard_map/backward/pallas_call | solution.py:135
  105.5 4.5 %forward.9.rest_0_ = f32[4,4096]{1,0:T(4,128)S(1)} custom-call(s32[1]{0:T(128)} %bitcast.side, s32[4,4096]{1,0:T(4,128)S(1)} %get-tuple-element.44.code, bf16[4096,512]{1,0:T(8,128)(2,1)S(1)} %copy-done.3, bf16[4096,512]{1,0:T(8,128)(2,1)} %collective-permute-done.other, f32[4,4096]{1,0:T(4,128)S(1)} %forward.8.rest_0_, ...), custom_call_target="tpu_custom_call" | custom-call | flops 2147483648 | bytes 6291456 | tf_op jit(solution)/shard_map/forward/pallas_call | solution.py:109
  110.0 1.5 collective-permute-start.10
  111.6 2.1 %collective-permute-start.13 = (bf16[4,64,1024]{2,1,0:T(8,128)(2,1)S(1)}, bf16[4,64,1024]{2,1,0:T(8,128)(2,1)S(1)}, u32[]{:S(2)}, u32[]{:S(2)}) collective-permute-start(bf16[4,64,1024]{2,1,0:T(8,128)(2,1)S(1)} %convert_element_type.44), channel_id=1, source_target_pairs={{0,1},{1,0},{2,3},{3,2},{4,5},{5,4},{6,7},{7,6},{8,9},{9,8},{10,11... | collective-permute-start | bytes 1572872 | tf_op jit(solution)/shard_map/ppermute | solution.py:165
  113.7 0.7 collective-permute-done.10
  114.4 1.6 collective-permute-start.12
  116.0 0.1 add_convert_fusion.3
  116.1 2.5 %collective-permute-start.14 = (bf16[4,64,1024]{2,1,0:T(8,128)(2,1)S(1)}, bf16[4,64,1024]{2,1,0:T(8,128)(2,1)S(1)}, u32[]{:S(2)}, u32[]{:S(2)}) collective-permute-start(bf16[4,64,1024]{2,1,0:T(8,128)(2,1)S(1)} %add_convert_fusion.3), channel_id=1, source_target_pairs={{0,2},{1,3},{2,0},{3,1},{4,6},{5,7},{6,4},{7,5},{8,10},{9,11},{10,... | collective-permute-start | bytes 1572872 | tf_op jit(solution)/shard_map/ppermute | solution.py:165
  118.6 0.2 collective-permute-done.12
  118.8 4.8 %backward.9.rest_0_ = f32[4,64,1024]{2,1,0:T(8,128)S(1)} custom-call(s32[1]{0:T(128)} %bitcast.side, s32[4,4096]{1,0:T(4,128)S(1)} %get-tuple-element.44.code, bf16[4096,512]{1,0:T(8,128)(2,1)S(1)} %copy-done.3, bf16[4096,512]{1,0:T(8,128)(2,1)} %collective-permute-done.other, f32[4,4096]{1,0:T(4,128)S(1)} %add.68.logits, f32[8,4096]{1,0:T(8,128)S(1)} %add.66.logits.joined, ...), custom_call_target="tpu_custom_call" | custom-call | flops 2147483648 | bytes 6291456 | tf_op jit(solution)/shard_map/backward/pallas_call | solution.py:135
  123.6 2.1 %collective-permute-start.16 = (bf16[4,64,1024]{2,1,0:T(8,128)(2,1)S(1)}, bf16[4,64,1024]{2,1,0:T(8,128)(2,1)S(1)}, u32[]{:S(2)}, u32[]{:S(2)}) collective-permute-start(bf16[4,64,1024]{2,1,0:T(8,128)(2,1)S(1)} %convert_element_type.52), channel_id=1, source_target_pairs={{0,1},{1,0},{2,3},{3,2},{4,5},{5,4},{6,7},{7,6},{8,9},{9,8},{10,11... | collective-permute-start | bytes 1572872 | tf_op jit(solution)/shard_map/ppermute | solution.py:165
  125.7 7.7 %collective-permute-done.13.rest_1_ = bf16[4,64,1024]{2,1,0:T(8,128)(2,1)S(1)} collective-permute-done((bf16[4,64,1024]{2,1,0:T(8,128)(2,1)S(1)}, bf16[4,64,1024]{2,1,0:T(8,128)(2,1)S(1)}, u32[]{:S(2)}, u32[]{:S(2)}) %collective-permute-start.13) | collective-permute-done | bytes 524320 | tf_op jit(solution)/shard_map/ppermute | solution.py:165
  133.4 4.7 %backward.10.rest_0_ = f32[4,64,1024]{2,1,0:T(8,128)S(1)} custom-call(s32[1]{0:T(128)} %bitcast.side, s32[4,4096]{1,0:T(4,128)S(1)} %get-tuple-element.44.code, bf16[4096,512]{1,0:T(8,128)(2,1)S(1)} %copy-done.3, bf16[4096,512]{1,0:T(8,128)(2,1)} %collective-permute-done.other, f32[4,4096]{1,0:T(4,128)S(1)} %add.68.logits, f32[8,4096]{1,0:T(8,128)S(1)} %add.66.logits.joined, ...), custom_call_target="tpu_custom_call" | custom-call | flops 2147483648 | bytes 6291456 | tf_op jit(solution)/shard_map/backward/pallas_call | solution.py:135
  138.2 4.8 %backward.11.rest_0_ = f32[4,64,1024]{2,1,0:T(8,128)S(1)} custom-call(s32[1]{0:T(128)} %bitcast.side, s32[4,4096]{1,0:T(4,128)S(1)} %get-tuple-element.44.code, bf16[4096,512]{1,0:T(8,128)(2,1)S(1)} %copy-done.3, bf16[4096,512]{1,0:T(8,128)(2,1)} %collective-permute-done.other, f32[4,4096]{1,0:T(4,128)S(1)} %add.68.logits, f32[8,4096]{1,0:T(8,128)S(1)} %add.66.logits.joined, ...), custom_call_target="tpu_custom_call" | custom-call | flops 2147483648 | bytes 6291456 | tf_op jit(solution)/shard_map/backward/pallas_call | solution.py:135
  143.0 2.0 %collective-permute-start.15 = (bf16[4,64,1024]{2,1,0:T(8,128)(2,1)S(1)}, bf16[4,64,1024]{2,1,0:T(8,128)(2,1)S(1)}, u32[]{:S(2)}, u32[]{:S(2)}) collective-permute-start(bf16[4,64,1024]{2,1,0:T(8,128)(2,1)S(1)} %convert_element_type.50), channel_id=1, source_target_pairs={{0,1},{1,0},{2,3},{3,2},{4,5},{5,4},{6,7},{7,6},{8,9},{9,8},{10,11... | collective-permute-start | bytes 1572872 | tf_op jit(solution)/shard_map/ppermute | solution.py:165
  145.1 5.2 %collective-permute-done.16 = bf16[4,64,1024]{2,1,0:T(8,128)(2,1)S(1)} collective-permute-done((bf16[4,64,1024]{2,1,0:T(8,128)(2,1)S(1)}, bf16[4,64,1024]{2,1,0:T(8,128)(2,1)S(1)}, u32[]{:S(2)}, u32[]{:S(2)}) %collective-permute-start.16) | collective-permute-done | bytes 524320 | tf_op jit(solution)/shard_map/ppermute | solution.py:165
  150.3 0.9 add_convert_fusion.1
  151.2 1.1 collective-permute-start.17
  152.3 4.8 %backward.12.rest_0_ = f32[4,64,1024]{2,1,0:T(8,128)S(1)} custom-call(s32[1]{0:T(128)} %bitcast.side, s32[4,4096]{1,0:T(4,128)S(1)} %get-tuple-element.43.code, bf16[4096,512]{1,0:T(8,128)(2,1)S(1)} %copy-done.3, bf16[4096,512]{1,0:T(8,128)(2,1)} %collective-permute-done.other, f32[8,4096]{1,0:T(8,128)S(1)} %add.66.logits.joined, ...), custom_call_target="tpu_custom_call" | custom-call | flops 2147483648 | bytes 6291456 | tf_op jit(solution)/shard_map/backward/pallas_call | solution.py:135
  157.1 1.1 add_convert_fusion.2
  158.2 3.5 %all-to-all-start.2 = ((bf16[4,64,1024]{2,1,0:T(8,128)(2,1)}), bf16[4,64,1024]{2,1,0:T(8,128)(2,1)S(1)}, u32[]{:S(2)}, u32[]{:S(2)}) async-start(bf16[4,64,1024]{2,1,0:T(8,128)(2,1)} %add_convert_fusion.2), calls=%async_computation.2 | async-start | bytes 1048576 | tf_op jit(solution)/shard_map/all_to_all | solution.py:186
  161.7 2.2 %copy-done.4 = bf16[4096,512]{1,0:T(8,128)(2,1)S(1)} copy-done((bf16[4096,512]{1,0:T(8,128)(2,1)S(1)}, bf16[4096,512]{1,0:T(8,128)(2,1)}, u32[]{:S(2)}) %copy-start.4) | copy-done | bytes 4194328
  163.9 4.7 %backward.13 = f32[4,64,1024]{2,1,0:T(8,128)S(1)} custom-call(s32[1]{0:T(128)} %bitcast.side, s32[4,4096]{1,0:T(4,128)S(1)} %get-tuple-element.44.code, bf16[4096,512]{1,0:T(8,128)(2,1)S(1)} %copy-done.4, bf16[4096,512]{1,0:T(8,128)(2,1)} %collective-permute-done.other, f32[4,4096]{1,0:T(4,128)S(1)} %add.68.logits, f32[8,4096]{1,0:T(8,128)S(1)} %add.66.logits.joined, ...), custom_call_target="tpu_custom_call" | custom-call | flops 2147483648 | bytes 6291456 | tf_op jit(solution)/shard_map/backward/pallas_call | solution.py:135
  168.6 0.6 collective-permute-done.17
  169.2 2.1 %add_convert_fusion = bf16[4,64,1024]{2,1,0:T(8,128)(2,1)} fusion(bf16[4,64,1024]{2,1,0:T(8,128)(2,1)} %collective-permute-done.17, f32[4,64,1024]{2,1,0:T(8,128)S(1)} %backward.13, bf16[4,64,1024]{2,1,0:T(8,128)(2,1)S(1)} %collective-permute-done.15), kind=kLoop, calls=%fused_computation.1 | loop fusion | flops 1310720 | bytes 2621440 | tf_op jit(solution)/shard_map/convert_element_type | solution.py:330
  171.3 3.6 %all-to-all-start.3 = ((bf16[4,64,1024]{2,1,0:T(8,128)(2,1)}), bf16[4,64,1024]{2,1,0:T(8,128)(2,1)S(1)}, u32[]{:S(2)}, u32[]{:S(2)}) async-start(bf16[4,64,1024]{2,1,0:T(8,128)(2,1)} %add_convert_fusion), calls=%async_computation.3 | async-start | bytes 1048576 | tf_op jit(solution)/shard_map/all_to_all | solution.py:186
  174.9 6.5 %all-to-all-done.3 = bf16[4,64,1024]{2,1,0:T(8,128)(2,1)S(1)} async-done(((bf16[4,64,1024]{2,1,0:T(8,128)(2,1)}), bf16[4,64,1024]{2,1,0:T(8,128)(2,1)S(1)}, u32[]{:S(2)}, u32[]{:S(2)}) %all-to-all-start.3) | async-done | bytes 524320 | tf_op jit(solution)/shard_map/all_to_all | solution.py:186
  181.5 1.1 pad_maximum_fusion
  (38 shorter events, 0.7 us)
Async XLA Ops:
  0.0 16.0 %copy-start = (s32[8,16384]{1,0:T(8,128)S(1)}, s32[8,16384]{1,0:T(8,128)}, u32[]{:S(2)}) copy-start(s32[8,16384]{1,0:T(8,128)} %param.10) | copy-start | bytes 1572868
  0.0 7.4 %copy-start.7 = (s32[8]{0:T(128)S(1)}, s32[8]{0:T(128)}, u32[]{:S(2)}) copy-start(s32[8]{0:T(128)} %param.11) | copy-start | bytes 100
  0.0 21.7 %collective-permute-start = (bf16[4096,512]{1,0:T(8,128)(2,1)}, bf16[4096,512]{1,0:T(8,128)(2,1)}, u32[]{:S(2)}, u32[]{:S(2)}) collective-permute-start(bf16[4096,512]{1,0:T(8,128)(2,1)} %mine.11), channel_id=1, source_target_pairs={{0,4},{4,0},{8,12},{12,8},{16,20},{20,16},{24,28},{28,24},{1,5},{5... | collective-permute-start | bytes 12582920 | tf_op jit(solution)/shard_map/ppermute | solution.py:165
  1.7 14.4 %copy-start.6 = (bf16[4,8]{1,0:T(4,128)(2,1)S(1)}, bf16[4,8]{1,0:T(4,128)(2,1)}, u32[]{:S(2)}) copy-start(bf16[4,8]{1,0:T(4,128)(2,1)} %param.13) | copy-start | bytes 196
  2.6 13.4 %all-to-all-start = ((bf16[4,64,1024]{2,1,0:T(8,128)(2,1)}), bf16[4,64,1024]{2,1,0:T(8,128)(2,1)S(1)}, u32[]{:S(2)}, u32[]{:S(2)}) async-start(bf16[4,64,1024]{2,1,0:T(8,128)(2,1)} %bitcast.72), calls=%async_computation | async-start | bytes 1048576 | tf_op jit(solution)/shard_map/all_to_all | solution.py:186
  17.2 24.3 %collective-permute-start.2 = (bf16[4,64,1024]{2,1,0:T(8,128)(2,1)S(1)}, bf16[4,64,1024]{2,1,0:T(8,128)(2,1)S(1)}, u32[]{:S(2)}, u32[]{:S(2)}) collective-permute-start(bf16[4,64,1024]{2,1,0:T(8,128)(2,1)S(1)} %all-to-all-done.rest_0_), channel_id=1, source_target_pairs={{0,1},{1,0},{2,3},{3,2},{4,5},{5,4},{6,7},{7,6},{8,9},{9,8},{10,11... | collective-permute-start | bytes 1572872 | tf_op jit(solution)/shard_map/ppermute | solution.py:165
  18.8 25.2 %collective-permute-start.1 = (bf16[4,64,1024]{2,1,0:T(8,128)(2,1)S(1)}, bf16[4,64,1024]{2,1,0:T(8,128)(2,1)S(1)}, u32[]{:S(2)}, u32[]{:S(2)}) collective-permute-start(bf16[4,64,1024]{2,1,0:T(8,128)(2,1)S(1)} %all-to-all-done.rest_0_), channel_id=1, source_target_pairs={{0,2},{1,3},{2,0},{3,1},{4,6},{5,7},{6,4},{7,5},{8,10},{9,11},{10,... | collective-permute-start | bytes 1572872 | tf_op jit(solution)/shard_map/ppermute | solution.py:165
  21.7 2.2 %copy-start.1 = (bf16[4096,512]{1,0:T(8,128)(2,1)S(1)}, bf16[4096,512]{1,0:T(8,128)(2,1)}, u32[]{:S(2)}) copy-start(bf16[4096,512]{1,0:T(8,128)(2,1)} %mine.11) | copy-start | bytes 12582916
  28.5 15.5 %all-to-all-start.1 = ((bf16[4,64,1024]{2,1,0:T(8,128)(2,1)}), bf16[4,64,1024]{2,1,0:T(8,128)(2,1)S(1)}, u32[]{:S(2)}, u32[]{:S(2)}) async-start(bf16[4,64,1024]{2,1,0:T(8,128)(2,1)} %bitcast.70), calls=%async_computation.1 | async-start | bytes 1048576 | tf_op jit(solution)/shard_map/all_to_all | solution.py:186
  32.2 12.1 %collective-permute-start.4 = (f32[4,1,4096]{2,0,1:T(4,128)S(1)}, f32[4,1,4096]{2,0,1:T(4,128)S(1)}, u32[]{:S(2)}, u32[]{:S(2)}) collective-permute-start(f32[4,1,4096]{2,0,1:T(4,128)S(1)} %bitcast.87), channel_id=1, source_target_pairs={{0,4},{4,0},{8,12},{12,8},{16,20},{20,16},{24,28},{28,24},{1,5},{5... | collective-permute-start | bytes 196616 | tf_op jit(solution)/shard_map/ppermute | solution.py:165
  44.0 24.7 %collective-permute-start.3 = (bf16[4,64,1024]{2,1,0:T(8,128)(2,1)S(1)}, bf16[4,64,1024]{2,1,0:T(8,128)(2,1)S(1)}, u32[]{:S(2)}, u32[]{:S(2)}) collective-permute-start(bf16[4,64,1024]{2,1,0:T(8,128)(2,1)S(1)} %collective-permute-done.1.rest_1_), channel_id=1, source_target_pairs={{0,1},{1,0},{2,3},{3,2},{4,5},{5,4},{6,7},{7,6},{8,9},{9,8},{10,11... | collective-permute-start | bytes 1572872 | tf_op jit(solution)/shard_map/ppermute | solution.py:165
  44.4 35.5 %collective-permute-start.8 = (bf16[4,64,1024]{2,1,0:T(8,128)(2,1)S(1)}, bf16[4,64,1024]{2,1,0:T(8,128)(2,1)S(1)}, u32[]{:S(2)}, u32[]{:S(2)}) collective-permute-start(bf16[4,64,1024]{2,1,0:T(8,128)(2,1)S(1)} %all-to-all-done.1.rest_0_), channel_id=1, source_target_pairs={{0,1},{1,0},{2,3},{3,2},{4,5},{5,4},{6,7},{7,6},{8,9},{9,8},{10,11... | collective-permute-start | bytes 1572872 | tf_op jit(solution)/shard_map/ppermute | solution.py:165
  46.1 33.7 %collective-permute-start.7 = (bf16[4,64,1024]{2,1,0:T(8,128)(2,1)S(1)}, bf16[4,64,1024]{2,1,0:T(8,128)(2,1)S(1)}, u32[]{:S(2)}, u32[]{:S(2)}) collective-permute-start(bf16[4,64,1024]{2,1,0:T(8,128)(2,1)S(1)} %all-to-all-done.1.rest_0_), channel_id=1, source_target_pairs={{0,2},{1,3},{2,0},{3,1},{4,6},{5,7},{6,4},{7,5},{8,10},{9,11},{10,... | collective-permute-start | bytes 1572872 | tf_op jit(solution)/shard_map/ppermute | solution.py:165
  47.2 2.2 %copy-start.2 = (bf16[4096,512]{1,0:T(8,128)(2,1)S(1)}, bf16[4096,512]{1,0:T(8,128)(2,1)}, u32[]{:S(2)}) copy-start(bf16[4096,512]{1,0:T(8,128)(2,1)} %mine.11) | copy-start | bytes 12582916
  56.2 23.7 %copy-start.5 = (bf16[4096]{0:T(1024)(128)(2,1)S(1)}, bf16[4096]{0:T(1024)(128)(2,1)}, u32[]{:S(2)}) copy-start(bf16[4096]{0:T(1024)(128)(2,1)} %param.9) | copy-start | bytes 24580
  73.3 5.0 %collective-permute-start.5 = (f32[8,4096]{1,0:T(8,128)S(1)}, f32[8,4096]{1,0:T(8,128)S(1)}, u32[]{:S(2)}, u32[]{:S(2)}) collective-permute-start(f32[8,4096]{1,0:T(8,128)S(1)} %forward.7.rest_0_), channel_id=1, source_target_pairs={{0,8},{4,12},{8,0},{12,4},{16,24},{20,28},{24,16},{28,20},{1,9},{5... | collective-permute-start | bytes 393224 | tf_op jit(solution)/shard_map/ppermute | solution.py:165
  78.3 5.0 %collective-permute-start.6 = (f32[8,4096]{1,0:T(8,128)S(1)}, f32[8,4096]{1,0:T(8,128)S(1)}, u32[]{:S(2)}, u32[]{:S(2)}) collective-permute-start(f32[8,4096]{1,0:T(8,128)S(1)} %add.65), channel_id=1, source_target_pairs={{0,16},{4,20},{8,24},{12,28},{16,0},{20,4},{24,8},{28,12},{1,17},{... | collective-permute-start | bytes 393224 | tf_op jit(solution)/shard_map/ppermute | solution.py:165
  79.9 25.6 %collective-permute-start.9 = (bf16[4,64,1024]{2,1,0:T(8,128)(2,1)S(1)}, bf16[4,64,1024]{2,1,0:T(8,128)(2,1)S(1)}, u32[]{:S(2)}, u32[]{:S(2)}) collective-permute-start(bf16[4,64,1024]{2,1,0:T(8,128)(2,1)S(1)} %collective-permute-done.7.rest_1_), channel_id=1, source_target_pairs={{0,1},{1,0},{2,3},{3,2},{4,5},{5,4},{6,7},{7,6},{8,9},{9,8},{10,11... | collective-permute-start | bytes 1572872 | tf_op jit(solution)/shard_map/ppermute | solution.py:165
  83.4 5.1 %copy-start.3 = (bf16[4096,512]{1,0:T(8,128)(2,1)S(1)}, bf16[4096,512]{1,0:T(8,128)(2,1)}, u32[]{:S(2)}) copy-start(bf16[4096,512]{1,0:T(8,128)(2,1)} %mine.11) | copy-start | bytes 12582916
  88.4 26.0 %collective-permute-start.11 = (bf16[4,64,1024]{2,1,0:T(8,128)(2,1)S(1)}, bf16[4,64,1024]{2,1,0:T(8,128)(2,1)S(1)}, u32[]{:S(2)}, u32[]{:S(2)}) collective-permute-start(bf16[4,64,1024]{2,1,0:T(8,128)(2,1)S(1)} %convert_element_type.43), channel_id=1, source_target_pairs={{0,1},{1,0},{2,3},{3,2},{4,5},{5,4},{6,7},{7,6},{8,9},{9,8},{10,11... | collective-permute-start | bytes 1572872 | tf_op jit(solution)/shard_map/ppermute | solution.py:165
  110.0 4.3 %collective-permute-start.10 = (f32[4,4096]{1,0:T(4,128)S(1)}, f32[4,4096]{1,0:T(4,128)S(1)}, u32[]{:S(2)}, u32[]{:S(2)}) collective-permute-start(f32[4,4096]{1,0:T(4,128)S(1)} %forward.9.rest_0_), channel_id=1, source_target_pairs={{0,8},{4,12},{8,0},{12,4},{16,24},{20,28},{24,16},{28,20},{1,9},{5... | collective-permute-start | bytes 196616 | tf_op jit(solution)/shard_map/ppermute | solution.py:165
  111.6 21.8 %collective-permute-start.13 = (bf16[4,64,1024]{2,1,0:T(8,128)(2,1)S(1)}, bf16[4,64,1024]{2,1,0:T(8,128)(2,1)S(1)}, u32[]{:S(2)}, u32[]{:S(2)}) collective-permute-start(bf16[4,64,1024]{2,1,0:T(8,128)(2,1)S(1)} %convert_element_type.44), channel_id=1, source_target_pairs={{0,1},{1,0},{2,3},{3,2},{4,5},{5,4},{6,7},{7,6},{8,9},{9,8},{10,11... | collective-permute-start | bytes 1572872 | tf_op jit(solution)/shard_map/ppermute | solution.py:165
  114.4 4.3 %collective-permute-start.12 = (f32[4,4096]{1,0:T(4,128)S(1)}, f32[4,4096]{1,0:T(4,128)S(1)}, u32[]{:S(2)}, u32[]{:S(2)}) collective-permute-start(f32[4,4096]{1,0:T(4,128)S(1)} %add.67), channel_id=1, source_target_pairs={{0,16},{4,20},{8,24},{12,28},{16,0},{20,4},{24,8},{28,12},{1,17},{... | collective-permute-start | bytes 196616 | tf_op jit(solution)/shard_map/ppermute | solution.py:165
  116.1 22.0 %collective-permute-start.14 = (bf16[4,64,1024]{2,1,0:T(8,128)(2,1)S(1)}, bf16[4,64,1024]{2,1,0:T(8,128)(2,1)S(1)}, u32[]{:S(2)}, u32[]{:S(2)}) collective-permute-start(bf16[4,64,1024]{2,1,0:T(8,128)(2,1)S(1)} %add_convert_fusion.3), channel_id=1, source_target_pairs={{0,2},{1,3},{2,0},{3,1},{4,6},{5,7},{6,4},{7,5},{8,10},{9,11},{10,... | collective-permute-start | bytes 1572872 | tf_op jit(solution)/shard_map/ppermute | solution.py:165
  123.6 26.6 %collective-permute-start.16 = (bf16[4,64,1024]{2,1,0:T(8,128)(2,1)S(1)}, bf16[4,64,1024]{2,1,0:T(8,128)(2,1)S(1)}, u32[]{:S(2)}, u32[]{:S(2)}) collective-permute-start(bf16[4,64,1024]{2,1,0:T(8,128)(2,1)S(1)} %convert_element_type.52), channel_id=1, source_target_pairs={{0,1},{1,0},{2,3},{3,2},{4,5},{5,4},{6,7},{7,6},{8,9},{9,8},{10,11... | collective-permute-start | bytes 1572872 | tf_op jit(solution)/shard_map/ppermute | solution.py:165
  143.0 25.6 %collective-permute-start.15 = (bf16[4,64,1024]{2,1,0:T(8,128)(2,1)S(1)}, bf16[4,64,1024]{2,1,0:T(8,128)(2,1)S(1)}, u32[]{:S(2)}, u32[]{:S(2)}) collective-permute-start(bf16[4,64,1024]{2,1,0:T(8,128)(2,1)S(1)} %convert_element_type.50), channel_id=1, source_target_pairs={{0,1},{1,0},{2,3},{3,2},{4,5},{5,4},{6,7},{7,6},{8,9},{9,8},{10,11... | collective-permute-start | bytes 1572872 | tf_op jit(solution)/shard_map/ppermute | solution.py:165
  151.2 18.0 %collective-permute-start.17 = (bf16[4,64,1024]{2,1,0:T(8,128)(2,1)}, bf16[4,64,1024]{2,1,0:T(8,128)(2,1)}, u32[]{:S(2)}, u32[]{:S(2)}) collective-permute-start(bf16[4,64,1024]{2,1,0:T(8,128)(2,1)} %add_convert_fusion.1), channel_id=1, source_target_pairs={{0,2},{1,3},{2,0},{3,1},{4,6},{5,7},{6,4},{7,5},{8,10},{9,11},{10,... | collective-permute-start | bytes 1572872 | tf_op jit(solution)/shard_map/ppermute | solution.py:165
  158.2 13.1 %all-to-all-start.2 = ((bf16[4,64,1024]{2,1,0:T(8,128)(2,1)}), bf16[4,64,1024]{2,1,0:T(8,128)(2,1)S(1)}, u32[]{:S(2)}, u32[]{:S(2)}) async-start(bf16[4,64,1024]{2,1,0:T(8,128)(2,1)} %add_convert_fusion.2), calls=%async_computation.2 | async-start | bytes 1048576 | tf_op jit(solution)/shard_map/all_to_all | solution.py:186
  161.7 2.2 %copy-start.4 = (bf16[4096,512]{1,0:T(8,128)(2,1)S(1)}, bf16[4096,512]{1,0:T(8,128)(2,1)}, u32[]{:S(2)}) copy-start(bf16[4096,512]{1,0:T(8,128)(2,1)} %mine.11) | copy-start | bytes 12582916
  171.3 10.2 %all-to-all-start.3 = ((bf16[4,64,1024]{2,1,0:T(8,128)(2,1)}), bf16[4,64,1024]{2,1,0:T(8,128)(2,1)S(1)}, u32[]{:S(2)}, u32[]{:S(2)}) async-start(bf16[4,64,1024]{2,1,0:T(8,128)(2,1)} %add_convert_fusion), calls=%async_computation.3 | async-start | bytes 1048576 | tf_op jit(solution)/shard_map/all_to_all | solution.py:186

commit v6 on v5

--- a/solution.py
+++ b/solution.py
@@ -307,7 +307,7 @@
             logits[c - 1] = run_sum(value, start=4)
         else:
             logits[c - 1] = run_sum(value)
-        run_backward(c - 1, far)
+        run_backward(c - 1, far, *([grads[c - 2][1]] if c > 1 else ()))
         reduce_far(c - 1)
         if more:
             arrived = together(*[held[c][slot] for slot in near])
@@ -316,7 +316,7 @@
             run_forward(c, (0,) + near)
             run_backward(c - 1, near)
         else:
-            run_backward(c - 1, even, *((grads[c - 2][1],) if c > 1 else ()))
+            run_backward(c - 1, even)
             run_backward(c - 1, (1,), *([grads[c - 2][bit] for bit in bits[1:]] if c > 1 else ()))
     reduce_near(count - 1)
     for c in range(count):

time: 183 us -> 181 us (0.989)
  starting transfers between devices: 39.2 us -> 36.2 us
    ppermute x18, starting transfers between devices: 23.9 us -> 21 us  [exchange(): lax.ppermute(value, axis, [(i, i ^ bit) for i in range(lax.axis_size(axis...]
  transfers between devices with their start and end apart: 22 -> 22, of which waited for: 12 -> 11; matrix products, arithmetic and copies ran while one was open for 5% -> 5% of each run, Pallas kernels for 36% -> 37%
where the time goes in v6:
time: 181 us; the launch traced here: 180 us
  Pallas kernels  66.1 us (37%)
  waiting for transfers between devices  60.1 us (33%)
  starting transfers between devices  36.2 us (20%)
  local copies, waits for them, and re-layouts  10.3 us (6%)
  other arithmetic  5.91 us (3%)
    ppermute x18, waiting for transfers between devices, exchange(): lax.ppermute(value, axis, [(i, i ^ bit) for i in range(lax.axis_size(axis...  46 us
    pallas_call x7, Pallas kernels, backward(): pl.pallas_call(functools.partial(backward_kernel, slots, len(waits)), out...  36.7 us
    pallas_call x5, Pallas kernels, forward(): pl.pallas_call(functools.partial(forward_kernel, slots, len(before), len(...  29.4 us
    ppermute x18, starting transfers between devices, exchange(): lax.ppermute(value, axis, [(i, i ^ bit) for i in range(lax.axis_size(axis...  21 us
    all_to_all x4, starting transfers between devices, swap(): lax.all_to_all(x, 'dp', split_axis=0, concat_axis=0, axis_index_groups=gr...  15.2 us
    all_to_all x4, waiting for transfers between devices, swap(): lax.all_to_all(x, 'dp', split_axis=0, concat_axis=0, axis_index_groups=gr...  14 us
    unnamed x17, local copies, waits for them, and re-layouts  6.63 us
  transfers between devices with their start and end apart: 22, of which 11 were waited for; matrix products, arithmetic and copies ran while one was open for 5% of the time, Pallas kernels for 37%

profile of v6, /device:TPU:0, one launch (start us, length us, event | category | flops | bytes accessed | tf_op | source)
XLA Modules:
  0.0 179.9 jit_solution(55720591394298323)
XLA Ops:
  0.0 0.5 collective-permute-start
  0.5 1.3 fusion.9
  1.7 0.9 copy.47
  2.6 4.8 %all-to-all-start = ((bf16[4,64,1024]{2,1,0:T(8,128)(2,1)}), bf16[4,64,1024]{2,1,0:T(8,128)(2,1)S(1)}, u32[]{:S(2)}, u32[]{:S(2)}) async-start(bf16[4,64,1024]{2,1,0:T(8,128)(2,1)} %bitcast.72), calls=%async_computation | async-start | bytes 1048576 | tf_op jit(solution)/shard_map/all_to_all | solution.py:186
  7.4 0.1 reshape.49
  7.5 0.8 copy.46
  8.3 0.2 dynamic-slice_reduce_fusion
  8.5 7.5 %all-to-all-done.rest_0_ = bf16[4,64,1024]{2,1,0:T(8,128)(2,1)S(1)} async-done(((bf16[4,64,1024]{2,1,0:T(8,128)(2,1)}), bf16[4,64,1024]{2,1,0:T(8,128)(2,1)S(1)}, u32[]{:S(2)}, u32[]{:S(2)}) %all-to-all-start) | async-done | bytes 524320 | tf_op jit(solution)/shard_map/all_to_all | solution.py:186
  16.0 0.1 reshape.47
  16.1 1.0 fusion.6
  17.1 0.1 reshape.52
  17.2 1.6 collective-permute-start.2
  18.8 2.6 %collective-permute-start.1 = (bf16[4,64,1024]{2,1,0:T(8,128)(2,1)S(1)}, bf16[4,64,1024]{2,1,0:T(8,128)(2,1)S(1)}, u32[]{:S(2)}, u32[]{:S(2)}) collective-permute-start(bf16[4,64,1024]{2,1,0:T(8,128)(2,1)S(1)} %all-to-all-done.rest_0_), channel_id=1, source_target_pairs={{0,2},{1,3},{2,0},{3,1},{4,6},{5,7},{6,4},{7,5},{8,10},{9,11},{10,... | collective-permute-start | bytes 1572872 | tf_op jit(solution)/shard_map/ppermute | solution.py:165
  21.5 0.2 and_select_fusion
  21.7 2.2 %copy-done.1 = bf16[4096,512]{1,0:T(8,128)(2,1)S(1)} copy-done((bf16[4096,512]{1,0:T(8,128)(2,1)S(1)}, bf16[4096,512]{1,0:T(8,128)(2,1)}, u32[]{:S(2)}) %copy-start.1) | copy-done | bytes 4194328
  23.9 4.6 %forward.5.rest_0_.rest_3_ = f32[4,4096]{1,0:T(4,128)S(1)} custom-call(s32[1]{0:T(128)} %bitcast.side, s32[4,4096]{1,0:T(4,128)S(1)} %get-tuple-element.43.code, bf16[4096,512]{1,0:T(8,128)(2,1)S(1)} %copy-done.1, bf16[4096,512]{1,0:T(8,128)(2,1)} %collective-permute-done.other, bf16[4,64,1024]{2,1,0:T(8,128)(2,1)S(1)} %all-to-all-done.rest_0_), custom_call_target="tpu_custom_call" | custom-call | flops 2147483648 | bytes 6291456 | tf_op jit(solution)/shard_map/forward/pallas_call | solution.py:109
  28.5 3.5 %all-to-all-start.1 = ((bf16[4,64,1024]{2,1,0:T(8,128)(2,1)}), bf16[4,64,1024]{2,1,0:T(8,128)(2,1)S(1)}, u32[]{:S(2)}, u32[]{:S(2)}) async-start(bf16[4,64,1024]{2,1,0:T(8,128)(2,1)} %bitcast.70), calls=%async_computation.1 | async-start | bytes 1048576 | tf_op jit(solution)/shard_map/all_to_all | solution.py:186
  32.0 0.1 constant_dynamic-slice_fusion.1
  32.2 0.1 collective-permute-start.4
  32.3 9.2 %collective-permute-done.2.rest_2_ = bf16[4,64,1024]{2,1,0:T(8,128)(2,1)S(1)} collective-permute-done((bf16[4,64,1024]{2,1,0:T(8,128)(2,1)S(1)}, bf16[4,64,1024]{2,1,0:T(8,128)(2,1)S(1)}, u32[]{:S(2)}, u32[]{:S(2)}) %collective-permute-start.2) | collective-permute-done | bytes 524320 | tf_op jit(solution)/shard_map/ppermute | solution.py:165
  41.5 2.5 %collective-permute-done.1.rest_1_ = bf16[4,64,1024]{2,1,0:T(8,128)(2,1)S(1)} collective-permute-done((bf16[4,64,1024]{2,1,0:T(8,128)(2,1)S(1)}, bf16[4,64,1024]{2,1,0:T(8,128)(2,1)S(1)}, u32[]{:S(2)}, u32[]{:S(2)}) %collective-permute-start.1) | collective-permute-done | bytes 524320 | tf_op jit(solution)/shard_map/ppermute | solution.py:165
  44.0 0.3 collective-permute-start.3
  44.4 1.8 collective-permute-start.8
  46.1 1.1 collective-permute-start.7
  47.2 2.2 %copy-done.2 = bf16[4096,512]{1,0:T(8,128)(2,1)S(1)} copy-done((bf16[4096,512]{1,0:T(8,128)(2,1)S(1)}, bf16[4096,512]{1,0:T(8,128)(2,1)}, u32[]{:S(2)}) %copy-start.2) | copy-done | bytes 4194328
  49.4 6.7 %forward.6.rest_0_.rest_3_ = f32[4,4096]{1,0:T(4,128)S(1)} custom-call(s32[1]{0:T(128)} %bitcast.side, s32[4,4096]{1,0:T(4,128)S(1)} %get-tuple-element.43.code, bf16[4096,512]{1,0:T(8,128)(2,1)S(1)} %copy-done.2, bf16[4096,512]{1,0:T(8,128)(2,1)} %collective-permute-done.other, f32[4,4096]{1,0:T(4,128)S(1)} %forward.5.rest_0_.rest_3_, ...), custom_call_target="tpu_custom_call" | custom-call | flops 4294967296 | bytes 6291456 | tf_op jit(solution)/shard_map/forward/pallas_call | solution.py:109
  56.2 12.6 %collective-permute-done.3.rest_1_ = bf16[4,64,1024]{2,1,0:T(8,128)(2,1)S(1)} collective-permute-done((bf16[4,64,1024]{2,1,0:T(8,128)(2,1)S(1)}, bf16[4,64,1024]{2,1,0:T(8,128)(2,1)S(1)}, u32[]{:S(2)}, u32[]{:S(2)}) %collective-permute-start.3) | collective-permute-done | bytes 524320 | tf_op jit(solution)/shard_map/ppermute | solution.py:165
  68.7 4.5 %forward.7.rest_0_ = f32[8,4096]{1,0:T(8,128)S(1)} custom-call(s32[1]{0:T(128)} %bitcast.side, s32[4,4096]{1,0:T(4,128)S(1)} %get-tuple-element.43.code, bf16[4096,512]{1,0:T(8,128)(2,1)S(1)} %copy-done.2, bf16[4096,512]{1,0:T(8,128)(2,1)} %collective-permute-done.other, f32[4,4096]{1,0:T(4,128)S(1)} %forward.6.rest_0_.rest_3_, ...), custom_call_target="tpu_custom_call" | custom-call | flops 2147483648 | bytes 6291456 | tf_op jit(solution)/shard_map/forward/pallas_call | solution.py:109
  73.3 1.5 collective-permute-start.5
  74.8 3.5 %collective-permute-done.5 = f32[8,4096]{1,0:T(8,128)S(1)} collective-permute-done((f32[8,4096]{1,0:T(8,128)S(1)}, f32[8,4096]{1,0:T(8,128)S(1)}, u32[]{:S(2)}, u32[]{:S(2)}) %collective-permute-start.5) | collective-permute-done | bytes 131104 | tf_op jit(solution)/shard_map/ppermute | solution.py:165
  78.3 1.6 collective-permute-start.6
  79.9 0.1 collective-permute-start.9
  80.0 3.4 %collective-permute-done.6 = f32[8,4096]{1,0:T(8,128)S(1)} collective-permute-done((f32[8,4096]{1,0:T(8,128)S(1)}, f32[8,4096]{1,0:T(8,128)S(1)}, u32[]{:S(2)}, u32[]{:S(2)}) %collective-permute-start.6) | collective-permute-done | bytes 131104 | tf_op jit(solution)/shard_map/ppermute | solution.py:165
  83.4 4.9 %backward.7.rest_3_ = f32[4,64,1024]{2,1,0:T(8,128)S(1)} custom-call(s32[1]{0:T(128)} %bitcast.side, s32[4,4096]{1,0:T(4,128)S(1)} %get-tuple-element.43.code, bf16[4096,512]{1,0:T(8,128)(2,1)S(1)} %copy-done.2, bf16[4096,512]{1,0:T(8,128)(2,1)} %collective-permute-done.other, f32[8,4096]{1,0:T(8,128)S(1)} %add.66.logits.joined, ...), custom_call_target="tpu_custom_call" | custom-call | flops 2147483648 | bytes 6291456 | tf_op jit(solution)/shard_map/backward/pallas_call | solution.py:135
  88.4 0.1 convert_element_type.43
  88.4 0.1 collective-permute-start.11
  88.5 9.0 %forward.8.rest_0_ = f32[4,4096]{1,0:T(4,128)S(1)} custom-call(s32[1]{0:T(128)} %bitcast.side, s32[4,4096]{1,0:T(4,128)S(1)} %get-tuple-element.44.code, bf16[4096,512]{1,0:T(8,128)(2,1)S(1)} %copy-done.3, bf16[4096,512]{1,0:T(8,128)(2,1)} %collective-permute-done.other, bf16[4,64,1024]{2,1,0:T(8,128)(2,1)S(1)} %all-to-all-done.1.rest_0_, ...), custom_call_target="tpu_custom_call" | custom-call | flops 6442450944 | bytes 6291456 | tf_op jit(solution)/shard_map/forward/pallas_call | solution.py:109
  97.5 8.0 %backward.8 = (f32[4,64,1024]{2,1,0:T(8,128)S(1)}, f32[4,64,1024]{2,1,0:T(8,128)S(1)}) custom-call(s32[1]{0:T(128)} %bitcast.side, s32[4,4096]{1,0:T(4,128)S(1)} %get-tuple-element.43.code, bf16[4096,512]{1,0:T(8,128)(2,1)S(1)} %copy-done.3, bf16[4096,512]{1,0:T(8,128)(2,1)} %collective-permute-done.other, f32[8,4096]{1,0:T(8,128)S(1)} %add.66.logits.joined, ...), custom_call_target="tpu_custom_call" | custom-call | flops 4294967296 | bytes 6291456 | tf_op jit(solution)/shard_map/backward/pallas_call | solution.py:135
  105.6 2.1 %collective-permute-start.13 = (bf16[4,64,1024]{2,1,0:T(8,128)(2,1)S(1)}, bf16[4,64,1024]{2,1,0:T(8,128)(2,1)S(1)}, u32[]{:S(2)}, u32[]{:S(2)}) collective-permute-start(bf16[4,64,1024]{2,1,0:T(8,128)(2,1)S(1)} %convert_element_type.44), channel_id=1, source_target_pairs={{0,1},{1,0},{2,3},{3,2},{4,5},{5,4},{6,7},{7,6},{8,9},{9,8},{10,11... | collective-permute-start | bytes 1572872 | tf_op jit(solution)/shard_map/ppermute | solution.py:165
  107.6 4.5 %forward.9.rest_0_ = f32[4,4096]{1,0:T(4,128)S(1)} custom-call(s32[1]{0:T(128)} %bitcast.side, s32[4,4096]{1,0:T(4,128)S(1)} %get-tuple-element.44.code, bf16[4096,512]{1,0:T(8,128)(2,1)S(1)} %copy-done.3, bf16[4096,512]{1,0:T(8,128)(2,1)} %collective-permute-done.other, f32[4,4096]{1,0:T(4,128)S(1)} %forward.8.rest_0_, ...), custom_call_target="tpu_custom_call" | custom-call | flops 2147483648 | bytes 6291456 | tf_op jit(solution)/shard_map/forward/pallas_call | solution.py:109
  112.1 1.5 collective-permute-start.10
  113.6 2.8 %collective-permute-done.10 = f32[4,4096]{1,0:T(4,128)S(1)} collective-permute-done((f32[4,4096]{1,0:T(4,128)S(1)}, f32[4,4096]{1,0:T(4,128)S(1)}, u32[]{:S(2)}, u32[]{:S(2)}) %collective-permute-start.10) | collective-permute-done | bytes 65568 | tf_op jit(solution)/shard_map/ppermute | solution.py:165
  116.5 1.6 collective-permute-start.12
  118.1 0.1 add_convert_fusion.3
  118.2 0.5 collective-permute-start.14
  118.7 2.1 %collective-permute-done.12 = f32[4,4096]{1,0:T(4,128)S(1)} collective-permute-done((f32[4,4096]{1,0:T(4,128)S(1)}, f32[4,4096]{1,0:T(4,128)S(1)}, u32[]{:S(2)}, u32[]{:S(2)}) %collective-permute-start.12) | collective-permute-done | bytes 65568 | tf_op jit(solution)/shard_map/ppermute | solution.py:165
  120.9 4.8 %backward.9.rest_0_ = f32[4,64,1024]{2,1,0:T(8,128)S(1)} custom-call(s32[1]{0:T(128)} %bitcast.side, s32[4,4096]{1,0:T(4,128)S(1)} %get-tuple-element.44.code, bf16[4096,512]{1,0:T(8,128)(2,1)S(1)} %copy-done.3, bf16[4096,512]{1,0:T(8,128)(2,1)} %collective-permute-done.other, f32[4,4096]{1,0:T(4,128)S(1)} %add.68.logits, f32[8,4096]{1,0:T(8,128)S(1)} %add.66.logits.joined, ...), custom_call_target="tpu_custom_call" | custom-call | flops 2147483648 | bytes 6291456 | tf_op jit(solution)/shard_map/backward/pallas_call | solution.py:135
  125.7 0.1 collective-permute-start.16
  125.8 4.7 %backward.10.rest_0_ = f32[4,64,1024]{2,1,0:T(8,128)S(1)} custom-call(s32[1]{0:T(128)} %bitcast.side, s32[4,4096]{1,0:T(4,128)S(1)} %get-tuple-element.44.code, bf16[4096,512]{1,0:T(8,128)(2,1)S(1)} %copy-done.3, bf16[4096,512]{1,0:T(8,128)(2,1)} %collective-permute-done.other, f32[4,4096]{1,0:T(4,128)S(1)} %add.68.logits, f32[8,4096]{1,0:T(8,128)S(1)} %add.66.logits.joined, ...), custom_call_target="tpu_custom_call" | custom-call | flops 2147483648 | bytes 6291456 | tf_op jit(solution)/shard_map/backward/pallas_call | solution.py:135
  130.6 5.0 %collective-permute-done.14.rest_1_ = bf16[4,64,1024]{2,1,0:T(8,128)(2,1)S(1)} collective-permute-done((bf16[4,64,1024]{2,1,0:T(8,128)(2,1)S(1)}, bf16[4,64,1024]{2,1,0:T(8,128)(2,1)S(1)}, u32[]{:S(2)}, u32[]{:S(2)}) %collective-permute-start.14) | collective-permute-done | bytes 524320 | tf_op jit(solution)/shard_map/ppermute | solution.py:165
  135.6 4.7 %backward.11.rest_0_ = f32[4,64,1024]{2,1,0:T(8,128)S(1)} custom-call(s32[1]{0:T(128)} %bitcast.side, s32[4,4096]{1,0:T(4,128)S(1)} %get-tuple-element.44.code, bf16[4096,512]{1,0:T(8,128)(2,1)S(1)} %copy-done.3, bf16[4096,512]{1,0:T(8,128)(2,1)} %collective-permute-done.other, f32[4,4096]{1,0:T(4,128)S(1)} %add.68.logits, f32[8,4096]{1,0:T(8,128)S(1)} %add.66.logits.joined, ...), custom_call_target="tpu_custom_call" | custom-call | flops 2147483648 | bytes 6291456 | tf_op jit(solution)/shard_map/backward/pallas_call | solution.py:135
  140.4 0.7 collective-permute-start.15
  141.1 0.9 add_convert_fusion.1
  142.1 3.4 %collective-permute-start.17 = (bf16[4,64,1024]{2,1,0:T(8,128)(2,1)}, bf16[4,64,1024]{2,1,0:T(8,128)(2,1)}, u32[]{:S(2)}, u32[]{:S(2)}) collective-permute-start(bf16[4,64,1024]{2,1,0:T(8,128)(2,1)} %add_convert_fusion.1), channel_id=1, source_target_pairs={{0,2},{1,3},{2,0},{3,1},{4,6},{5,7},{6,4},{7,5},{8,10},{9,11},{10,... | collective-permute-start | bytes 1572872 | tf_op jit(solution)/shard_map/ppermute | solution.py:165
  145.5 4.8 %backward.12.rest_0_ = f32[4,64,1024]{2,1,0:T(8,128)S(1)} custom-call(s32[1]{0:T(128)} %bitcast.side, s32[4,4096]{1,0:T(4,128)S(1)} %get-tuple-element.43.code, bf16[4096,512]{1,0:T(8,128)(2,1)S(1)} %copy-done.3, bf16[4096,512]{1,0:T(8,128)(2,1)} %collective-permute-done.other, f32[8,4096]{1,0:T(8,128)S(1)} %add.66.logits.joined, ...), custom_call_target="tpu_custom_call" | custom-call | flops 2147483648 | bytes 6291456 | tf_op jit(solution)/shard_map/backward/pallas_call | solution.py:135
  150.3 1.1 add_convert_fusion.2
  151.3 3.5 %all-to-all-start.2 = ((bf16[4,64,1024]{2,1,0:T(8,128)(2,1)}), bf16[4,64,1024]{2,1,0:T(8,128)(2,1)S(1)}, u32[]{:S(2)}, u32[]{:S(2)}) async-start(bf16[4,64,1024]{2,1,0:T(8,128)(2,1)} %add_convert_fusion.2), calls=%async_computation.2 | async-start | bytes 1048576 | tf_op jit(solution)/shard_map/all_to_all | solution.py:186
  154.8 2.2 %copy-done.4 = bf16[4096,512]{1,0:T(8,128)(2,1)S(1)} copy-done((bf16[4096,512]{1,0:T(8,128)(2,1)S(1)}, bf16[4096,512]{1,0:T(8,128)(2,1)}, u32[]{:S(2)}) %copy-start.4) | copy-done | bytes 4194328
  157.0 4.7 %backward.13 = f32[4,64,1024]{2,1,0:T(8,128)S(1)} custom-call(s32[1]{0:T(128)} %bitcast.side, s32[4,4096]{1,0:T(4,128)S(1)} %get-tuple-element.44.code, bf16[4096,512]{1,0:T(8,128)(2,1)S(1)} %copy-done.4, bf16[4096,512]{1,0:T(8,128)(2,1)} %collective-permute-done.other, f32[4,4096]{1,0:T(4,128)S(1)} %add.68.logits, f32[8,4096]{1,0:T(8,128)S(1)} %add.66.logits.joined, ...), custom_call_target="tpu_custom_call" | custom-call | flops 2147483648 | bytes 6291456 | tf_op jit(solution)/shard_map/backward/pallas_call | solution.py:135
  161.8 4.9 %collective-permute-done.17 = bf16[4,64,1024]{2,1,0:T(8,128)(2,1)} collective-permute-done((bf16[4,64,1024]{2,1,0:T(8,128)(2,1)}, bf16[4,64,1024]{2,1,0:T(8,128)(2,1)}, u32[]{:S(2)}, u32[]{:S(2)}) %collective-permute-start.17) | collective-permute-done | bytes 524320 | tf_op jit(solution)/shard_map/ppermute | solution.py:165
  166.6 2.1 %add_convert_fusion = bf16[4,64,1024]{2,1,0:T(8,128)(2,1)} fusion(bf16[4,64,1024]{2,1,0:T(8,128)(2,1)} %collective-permute-done.17, f32[4,64,1024]{2,1,0:T(8,128)S(1)} %backward.13, bf16[4,64,1024]{2,1,0:T(8,128)(2,1)S(1)} %collective-permute-done.15), kind=kLoop, calls=%fused_computation.1 | loop fusion | flops 1310720 | bytes 2621440 | tf_op jit(solution)/shard_map/convert_element_type | solution.py:330
  168.7 3.5 %all-to-all-start.3 = ((bf16[4,64,1024]{2,1,0:T(8,128)(2,1)}), bf16[4,64,1024]{2,1,0:T(8,128)(2,1)S(1)}, u32[]{:S(2)}, u32[]{:S(2)}) async-start(bf16[4,64,1024]{2,1,0:T(8,128)(2,1)} %add_convert_fusion), calls=%async_computation.3 | async-start | bytes 1048576 | tf_op jit(solution)/shard_map/all_to_all | solution.py:186
  172.3 6.5 %all-to-all-done.3 = bf16[4,64,1024]{2,1,0:T(8,128)(2,1)S(1)} async-done(((bf16[4,64,1024]{2,1,0:T(8,128)(2,1)}), bf16[4,64,1024]{2,1,0:T(8,128)(2,1)S(1)}, u32[]{:S(2)}, u32[]{:S(2)}) %all-to-all-start.3) | async-done | bytes 524320 | tf_op jit(solution)/shard_map/all_to_all | solution.py:186
  178.8 1.1 pad_maximum_fusion
  (38 shorter events, 0.6 us)
Async XLA Ops:
  0.0 16.0 %copy-start = (s32[8,16384]{1,0:T(8,128)S(1)}, s32[8,16384]{1,0:T(8,128)}, u32[]{:S(2)}) copy-start(s32[8,16384]{1,0:T(8,128)} %param.10) | copy-start | bytes 1572868
  0.0 7.4 %copy-start.7 = (s32[8]{0:T(128)S(1)}, s32[8]{0:T(128)}, u32[]{:S(2)}) copy-start(s32[8]{0:T(128)} %param.11) | copy-start | bytes 100
  0.0 21.7 %collective-permute-start = (bf16[4096,512]{1,0:T(8,128)(2,1)}, bf16[4096,512]{1,0:T(8,128)(2,1)}, u32[]{:S(2)}, u32[]{:S(2)}) collective-permute-start(bf16[4096,512]{1,0:T(8,128)(2,1)} %mine.11), channel_id=1, source_target_pairs={{0,4},{4,0},{8,12},{12,8},{16,20},{20,16},{24,28},{28,24},{1,5},{5... | collective-permute-start | bytes 12582920 | tf_op jit(solution)/shard_map/ppermute | solution.py:165
  1.7 14.4 %copy-start.6 = (bf16[4,8]{1,0:T(4,128)(2,1)S(1)}, bf16[4,8]{1,0:T(4,128)(2,1)}, u32[]{:S(2)}) copy-start(bf16[4,8]{1,0:T(4,128)(2,1)} %param.13) | copy-start | bytes 196
  2.6 13.4 %all-to-all-start = ((bf16[4,64,1024]{2,1,0:T(8,128)(2,1)}), bf16[4,64,1024]{2,1,0:T(8,128)(2,1)S(1)}, u32[]{:S(2)}, u32[]{:S(2)}) async-start(bf16[4,64,1024]{2,1,0:T(8,128)(2,1)} %bitcast.72), calls=%async_computation | async-start | bytes 1048576 | tf_op jit(solution)/shard_map/all_to_all | solution.py:186
  17.2 24.3 %collective-permute-start.2 = (bf16[4,64,1024]{2,1,0:T(8,128)(2,1)S(1)}, bf16[4,64,1024]{2,1,0:T(8,128)(2,1)S(1)}, u32[]{:S(2)}, u32[]{:S(2)}) collective-permute-start(bf16[4,64,1024]{2,1,0:T(8,128)(2,1)S(1)} %all-to-all-done.rest_0_), channel_id=1, source_target_pairs={{0,1},{1,0},{2,3},{3,2},{4,5},{5,4},{6,7},{7,6},{8,9},{9,8},{10,11... | collective-permute-start | bytes 1572872 | tf_op jit(solution)/shard_map/ppermute | solution.py:165
  18.8 25.2 %collective-permute-start.1 = (bf16[4,64,1024]{2,1,0:T(8,128)(2,1)S(1)}, bf16[4,64,1024]{2,1,0:T(8,128)(2,1)S(1)}, u32[]{:S(2)}, u32[]{:S(2)}) collective-permute-start(bf16[4,64,1024]{2,1,0:T(8,128)(2,1)S(1)} %all-to-all-done.rest_0_), channel_id=1, source_target_pairs={{0,2},{1,3},{2,0},{3,1},{4,6},{5,7},{6,4},{7,5},{8,10},{9,11},{10,... | collective-permute-start | bytes 1572872 | tf_op jit(solution)/shard_map/ppermute | solution.py:165
  21.7 2.2 %copy-start.1 = (bf16[4096,512]{1,0:T(8,128)(2,1)S(1)}, bf16[4096,512]{1,0:T(8,128)(2,1)}, u32[]{:S(2)}) copy-start(bf16[4096,512]{1,0:T(8,128)(2,1)} %mine.11) | copy-start | bytes 12582916
  28.5 15.5 %all-to-all-start.1 = ((bf16[4,64,1024]{2,1,0:T(8,128)(2,1)}), bf16[4,64,1024]{2,1,0:T(8,128)(2,1)S(1)}, u32[]{:S(2)}, u32[]{:S(2)}) async-start(bf16[4,64,1024]{2,1,0:T(8,128)(2,1)} %bitcast.70), calls=%async_computation.1 | async-start | bytes 1048576 | tf_op jit(solution)/shard_map/all_to_all | solution.py:186
  32.2 12.1 %collective-permute-start.4 = (f32[4,1,4096]{2,0,1:T(4,128)S(1)}, f32[4,1,4096]{2,0,1:T(4,128)S(1)}, u32[]{:S(2)}, u32[]{:S(2)}) collective-permute-start(f32[4,1,4096]{2,0,1:T(4,128)S(1)} %bitcast.87), channel_id=1, source_target_pairs={{0,4},{4,0},{8,12},{12,8},{16,20},{20,16},{24,28},{28,24},{1,5},{5... | collective-permute-start | bytes 196616 | tf_op jit(solution)/shard_map/ppermute | solution.py:165
  44.0 24.7 %collective-permute-start.3 = (bf16[4,64,1024]{2,1,0:T(8,128)(2,1)S(1)}, bf16[4,64,1024]{2,1,0:T(8,128)(2,1)S(1)}, u32[]{:S(2)}, u32[]{:S(2)}) collective-permute-start(bf16[4,64,1024]{2,1,0:T(8,128)(2,1)S(1)} %collective-permute-done.1.rest_1_), channel_id=1, source_target_pairs={{0,1},{1,0},{2,3},{3,2},{4,5},{5,4},{6,7},{7,6},{8,9},{9,8},{10,11... | collective-permute-start | bytes 1572872 | tf_op jit(solution)/shard_map/ppermute | solution.py:165
  44.4 35.5 %collective-permute-start.8 = (bf16[4,64,1024]{2,1,0:T(8,128)(2,1)S(1)}, bf16[4,64,1024]{2,1,0:T(8,128)(2,1)S(1)}, u32[]{:S(2)}, u32[]{:S(2)}) collective-permute-start(bf16[4,64,1024]{2,1,0:T(8,128)(2,1)S(1)} %all-to-all-done.1.rest_0_), channel_id=1, source_target_pairs={{0,1},{1,0},{2,3},{3,2},{4,5},{5,4},{6,7},{7,6},{8,9},{9,8},{10,11... | collective-permute-start | bytes 1572872 | tf_op jit(solution)/shard_map/ppermute | solution.py:165
  46.1 33.7 %collective-permute-start.7 = (bf16[4,64,1024]{2,1,0:T(8,128)(2,1)S(1)}, bf16[4,64,1024]{2,1,0:T(8,128)(2,1)S(1)}, u32[]{:S(2)}, u32[]{:S(2)}) collective-permute-start(bf16[4,64,1024]{2,1,0:T(8,128)(2,1)S(1)} %all-to-all-done.1.rest_0_), channel_id=1, source_target_pairs={{0,2},{1,3},{2,0},{3,1},{4,6},{5,7},{6,4},{7,5},{8,10},{9,11},{10,... | collective-permute-start | bytes 1572872 | tf_op jit(solution)/shard_map/ppermute | solution.py:165
  47.2 2.2 %copy-start.2 = (bf16[4096,512]{1,0:T(8,128)(2,1)S(1)}, bf16[4096,512]{1,0:T(8,128)(2,1)}, u32[]{:S(2)}) copy-start(bf16[4096,512]{1,0:T(8,128)(2,1)} %mine.11) | copy-start | bytes 12582916
  56.2 23.7 %copy-start.5 = (bf16[4096]{0:T(1024)(128)(2,1)S(1)}, bf16[4096]{0:T(1024)(128)(2,1)}, u32[]{:S(2)}) copy-start(bf16[4096]{0:T(1024)(128)(2,1)} %param.9) | copy-start | bytes 24580
  73.3 5.0 %collective-permute-start.5 = (f32[8,4096]{1,0:T(8,128)S(1)}, f32[8,4096]{1,0:T(8,128)S(1)}, u32[]{:S(2)}, u32[]{:S(2)}) collective-permute-start(f32[8,4096]{1,0:T(8,128)S(1)} %forward.7.rest_0_), channel_id=1, source_target_pairs={{0,8},{4,12},{8,0},{12,4},{16,24},{20,28},{24,16},{28,20},{1,9},{5... | collective-permute-start | bytes 393224 | tf_op jit(solution)/shard_map/ppermute | solution.py:165
  78.3 5.0 %collective-permute-start.6 = (f32[8,4096]{1,0:T(8,128)S(1)}, f32[8,4096]{1,0:T(8,128)S(1)}, u32[]{:S(2)}, u32[]{:S(2)}) collective-permute-start(f32[8,4096]{1,0:T(8,128)S(1)} %add.65), channel_id=1, source_target_pairs={{0,16},{4,20},{8,24},{12,28},{16,0},{20,4},{24,8},{28,12},{1,17},{... | collective-permute-start | bytes 393224 | tf_op jit(solution)/shard_map/ppermute | solution.py:165
  79.9 27.7 %collective-permute-start.9 = (bf16[4,64,1024]{2,1,0:T(8,128)(2,1)S(1)}, bf16[4,64,1024]{2,1,0:T(8,128)(2,1)S(1)}, u32[]{:S(2)}, u32[]{:S(2)}) collective-permute-start(bf16[4,64,1024]{2,1,0:T(8,128)(2,1)S(1)} %collective-permute-done.7.rest_1_), channel_id=1, source_target_pairs={{0,1},{1,0},{2,3},{3,2},{4,5},{5,4},{6,7},{7,6},{8,9},{9,8},{10,11... | collective-permute-start | bytes 1572872 | tf_op jit(solution)/shard_map/ppermute | solution.py:165
  83.4 5.1 %copy-start.3 = (bf16[4096,512]{1,0:T(8,128)(2,1)S(1)}, bf16[4096,512]{1,0:T(8,128)(2,1)}, u32[]{:S(2)}) copy-start(bf16[4096,512]{1,0:T(8,128)(2,1)} %mine.11) | copy-start | bytes 12582916
  88.4 28.1 %collective-permute-start.11 = (bf16[4,64,1024]{2,1,0:T(8,128)(2,1)S(1)}, bf16[4,64,1024]{2,1,0:T(8,128)(2,1)S(1)}, u32[]{:S(2)}, u32[]{:S(2)}) collective-permute-start(bf16[4,64,1024]{2,1,0:T(8,128)(2,1)S(1)} %convert_element_type.43), channel_id=1, source_target_pairs={{0,1},{1,0},{2,3},{3,2},{4,5},{5,4},{6,7},{7,6},{8,9},{9,8},{10,11... | collective-permute-start | bytes 1572872 | tf_op jit(solution)/shard_map/ppermute | solution.py:165
  105.6 15.3 %collective-permute-start.13 = (bf16[4,64,1024]{2,1,0:T(8,128)(2,1)S(1)}, bf16[4,64,1024]{2,1,0:T(8,128)(2,1)S(1)}, u32[]{:S(2)}, u32[]{:S(2)}) collective-permute-start(bf16[4,64,1024]{2,1,0:T(8,128)(2,1)S(1)} %convert_element_type.44), channel_id=1, source_target_pairs={{0,1},{1,0},{2,3},{3,2},{4,5},{5,4},{6,7},{7,6},{8,9},{9,8},{10,11... | collective-permute-start | bytes 1572872 | tf_op jit(solution)/shard_map/ppermute | solution.py:165
  112.1 4.3 %collective-permute-start.10 = (f32[4,4096]{1,0:T(4,128)S(1)}, f32[4,4096]{1,0:T(4,128)S(1)}, u32[]{:S(2)}, u32[]{:S(2)}) collective-permute-start(f32[4,4096]{1,0:T(4,128)S(1)} %forward.9.rest_0_), channel_id=1, source_target_pairs={{0,8},{4,12},{8,0},{12,4},{16,24},{20,28},{24,16},{28,20},{1,9},{5... | collective-permute-start | bytes 196616 | tf_op jit(solution)/shard_map/ppermute | solution.py:165
  116.5 4.3 %collective-permute-start.12 = (f32[4,4096]{1,0:T(4,128)S(1)}, f32[4,4096]{1,0:T(4,128)S(1)}, u32[]{:S(2)}, u32[]{:S(2)}) collective-permute-start(f32[4,4096]{1,0:T(4,128)S(1)} %add.67), channel_id=1, source_target_pairs={{0,16},{4,20},{8,24},{12,28},{16,0},{20,4},{24,8},{28,12},{1,17},{... | collective-permute-start | bytes 196616 | tf_op jit(solution)/shard_map/ppermute | solution.py:165
  118.2 17.4 %collective-permute-start.14 = (bf16[4,64,1024]{2,1,0:T(8,128)(2,1)S(1)}, bf16[4,64,1024]{2,1,0:T(8,128)(2,1)S(1)}, u32[]{:S(2)}, u32[]{:S(2)}) collective-permute-start(bf16[4,64,1024]{2,1,0:T(8,128)(2,1)S(1)} %add_convert_fusion.3), channel_id=1, source_target_pairs={{0,2},{1,3},{2,0},{3,1},{4,6},{5,7},{6,4},{7,5},{8,10},{9,11},{10,... | collective-permute-start | bytes 1572872 | tf_op jit(solution)/shard_map/ppermute | solution.py:165
  125.7 15.4 %collective-permute-start.16 = (bf16[4,64,1024]{2,1,0:T(8,128)(2,1)S(1)}, bf16[4,64,1024]{2,1,0:T(8,128)(2,1)S(1)}, u32[]{:S(2)}, u32[]{:S(2)}) collective-permute-start(bf16[4,64,1024]{2,1,0:T(8,128)(2,1)S(1)} %convert_element_type.52), channel_id=1, source_target_pairs={{0,1},{1,0},{2,3},{3,2},{4,5},{5,4},{6,7},{7,6},{8,9},{9,8},{10,11... | collective-permute-start | bytes 1572872 | tf_op jit(solution)/shard_map/ppermute | solution.py:165
  140.4 21.4 %collective-permute-start.15 = (bf16[4,64,1024]{2,1,0:T(8,128)(2,1)S(1)}, bf16[4,64,1024]{2,1,0:T(8,128)(2,1)S(1)}, u32[]{:S(2)}, u32[]{:S(2)}) collective-permute-start(bf16[4,64,1024]{2,1,0:T(8,128)(2,1)S(1)} %convert_element_type.50), channel_id=1, source_target_pairs={{0,1},{1,0},{2,3},{3,2},{4,5},{5,4},{6,7},{7,6},{8,9},{9,8},{10,11... | collective-permute-start | bytes 1572872 | tf_op jit(solution)/shard_map/ppermute | solution.py:165
  142.1 24.6 %collective-permute-start.17 = (bf16[4,64,1024]{2,1,0:T(8,128)(2,1)}, bf16[4,64,1024]{2,1,0:T(8,128)(2,1)}, u32[]{:S(2)}, u32[]{:S(2)}) collective-permute-start(bf16[4,64,1024]{2,1,0:T(8,128)(2,1)} %add_convert_fusion.1), channel_id=1, source_target_pairs={{0,2},{1,3},{2,0},{3,1},{4,6},{5,7},{6,4},{7,5},{8,10},{9,11},{10,... | collective-permute-start | bytes 1572872 | tf_op jit(solution)/shard_map/ppermute | solution.py:165
  151.3 17.4 %all-to-all-start.2 = ((bf16[4,64,1024]{2,1,0:T(8,128)(2,1)}), bf16[4,64,1024]{2,1,0:T(8,128)(2,1)S(1)}, u32[]{:S(2)}, u32[]{:S(2)}) async-start(bf16[4,64,1024]{2,1,0:T(8,128)(2,1)} %add_convert_fusion.2), calls=%async_computation.2 | async-start | bytes 1048576 | tf_op jit(solution)/shard_map/all_to_all | solution.py:186
  154.8 2.2 %copy-start.4 = (bf16[4096,512]{1,0:T(8,128)(2,1)S(1)}, bf16[4096,512]{1,0:T(8,128)(2,1)}, u32[]{:S(2)}) copy-start(bf16[4096,512]{1,0:T(8,128)(2,1)} %mine.11) | copy-start | bytes 12582916
  168.7 10.0 %all-to-all-start.3 = ((bf16[4,64,1024]{2,1,0:T(8,128)(2,1)}), bf16[4,64,1024]{2,1,0:T(8,128)(2,1)S(1)}, u32[]{:S(2)}, u32[]{:S(2)}) async-start(bf16[4,64,1024]{2,1,0:T(8,128)(2,1)} %add_convert_fusion), calls=%async_computation.3 | async-start | bytes 1048576 | tf_op jit(solution)/shard_map/all_to_all | solution.py:186
